TPU v7x, 32 devices: a whole 2x2x4 slice. The times are simulated.
32 devices in a mesh: ctx: 2 (over y), head: 4 (over x, core), resp: 4 (over z).
Axes of the slice: x: 2, y: 2, z: 4, core: 2. Of those that a mesh axis runs over, the one named last changes fastest.
Arguments:
- prompt_query: bfloat16 [2048, 64, 128], P(('ctx', 'head'), 'resp'), may hold values from -6 to 6
- prompt_key: bfloat16 [2048, 64, 128], P(('ctx', 'head'), 'resp'), may hold values from -6 to 6
- prompt_value: bfloat16 [2048, 64, 128], P(('ctx', 'head'), 'resp'), may hold values from -6 to 6
- prompt_cotangent: bfloat16 [2048, 64, 128], P(('ctx', 'head'), 'resp'), may hold values from -6 to 6
- reply_query: bfloat16 [4, 512, 64, 128], P('resp', None, ('ctx', 'head')), may hold values from -6 to 6
- reply_key: bfloat16 [4, 512, 64, 128], P('resp', None, ('ctx', 'head')), may hold values from -6 to 6
- reply_value: bfloat16 [4, 512, 64, 128], P('resp', None, ('ctx', 'head')), may hold values from -6 to 6
- reply_cotangent: bfloat16 [4, 512, 64, 128], P('resp', None, ('ctx', 'head')), may hold values from -6 to 6
- reply_weight: float32 [4], P('resp'), may hold values from 0.5 to 2
- reply_length: int32 [4], P('resp'), may hold values from 1 to 512, 1536 in all
Outputs:
- prompt_output: bfloat16 [2048, 64, 128], P(('ctx', 'head'), 'resp')
- reply_output: bfloat16 [4, 512, 64, 128], P('resp', None, ('ctx', 'head'))
- prompt_query_grad: bfloat16 [2048, 64, 128], P(('ctx', 'head'), 'resp')
- prompt_key_grad: bfloat16 [2048, 64, 128], P(('ctx', 'head'), 'resp')
- prompt_value_grad: bfloat16 [2048, 64, 128], P(('ctx', 'head'), 'resp')
- reply_query_grad: bfloat16 [4, 512, 64, 128], P('resp', None, ('ctx', 'head'))
- reply_key_grad: bfloat16 [4, 512, 64, 128], P('resp', None, ('ctx', 'head'))
- reply_value_grad: bfloat16 [4, 512, 64, 128], P('resp', None, ('ctx', 'head'))
Inputs may be any that keep to these rules, and one draw needn't show every extreme that they name: `reply_length`: the longest response has exactly 512 live tokens; the slots of a response from its length on are padding.
All inputs are finite; a program needn't handle non-finite values. No bound on the sum of `reply_length` on one device may be relied on, other than what follows from the above.
Results may differ from a plain program's by a relative error of at most 0.0095.
Values sent between devices are 32-bit elements; how exact they have to be, the bound alone decides.
No kernel may reach another device: no remote copies, remote signals or barrier semaphores. Data moves between devices by JAX's collectives and lax.ppermute only.
A program may use at most 128 MiB of HBM per device.

v0:
```python
import jax
import jax.numpy as jnp
from jax import lax
from jax.sharding import PartitionSpec as P


def prefix(part, axis, combine, identity, reverse):
    count = lax.axis_size(axis)
    place = lax.axis_index(axis)
    ahead = count - 1 - place if reverse else place
    gathered = lax.all_gather(part, axis)
    state = jnp.zeros_like(part) + jnp.asarray(identity, part.dtype)

    def one(lap, state):
        source = count - 1 - lap if reverse else lap
        return combine(state, lax.dynamic_index_in_dim(gathered, source, 0, False))

    return lax.fori_loop(0, ahead, one, state)


def from_root(block, axis, owner):
    block = jnp.where(lax.axis_index(axis) == owner, block, jnp.zeros_like(block))
    return lax.psum(block, axis)


def position_scale(first_row, row_total, head_size):
    positions = (first_row + jnp.arange(row_total, dtype=jnp.int32)).astype(jnp.float32)
    return lax.rsqrt(float(head_size) * (positions + 1.0))


def causal_mask(row_total):
    return jnp.arange(row_total)[:, None] >= jnp.arange(row_total)[None, :]


def split_wide(wide):
    upper = wide.astype(jnp.bfloat16)
    lower = (wide - upper.astype(jnp.float32)).astype(jnp.bfloat16)
    return (upper, lower)


def narrow_first(form, narrow, wide):
    upper, lower = split_wide(wide)
    first = jnp.einsum(form, narrow, upper, preferred_element_type=jnp.float32)
    return first + jnp.einsum(form, narrow, lower, preferred_element_type=jnp.float32)


def wide_first(form, wide, narrow):
    upper, lower = split_wide(wide)
    first = jnp.einsum(form, upper, narrow, preferred_element_type=jnp.float32)
    return first + jnp.einsum(form, lower, narrow, preferred_element_type=jnp.float32)


def forward_pieces(query, key_rows, value_rows, row_scale):
    causal = causal_mask(query.shape[0])
    scores = jnp.einsum("thd,shd->hts", query, key_rows, preferred_element_type=jnp.float32)
    mixing = jnp.where(causal[None], scores * row_scale[None, :, None], 0.0).astype(jnp.bfloat16)
    inner_sum = jnp.einsum("hts,she->the", mixing, value_rows, preferred_element_type=jnp.float32)
    return (mixing, inner_sum)


def carried_term(query, state_in, row_scale):
    product = narrow_first("thd,hde->the", query, state_in)
    return row_scale[:, None, None] * product


def local_state(key_rows, value_rows):
    return jnp.einsum("shd,she->hde", key_rows, value_rows, preferred_element_type=jnp.float32)


def local_moment(query, cotangent, row_scale):
    scaled = query.astype(jnp.float32) * row_scale[:, None, None]
    return wide_first("thd,the->hde", scaled, cotangent)


def backward_pieces(query, key_rows, value_rows, cotangent, mixing, row_scale, state_in, suffix_in):
    causal = causal_mask(query.shape[0])
    grad_mixing = jnp.einsum(
        "the,she->hts", cotangent, value_rows, preferred_element_type=jnp.float32
    )
    grad_scores = jnp.where(causal[None], grad_mixing * row_scale[None, :, None], 0.0).astype(
        jnp.bfloat16
    )
    grad_query = jnp.einsum(
        "hts,shd->thd", grad_scores, key_rows, preferred_element_type=jnp.float32
    )
    grad_query = grad_query + row_scale[:, None, None] * narrow_first(
        "the,hde->thd", cotangent, state_in
    )
    grad_key = jnp.einsum("hts,thd->shd", grad_scores, query, preferred_element_type=jnp.float32)
    grad_value = jnp.einsum("hts,the->she", mixing, cotangent, preferred_element_type=jnp.float32)
    if suffix_in is not None:
        grad_key = grad_key + narrow_first("she,hde->shd", value_rows, suffix_in)
        grad_value = grad_value + narrow_first("shd,hde->she", key_rows, suffix_in)
    return (
        grad_query.astype(jnp.bfloat16),
        grad_key.astype(jnp.bfloat16),
        grad_value.astype(jnp.bfloat16),
    )


def add_states(earlier, later):
    return earlier + later


def shards(
    prompt_query,
    prompt_key,
    prompt_value,
    prompt_cotangent,
    reply_query,
    reply_key,
    reply_value,
    reply_cotangent,
    reply_weight,
    reply_length,
):
    prompt_rows = prompt_query.shape[0]
    prompt_heads = prompt_query.shape[1]
    head_size = prompt_query.shape[2]
    reply_rows = reply_query.shape[1]
    reply_heads = reply_query.shape[2]
    ctx_count = lax.axis_size("ctx")
    head_count = lax.axis_size("head")
    block_index = lax.axis_index("ctx") * head_count + lax.axis_index("head")
    resp_index = lax.axis_index("resp")
    prompt_scale = position_scale(block_index * prompt_rows, prompt_rows, head_size)
    prompt_mixing, prompt_inner = forward_pieces(
        prompt_query, prompt_key, prompt_value, prompt_scale
    )
    prompt_local = local_state(prompt_key, prompt_value)
    zero_state = jnp.zeros_like(prompt_local)
    prompt_before = prefix(prompt_local, ("ctx", "head"), add_states, zero_state, False)
    prompt_total = lax.psum(prompt_local, ("ctx", "head"))
    prompt_output = (prompt_inner + carried_term(prompt_query, prompt_before, prompt_scale)).astype(
        jnp.bfloat16
    )
    reply_first = block_index * reply_heads
    owner_index = reply_first // prompt_heads
    owner_state = from_root(prompt_total, "resp", owner_index)
    reply_state = lax.dynamic_slice_in_dim(
        owner_state, reply_first - owner_index * prompt_heads, reply_heads, 0
    )
    query_rows = reply_query[0]
    key_rows = reply_key[0]
    value_rows = reply_value[0]
    reply_scale = position_scale(ctx_count * head_count * prompt_rows, reply_rows, head_size)
    live_mask = (jnp.arange(reply_rows, dtype=jnp.int32) < reply_length[0])[:, None, None]
    reply_mixing, reply_inner = forward_pieces(query_rows, key_rows, value_rows, reply_scale)
    reply_output = jnp.where(
        live_mask, reply_inner + carried_term(query_rows, reply_state, reply_scale), 0.0
    ).astype(jnp.bfloat16)
    weighted = (
        reply_weight[0] * jnp.where(live_mask, reply_cotangent[0].astype(jnp.float32), 0.0)
    ).astype(jnp.bfloat16)
    reply_dquery, reply_dkey, reply_dvalue = backward_pieces(
        query_rows, key_rows, value_rows, weighted, reply_mixing, reply_scale, reply_state, None
    )
    reply_local = local_moment(query_rows, weighted, reply_scale)
    moment_sum = lax.psum(reply_local, "resp")
    prompt_first = resp_index * prompt_heads
    pieces = []
    for part_index in range(prompt_heads // reply_heads):
        source_index = prompt_first // reply_heads + part_index
        pieces.append(from_root(moment_sum, ("ctx", "head"), source_index))
    prompt_after = jnp.concatenate(pieces, 0)
    prompt_moment = local_moment(prompt_query, prompt_cotangent, prompt_scale)
    later_sum = prefix(prompt_moment, ("ctx", "head"), add_states, zero_state, True)
    suffix = later_sum + prompt_after
    prompt_dquery, prompt_dkey, prompt_dvalue = backward_pieces(
        prompt_query,
        prompt_key,
        prompt_value,
        prompt_cotangent,
        prompt_mixing,
        prompt_scale,
        prompt_before,
        suffix,
    )
    return (
        prompt_output,
        reply_output[None],
        prompt_dquery,
        prompt_dkey,
        prompt_dvalue,
        reply_dquery[None],
        reply_dkey[None],
        reply_dvalue[None],
    )


def solution(mesh):
    placed = (
        P(("ctx", "head"), "resp", None),
        P(("ctx", "head"), "resp", None),
        P(("ctx", "head"), "resp", None),
        P(("ctx", "head"), "resp", None),
        P("resp", None, ("ctx", "head"), None),
        P("resp", None, ("ctx", "head"), None),
        P("resp", None, ("ctx", "head"), None),
        P("resp", None, ("ctx", "head"), None),
        P("resp"),
        P("resp"),
    )
    return jax.shard_map(
        shards,
        mesh=mesh,
        in_specs=placed,
        out_specs=(
            P(("ctx", "head"), "resp", None),
            P("resp", None, ("ctx", "head"), None),
            P(("ctx", "head"), "resp", None),
            P(("ctx", "head"), "resp", None),
            P(("ctx", "head"), "resp", None),
            P("resp", None, ("ctx", "head"), None),
            P("resp", None, ("ctx", "head"), None),
            P("resp", None, ("ctx", "head"), None),
        ),
        check_vma=False,
    )
```

profile of v0, /device:TPU:0, one launch (start us, length us, event | category | flops | bytes accessed | tf_op | source)
XLA Modules:
  0.0 271.4 jit_solution(3218367287383065331)
XLA Ops:
  9.5 2.6 subtract_convert_fusion
  16.7 1.7 subtract_convert_fusion.1
  20.8 3.4 %select_convert_fusion = bf16[8,512,512]{2,1,0:T(8,128)(2,1)S(1)} fusion(f32[512]{0:T(512)S(1)} %multiply_rsqrt_fusion, pred[512,512]{1,0:T(8,128)(4,1)S(1)} %iota_compare_fusion, bf16[512,8,128]{2,1,0:T(8,128)(2,1)} %bitcast.115, bf16[1,512,8,128]{3,2,1,0:T(8,128)(2,1)} %param.21, f32[]{:T(128)} %bitcast.104, pred[512]{0:T(512)(128)(4,1)S(1)} %iota_compare_fusion.2), kind=kOutput, calls=%fused_computation.2 | convolution fusion | flops 545259520 | bytes 6556164 | tf_op jit(solution)/shard_map/the,she->hts/dot_general | solution.py:77
  29.5 2.0 copy-done.21
  31.5 2.0 fusion.13
  33.5 2.4 copy.143
  35.9 2.2 select_convert_fusion.2
  39.0 2.2 fusion.52
  41.2 2.0 fusion.43
  43.2 2.2 fusion.31
  45.4 2.1 fusion.49
  47.5 8.6 %all-reduce.7.cloned.1.call-done = f32[8,128,128]{2,1,0:T(8,128)} async-done(((f32[8,128,128]{2,1,0:T(8,128)}), f32[8,128,128]{2,1,0:T(8,128)}) %all-reduce.7.cloned.1.call-update) | async-done | bytes 524304 | tf_op jit(solution)/shard_map/psum | solution.py:159
  56.1 2.1 broadcast_select_fusion.2
  58.2 16.6 %all-gather.5.cloned.1.call-done = f32[128,128,128]{2,1,0:T(8,128)} async-done(((f32[16,128,128]{2,1,0:T(8,128)}), f32[128,128,128]{2,1,0:T(8,128)}) %all-gather.5.cloned.1.call-update) | async-done | bytes 8388624 | tf_op jit(solution)/shard_map/all_gather | solution.py:11
  77.3 1.6 copy.138
  83.0 48.5 %all-gather.7.cloned.1.call-done = f32[128,128,128]{2,1,0:T(8,128)} async-done(((f32[16,128,128]{2,1,0:T(8,128)}), f32[128,128,128]{2,1,0:T(8,128)}) %all-gather.7.cloned.1.call-update) | async-done | bytes 8388624 | tf_op jit(solution)/shard_map/all_gather | solution.py:11
  131.5 10.8 %while.23 = (s32[]{:T(128)}, f32[16,128,128]{2,1,0:T(8,128)S(1)}, s32[]{:T(128)}, f32[8,16,128,128]{3,2,1,0:T(8,128)}, s32[]{:T(128)}, /*index=5*/s32[]{:T(128)}, s32[]{:T(128)}, s32[]{:T(128)}) while((s32[]{:T(128)}, f32[16,128,128]{2,1,0:T(8,128)S(1)}, s32[]{:T(128)}, f32[8,16,128,128]{3,2,1,0:T(8,128)}, s32[]{:T(128)}, ...), condition=%wide.region_5.6_spmd, body=%wide.region_4.5_spmd.sunk | while | flops 262150 | bytes 3145871 | solution.py:18
  142.4 54.5 %all-reduce.9.cloned.1.call-done = (f32[16,128,128]{2,1,0:T(8,128)}, f32[8,128,128]{2,1,0:T(8,128)}, f32[8,128,128]{2,1,0:T(8,128)}) async-done(((f32[16,128,128]{2,1,0:T(8,128)}, f32[8,128,128]{2,1,0:T(8,128)}, f32[8,128,128]{2,1,0:T(8,128)}), (f32[16,128,128]{2,1,0:T(8,128)}, f32[8,128,128]{2,1,0:T(8,128)}, f32[8,128,128]{2,1,0:T(8,128)})) %all-reduce.9.cloned.1.call-update) | async-done | bytes 2097168 | tf_op jit(solution)/shard_map/psum | solution.py:133
  196.9 2.2 subtract_convert_fusion.2
  199.1 1.9 fusion.47
  202.0 2.9 %fusion.3 = bf16[256,16,128]{2,0,1:T(8,128)(2,1)S(1)} fusion(f32[16,256,128]{2,1,0:T(8,128)} %fusion.52, f32[16,128,256]{1,2,0:T(8,128)} %fusion.47, bf16[16,128,128]{2,1,0:T(8,128)(2,1)} %subtract_convert_fusion.2, bf16[256,16,128]{2,1,0:T(8,128)(2,1)S(1)} %copy-done.3), kind=kOutput, calls=%fused_computation.12 | convolution fusion | flops 135790592 | bytes 6815744 | tf_op jit(solution)/shard_map/shd,hde->she/dot_general | solution.py:44
  205.0 1.6 copy.140
  210.6 42.8 %all-reduce.5.cloned.1.call-done = f32[16,128,128]{2,1,0:T(8,128)} async-done(((f32[16,128,128]{2,1,0:T(8,128)}), f32[16,128,128]{2,1,0:T(8,128)}) %all-reduce.5.cloned.1.call-update) | async-done | bytes 1048592 | tf_op jit(solution)/shard_map/psum | solution.py:23
  262.2 1.6 copy.137
  (108 shorter events, 43.7 us)
Async XLA Ops:
  8.0 19.9 %copy-start = (bf16[1,512,8,128]{3,2,1,0:T(8,128)(2,1)S(1)}, bf16[1,512,8,128]{3,2,1,0:T(8,128)(2,1)}, u32[]{:S(2)}) copy-start(bf16[1,512,8,128]{3,2,1,0:T(8,128)(2,1)} %param.19) | copy-start | bytes 3145732
  8.0 4.1 %copy-start.23 = (bf16[1,512,8,128]{3,2,1,0:T(8,128)(2,1)S(1)}, bf16[1,512,8,128]{3,2,1,0:T(8,128)(2,1)}, u32[]{:S(2)}) copy-start(bf16[1,512,8,128]{3,2,1,0:T(8,128)(2,1)} %param.21) | copy-start | bytes 3145732
  8.0 48.1 %all-reduce.7.cloned.1.call-start = ((), (), s32[]{:S(2)}) async-start(), calls=%async_computation.1 | async-start | bytes 1048576 | tf_op jit(solution)/shard_map/psum | solution.py:159
  13.3 1.7 copy-start.2
  13.3 1.7 copy-start.4
  15.0 59.9 %all-gather.5.cloned.1.call-start = ((), (), s32[]{:S(2)}) async-start(), calls=%async_computation.2 | async-start | bytes 9437184 | tf_op jit(solution)/shard_map/all_gather | solution.py:11
  16.6 1.8 copy-start.1
  16.6 114.8 %all-gather.7.cloned.1.call-start = ((), (), s32[]{:S(2)}) async-start(), calls=%async_computation.3 | async-start | bytes 9437184 | tf_op jit(solution)/shard_map/all_gather | solution.py:11
  20.8 3.5 %copy-start.11 = (bf16[1,512,8,128]{3,2,1,0:T(8,128)(2,1)S(1)}, bf16[1,512,8,128]{3,2,1,0:T(8,128)(2,1)}, u32[]{:S(2)}) copy-start(bf16[1,512,8,128]{3,2,1,0:T(8,128)(2,1)} %param.18) | copy-start | bytes 3145732
  24.3 2.0 copy-start.7
  27.9 3.5 %copy-start.25 = (bf16[1,512,8,128]{3,2,1,0:T(8,128)(2,1)S(1)}, bf16[1,512,8,128]{3,2,1,0:T(8,128)(2,1)}, u32[]{:S(2)}) copy-start(bf16[1,512,8,128]{3,2,1,0:T(8,128)(2,1)} %param.21) | copy-start | bytes 3145732
  29.5 2.0 copy-start.21
  35.9 2.2 copy-start.9
  39.0 2.2 copy-start.5
  74.9 122.0 %all-reduce.9.cloned.1.call-start = ((), (), s32[]{:S(2)}) async-start(), calls=%async_computation.4 | async-start | bytes 4194304 | tf_op jit(solution)/shard_map/psum | solution.py:133
  82.9 170.4 %all-reduce.5.cloned.1.call-start = ((), (), s32[]{:S(2)}) async-start(), calls=%async_computation | async-start | bytes 2097152 | tf_op jit(solution)/shard_map/psum | solution.py:23
  142.4 56.7 %copy-start.3 = (bf16[256,16,128]{2,1,0:T(8,128)(2,1)S(1)}, bf16[256,16,128]{2,1,0:T(8,128)(2,1)}, u32[]{:S(2)}) copy-start(bf16[256,16,128]{2,1,0:T(8,128)(2,1)} %param.15) | copy-start | bytes 3145732
  196.9 2.2 copy-start.16
  196.9 2.2 copy-start.18
  199.1 1.9 copy-start.28
  208.9 45.8 %copy-start.12 = (bf16[1,512,8,128]{3,2,1,0:T(8,128)(2,1)S(1)}, bf16[1,512,8,128]{3,2,1,0:T(8,128)(2,1)}, u32[]{:S(2)}) copy-start(bf16[1,512,8,128]{3,2,1,0:T(8,128)(2,1)} %param.18) | copy-start | bytes 3145732
  210.6 44.5 %copy-start.26 = (bf16[1,512,8,128]{3,2,1,0:T(8,128)(2,1)S(1)}, bf16[1,512,8,128]{3,2,1,0:T(8,128)(2,1)}, u32[]{:S(2)}) copy-start(bf16[1,512,8,128]{3,2,1,0:T(8,128)(2,1)} %param.21) | copy-start | bytes 3145732
  255.6 2.2 copy-start.8
  257.8 3.0 %copy-start.22 = (bf16[8,512,512]{2,1,0:T(8,128)(2,1)S(1)}, bf16[8,512,512]{2,1,0:T(8,128)(2,1)}, u32[]{:S(2)}) copy-start(bf16[8,512,512]{2,1,0:T(8,128)(2,1)} %copy-done.21) | copy-start | bytes 12582916
  (10 other events, 16.1 us)
Sparse Core Ops, SparseCore 0:
  15.1 40.9 all-reduce.6
  202.2 51.1 all-reduce.4
Sparse Core Ops, SparseCore 1:
  17.9 56.9 all-gather.4
  77.2 54.2 all-gather.6
  135.3 61.5 all-reduce.8
where the time goes:
time: 272 us; the launch traced here: 271 us
  waiting for transfers between devices  171 us (63%)
  matrix products  38.9 us (14%)
  local copies, waits for them, and re-layouts  21.8 us (8%)
  other arithmetic  21.5 us (8%)
  between operations  17.6 us (6%)
    all_gather x2, waiting for transfers between devices, prefix(): gathered = lax.all_gather(part, axis)  65.1 us
    psum x1, waiting for transfers between devices, shards(): prompt_total = lax.psum(prompt_local, ('ctx', 'head'))  54.5 us
    psum x1, waiting for transfers between devices, from_root(): return lax.psum(block, axis)  42.8 us
    unnamed x66, local copies, waits for them, and re-layouts  21.7 us
    add x7, other arithmetic, add_states(): return earlier + later  10.5 us
    psum x1, waiting for transfers between devices, shards(): moment_sum = lax.psum(reply_local, 'resp')  8.64 us
    convert_element_type x4, other arithmetic, split_wide(): lower = (wide - upper.astype(jnp.float32)).astype(jnp.bfloat16)  7.77 us
    dot_general x6, matrix products, narrow_first(): jnp.einsum(form, narrow, lower, preferred_element_type=jnp.float32)  5.77 us
  transfers between devices with their start and end apart: 5, of which 5 were waited for; matrix products, arithmetic and copies ran while one was open for 20% of the time, Pallas kernels for 0%

commit v1 on v0

--- a/solution.py
+++ b/solution.py
@@ -3,24 +3,54 @@
 from jax import lax
 from jax.sharding import PartitionSpec as P
 
-
-def prefix(part, axis, combine, identity, reverse):
-    count = lax.axis_size(axis)
-    place = lax.axis_index(axis)
-    ahead = count - 1 - place if reverse else place
-    gathered = lax.all_gather(part, axis)
-    state = jnp.zeros_like(part) + jnp.asarray(identity, part.dtype)
-
-    def one(lap, state):
-        source = count - 1 - lap if reverse else lap
-        return combine(state, lax.dynamic_index_in_dim(gathered, source, 0, False))
-
-    return lax.fori_loop(0, ahead, one, state)
-
-
-def from_root(block, axis, owner):
-    block = jnp.where(lax.axis_index(axis) == owner, block, jnp.zeros_like(block))
-    return lax.psum(block, axis)
+PLANE = ("ctx", "head")
+
+
+def pair_step(block):
+    count = lax.axis_size(PLANE)
+    return lax.ppermute(block, PLANE, [(b, b ^ 1) for b in range(count)])
+
+
+def plane_exchange(pieces):
+    count = lax.axis_size(PLANE)
+    moved = [pieces[0]]
+    for k in range(1, len(pieces)):
+        moved.append(lax.ppermute(pieces[k], PLANE, [(b, b ^ (2 * k)) for b in range(count)]))
+    return moved
+
+
+def resp_exchange(pieces):
+    count = lax.axis_size("resp")
+    moved = [pieces[0]]
+    for k in range(1, len(pieces)):
+        moved.append(lax.ppermute(pieces[k], "resp", [(z, z ^ k) for z in range(count)]))
+    return moved
+
+
+def choose(pieces, place):
+    chosen = pieces[0]
+    for k in range(1, len(pieces)):
+        chosen = jnp.where(place == k, pieces[k], chosen)
+    return chosen
+
+
+def masked_sum(pieces, keep):
+    total = None
+    for piece, kept in zip(pieces, keep):
+        term = jnp.where(kept, piece, 0.0)
+        total = term if total is None else total + term
+    return total
+
+
+def joined(pieces, place):
+    return jnp.concatenate([choose(pieces, place ^ q) for q in range(len(pieces))], 0)
+
+
+def both_halves(half, member):
+    other = pair_step(half)
+    return jnp.concatenate(
+        [jnp.where(member == 0, half, other), jnp.where(member == 0, other, half)], 0
+    )
 
 
 def position_scale(first_row, row_total, head_size):
@@ -96,10 +126,6 @@
         grad_key.astype(jnp.bfloat16),
         grad_value.astype(jnp.bfloat16),
     )
-
-
-def add_states(earlier, later):
-    return earlier + later
 
 
 def shards(
@@ -119,53 +145,100 @@
     head_size = prompt_query.shape[2]
     reply_rows = reply_query.shape[1]
     reply_heads = reply_query.shape[2]
-    ctx_count = lax.axis_size("ctx")
-    head_count = lax.axis_size("head")
-    block_index = lax.axis_index("ctx") * head_count + lax.axis_index("head")
+    block_count = lax.axis_size(PLANE)
+    resp_count = lax.axis_size("resp")
+    assert block_count == 2 * resp_count and resp_count & (resp_count - 1) == 0
+    block_index = lax.axis_index(PLANE)
     resp_index = lax.axis_index("resp")
+    pair_index, member = block_index // 2, block_index % 2
+    state_rows = prompt_heads * head_size
+    half_rows = state_rows // 2
+    chunk_rows = half_rows // resp_count
+    steps = range(resp_count)
     prompt_scale = position_scale(block_index * prompt_rows, prompt_rows, head_size)
-    prompt_mixing, prompt_inner = forward_pieces(
-        prompt_query, prompt_key, prompt_value, prompt_scale
-    )
-    prompt_local = local_state(prompt_key, prompt_value)
-    zero_state = jnp.zeros_like(prompt_local)
-    prompt_before = prefix(prompt_local, ("ctx", "head"), add_states, zero_state, False)
-    prompt_total = lax.psum(prompt_local, ("ctx", "head"))
-    prompt_output = (prompt_inner + carried_term(prompt_query, prompt_before, prompt_scale)).astype(
-        jnp.bfloat16
-    )
-    reply_first = block_index * reply_heads
-    owner_index = reply_first // prompt_heads
-    owner_state = from_root(prompt_total, "resp", owner_index)
-    reply_state = lax.dynamic_slice_in_dim(
-        owner_state, reply_first - owner_index * prompt_heads, reply_heads, 0
-    )
+    reply_scale = position_scale(block_count * prompt_rows, reply_rows, head_size)
     query_rows = reply_query[0]
     key_rows = reply_key[0]
     value_rows = reply_value[0]
-    reply_scale = position_scale(ctx_count * head_count * prompt_rows, reply_rows, head_size)
     live_mask = (jnp.arange(reply_rows, dtype=jnp.int32) < reply_length[0])[:, None, None]
+    weighted = (
+        reply_weight[0] * jnp.where(live_mask, reply_cotangent[0].astype(jnp.float32), 0.0)
+    ).astype(jnp.bfloat16)
+
+    def scattered(mine, other):
+        pair_sum = mine + other
+        pieces = [
+            lax.dynamic_slice_in_dim(
+                pair_sum, member * half_rows + (pair_index ^ k) * chunk_rows, chunk_rows, 0
+            )
+            for k in steps
+        ]
+        return plane_exchange(pieces)
+
+    reply_local = local_moment(query_rows, weighted, reply_scale).reshape(half_rows, head_size)
+    reply_parts = plane_exchange(
+        [
+            lax.dynamic_slice_in_dim(reply_local, (pair_index ^ k) * chunk_rows, chunk_rows, 0)
+            for k in steps
+        ]
+    )
+    prompt_local = local_state(prompt_key, prompt_value).reshape(state_rows, head_size)
+    other_local = pair_step(prompt_local)
+    state_parts = scattered(prompt_local, other_local)
+    moment_local = local_moment(prompt_query, prompt_cotangent, prompt_scale)
+    moment_local = moment_local.reshape(state_rows, head_size)
+    other_moment = pair_step(moment_local)
+    moment_parts = scattered(moment_local, other_moment)
+
+    final_chunk = masked_sum(state_parts, [True] * resp_count)
+    final_parts = resp_exchange([final_chunk] * resp_count)
+    reply_state = joined(
+        plane_exchange([choose(final_parts, resp_index ^ pair_index ^ k) for k in steps]),
+        pair_index,
+    ).reshape(reply_heads, head_size, head_size)
+
+    before_half = joined(
+        plane_exchange(
+            [
+                masked_sum(state_parts, [(pair_index ^ m) < (pair_index ^ k) for m in steps])
+                for k in steps
+            ]
+        ),
+        pair_index,
+    )
+    prompt_before = both_halves(before_half, member) + jnp.where(member == 1, other_local, 0.0)
+    prompt_before = prompt_before.reshape(prompt_heads, head_size, head_size)
+
+    reply_chunk = masked_sum(
+        resp_exchange([choose(reply_parts, resp_index ^ pair_index ^ j) for j in steps]),
+        [True] * resp_count,
+    )
+    after_half = joined(
+        plane_exchange(
+            [
+                reply_chunk
+                + masked_sum(moment_parts, [(pair_index ^ m) > (pair_index ^ k) for m in steps])
+                for k in steps
+            ]
+        ),
+        pair_index,
+    )
+    suffix = both_halves(after_half, member) + jnp.where(member == 0, other_moment, 0.0)
+    suffix = suffix.reshape(prompt_heads, head_size, head_size)
+
+    prompt_mixing, prompt_inner = forward_pieces(
+        prompt_query, prompt_key, prompt_value, prompt_scale
+    )
+    prompt_output = (prompt_inner + carried_term(prompt_query, prompt_before, prompt_scale)).astype(
+        jnp.bfloat16
+    )
     reply_mixing, reply_inner = forward_pieces(query_rows, key_rows, value_rows, reply_scale)
     reply_output = jnp.where(
         live_mask, reply_inner + carried_term(query_rows, reply_state, reply_scale), 0.0
     ).astype(jnp.bfloat16)
-    weighted = (
-        reply_weight[0] * jnp.where(live_mask, reply_cotangent[0].astype(jnp.float32), 0.0)
-    ).astype(jnp.bfloat16)
     reply_dquery, reply_dkey, reply_dvalue = backward_pieces(
         query_rows, key_rows, value_rows, weighted, reply_mixing, reply_scale, reply_state, None
     )
-    reply_local = local_moment(query_rows, weighted, reply_scale)
-    moment_sum = lax.psum(reply_local, "resp")
-    prompt_first = resp_index * prompt_heads
-    pieces = []
-    for part_index in range(prompt_heads // reply_heads):
-        source_index = prompt_first // reply_heads + part_index
-        pieces.append(from_root(moment_sum, ("ctx", "head"), source_index))
-    prompt_after = jnp.concatenate(pieces, 0)
-    prompt_moment = local_moment(prompt_query, prompt_cotangent, prompt_scale)
-    later_sum = prefix(prompt_moment, ("ctx", "head"), add_states, zero_state, True)
-    suffix = later_sum + prompt_after
     prompt_dquery, prompt_dkey, prompt_dvalue = backward_pieces(
         prompt_query,
         prompt_key,

time: 272 us -> 127 us (0.47)
  waiting for transfers between devices: 171 us -> 13 us
  starting transfers between devices: 0.17 us -> 34.1 us
  between operations: 17.6 us -> 2.59 us
  other arithmetic: 21.5 us -> 17.4 us
    psum x3 -> x0, waiting for transfers between devices: 106 us -> none  [the longest x1 54.5 us: shards(): prompt_total = lax.psum(prompt_local, ('ctx', 'head'))]
    all_gather x2 -> x0, waiting for transfers between devices: 65.1 us -> none  [prefix(): gathered = lax.all_gather(part, axis)]
    ppermute x0 -> x28, starting transfers between devices: none -> 34.1 us  [the longest x18 23.9 us: plane_exchange(): lax.ppermute(pieces[k], PLANE, [(b, b ^ 2 * k) for b in range(count)])]
    ppermute x0 -> x28, waiting for transfers between devices: none -> 13 us  [the longest x6 8.57 us: resp_exchange(): lax.ppermute(pieces[k], 'resp', [(z, z ^ k) for z in range(count)])]
    convert_element_type x4 -> x2, other arithmetic: 7.77 us -> 4.27 us  [split_wide(): lower = (wide - upper.astype(jnp.float32)).astype(jnp.bfloat16)]
    add x7, other arithmetic: 10.5 us -> 7.38 us  [the longest x2 3.3 us: scattered(): pair_sum = mine + other]
    dot_general x6, matrix products: 5.77 us -> 2.71 us  [narrow_first(): jnp.einsum(form, narrow, lower, preferred_element_type=jnp.float32)]
    unnamed x66 -> x80, local copies, waits for them, and re-layouts: 21.7 us -> 20.1 us
  transfers between devices with their start and end apart: 5 -> 28, of which waited for: 5 -> 5; matrix products, arithmetic and copies ran while one was open for 20% -> 43% of each run, Pallas kernels for 0% -> 0%
where the time goes in v1:
time: 127 us
  matrix products  36.6 us (29%)
  starting transfers between devices  34.1 us (27%)
  local copies, waits for them, and re-layouts  23 us (18%)
  other arithmetic  17.4 us (14%)
  waiting for transfers between devices  13 us (10%)
  between operations  2.59 us (2%)
    ppermute x18, starting transfers between devices, plane_exchange(): lax.ppermute(pieces[k], PLANE, [(b, b ^ 2 * k) for b in range(count)])  23.9 us
    unnamed x80, local copies, waits for them, and re-layouts  20.1 us
    ppermute x6, starting transfers between devices, resp_exchange(): lax.ppermute(pieces[k], 'resp', [(z, z ^ k) for z in range(count)])  9.24 us
    ppermute x6, waiting for transfers between devices, resp_exchange(): lax.ppermute(pieces[k], 'resp', [(z, z ^ k) for z in range(count)])  8.57 us
    dot_general x6, matrix products, narrow_first(): first = jnp.einsum(form, narrow, upper, preferred_element_type=jnp.float32)  5.16 us
    dot_general x2, matrix products, backward_pieces(): jnp.einsum('hts,thd->shd', grad_scores, query, preferred_element_type=jnp...  4.81 us
    ppermute x18, waiting for transfers between devices, plane_exchange(): lax.ppermute(pieces[k], PLANE, [(b, b ^ 2 * k) for b in range(count)])  4.45 us
    convert_element_type x2, other arithmetic, split_wide(): lower = (wide - upper.astype(jnp.float32)).astype(jnp.bfloat16)  4.27 us
  transfers between devices with their start and end apart: 28, of which 5 were waited for; matrix products, arithmetic and copies ran while one was open for 43% of the time, Pallas kernels for 0%

profile of v1, /device:TPU:0, one launch (start us, length us, event | category | flops | bytes accessed | tf_op | source)
XLA Modules:
  0.0 126.8 jit_solution(6977838143348009110)
XLA Ops:
  0.7 1.8 %subtract_convert_fusion = (bf16[256,16,128]{2,1,0:T(8,128)(2,1)S(1)}, bf16[256,16,128]{2,1,0:T(8,128)(2,1)S(1)}) fusion(bf16[256,16,128]{2,1,0:T(8,128)(2,1)} %param.10, f32[256]{0:T(256)S(1)} %multiply_rsqrt_fusion.1), kind=kLoop, calls=%fused_computation.20 | loop fusion | flops 3145728 | bytes 3146752 | tf_op jit(solution)/shard_map/convert_element_type | solution.py:67
  6.5 2.5 %subtract_convert_fusion.1 = (bf16[512,8,128]{2,1,0:T(8,128)(2,1)}, bf16[512,8,128]{2,1,0:T(8,128)(2,1)}) fusion(f32[512]{0:T(512)S(1)} %multiply_rsqrt_fusion, bf16[1,512,8,128]{3,2,1,0:T(8,128)(2,1)S(1)} %copy-done.8), kind=kLoop, calls=%fused_computation.23 | loop fusion | flops 3145728 | bytes 3147776 | tf_op jit(solution)/shard_map/convert_element_type | solution.py:67
  9.0 2.5 %fusion.19 = f32[8,128,128]{2,1,0:T(8,128)S(1)} fusion(bf16[512,8,128]{2,1,0:T(8,128)(2,1)} %get-tuple-element.39, bf16[1,512,8,128]{3,2,1,0:T(8,128)(2,1)} %param.17, f32[]{:T(128)} %bitcast.92, pred[512]{0:T(512)(128)(4,1)S(1)} %iota_compare_fusion.2), kind=kOutput, calls=%fused_computation.40 | convolution fusion | flops 136314880 | bytes 2621956 | tf_op jit(solution)/shard_map/thd,the->hde/dot_general | solution.py:79
  13.1 3.5 %collective-permute-start.14 = (f32[256,128]{1,0:T(8,128)}, f32[256,128]{1,0:T(8,128)S(1)}, u32[]{:S(2)}, u32[]{:S(2)}) collective-permute-start(f32[256,128]{1,0:T(8,128)} %get-tuple-element.60), channel_id=1, source_target_pairs={{0,24},{4,28},{8,16},{12,20},{16,8},{20,12},{24,0},{28,4},{1,25},{... | collective-permute-start | bytes 393224 | tf_op jit(solution)/shard_map/ppermute | solution.py:18
  20.6 2.0 %fusion.49 = f32[16,256,128]{2,1,0:T(8,128)} fusion(bf16[16,256,256]{2,1,0:T(8,128)(2,1)S(1)} %select_convert_fusion.2, bf16[256,16,128]{2,1,0:T(8,128)(2,1)S(1)} %copy-done.4), kind=kOutput, calls=%fused_computation.73 | convolution fusion | flops 268435456 | bytes 5242880 | tf_op jit(solution)/shard_map/hts,shd->thd/dot_general | solution.py:113
  22.6 2.3 %fusion.31 = f32[16,256,128]{2,1,0:T(8,128)} fusion(bf16[16,256,256]{2,1,0:T(8,128)(2,1)S(1)} %select_convert_fusion.2, bf16[256,16,128]{2,1,0:T(8,128)(2,1)S(1)} %copy-done.11), kind=kOutput, calls=%fused_computation.55 | convolution fusion | flops 268435456 | bytes 5242880 | tf_op jit(solution)/shard_map/hts,thd->shd/dot_general | solution.py:119
  26.5 2.7 %select_convert_fusion = bf16[8,512,512]{2,1,0:T(8,128)(2,1)S(1)} fusion(f32[512]{0:T(512)S(1)} %multiply_rsqrt_fusion, pred[512,512]{1,0:T(8,128)(4,1)S(1)} %iota_compare_fusion, bf16[512,8,128]{2,1,0:T(8,128)(2,1)S(1)} %bitcast.100, bf16[1,512,8,128]{3,2,1,0:T(8,128)(2,1)S(1)} %copy-done.20, f32[]{:T(128)} %bitcast.96, pred[512]{0:T(512)(128)(4,1)S(1)} %iota_compare_fusion.2), kind=kOutput, calls=%fused_computation | convolution fusion | flops 545259520 | bytes 6556164 | tf_op jit(solution)/shard_map/the,she->hts/dot_general | solution.py:107
  29.2 2.5 %fusion.12 = bf16[1,512,8,128]{3,1,2,0:T(8,128)(2,1)} fusion(bf16[8,512,512]{2,1,0:T(8,128)(2,1)S(1)} %select_convert_fusion, bf16[512,8,128]{2,1,0:T(8,128)(2,1)S(1)} %bitcast.111), kind=kOutput, calls=%fused_computation.29 | convolution fusion | flops 537395200 | bytes 6291456 | tf_op jit(solution)/shard_map/hts,thd->shd/dot_general | solution.py:119
  31.7 2.0 %fusion.43 = f32[16,256,128]{2,1,0:T(8,128)} fusion(bf16[16,256,256]{2,1,0:T(8,128)(2,1)S(1)} %select_convert_fusion.3, bf16[256,16,128]{2,1,0:T(8,128)(2,1)S(1)} %copy-done.3), kind=kOutput, calls=%fused_computation.67 | convolution fusion | flops 268435456 | bytes 5242880 | tf_op jit(solution)/shard_map/hts,she->the/dot_general | solution.py:87
  33.8 2.0 %fusion.13 = bf16[1,512,8,128]{1,3,2,0:T(8,128)(2,1)} fusion(bf16[8,512,512]{2,1,0:T(8,128)(2,1)S(1)} %select_convert_fusion.1, bf16[1,512,8,128]{3,2,1,0:T(8,128)(2,1)S(1)} %copy-done.20, f32[]{:T(128)} %bitcast.93, pred[512]{0:T(512)(128)(4,1)S(1)} %iota_compare_fusion.2), kind=kOutput, calls=%fused_computation.30 | convolution fusion | flops 539492352 | bytes 6291972 | tf_op jit(solution)/shard_map/hts,the->she/dot_general | solution.py:120
  35.8 2.1 %fusion.52 = f32[16,256,128]{2,1,0:T(8,128)} fusion(bf16[16,256,256]{2,1,0:T(8,128)(2,1)S(1)} %select_convert_fusion.3, bf16[256,16,128]{2,1,0:T(8,128)(2,1)S(1)} %copy-done.2), kind=kOutput, calls=%fused_computation.80 | convolution fusion | flops 268435456 | bytes 5242880 | tf_op jit(solution)/shard_map/hts,the->she/dot_general | solution.py:120
  37.9 2.9 %copy.144 = bf16[1,512,8,128]{3,2,1,0:T(8,128)(2,1)} copy(bf16[1,512,8,128]{3,1,2,0:T(8,128)(2,1)} %fusion.12) | data formatting | bytes 2097152
  40.8 2.4 %copy.145 = bf16[1,512,8,128]{3,2,1,0:T(8,128)(2,1)} copy(bf16[1,512,8,128]{1,3,2,0:T(8,128)(2,1)} %fusion.13) | data formatting | bytes 2097152
  44.2 4.1 %collective-permute-start.19 = (f32[256,128]{1,0:T(8,128)S(1)}, f32[256,128]{1,0:T(8,128)S(1)}, u32[]{:S(2)}, u32[]{:S(2)}) collective-permute-start(f32[256,128]{1,0:T(8,128)S(1)} %get-tuple-element.53), channel_id=1, source_target_pairs={{0,3},{1,2},{2,1},{3,0},{4,7},{5,6},{6,5},{7,4},{8,11},{9,10},{10,... | collective-permute-start | bytes 393224 | tf_op jit(solution)/shard_map/ppermute | solution.py:26
  50.6 2.7 %collective-permute-start.24 = (f32[256,128]{1,0:T(8,128)S(1)}, f32[256,128]{1,0:T(8,128)S(1)}, u32[]{:S(2)}, u32[]{:S(2)}) collective-permute-start(f32[256,128]{1,0:T(8,128)S(1)} %get-tuple-element.46), channel_id=1, source_target_pairs={{0,24},{4,28},{8,16},{12,20},{16,8},{20,12},{24,0},{28,4},{1,25},{... | collective-permute-start | bytes 393224 | tf_op jit(solution)/shard_map/ppermute | solution.py:18
  57.1 3.0 %collective-permute-done.18 = f32[256,128]{1,0:T(8,128)S(1)} collective-permute-done((f32[256,128]{1,0:T(8,128)S(1)}, f32[256,128]{1,0:T(8,128)S(1)}, u32[]{:S(2)}, u32[]{:S(2)}) %collective-permute-start.18) | collective-permute-done | bytes 131104 | tf_op jit(solution)/shard_map/ppermute | solution.py:26
  66.6 2.9 %collective-permute-start.8 = (f32[256,128]{1,0:T(8,128)S(1)}, f32[256,128]{1,0:T(8,128)S(1)}, u32[]{:S(2)}, u32[]{:S(2)}) collective-permute-start(f32[256,128]{1,0:T(8,128)S(1)} %get-tuple-element.34), channel_id=1, source_target_pairs={{0,3},{1,2},{2,1},{3,0},{4,7},{5,6},{6,5},{7,4},{8,11},{9,10},{10,... | collective-permute-start | bytes 393224 | tf_op jit(solution)/shard_map/ppermute | solution.py:26
  75.5 4.4 %collective-permute-done.9 = f32[256,128]{1,0:T(8,128)S(1)} collective-permute-done((f32[256,128]{1,0:T(8,128)S(1)}, f32[256,128]{1,0:T(8,128)S(1)}, u32[]{:S(2)}, u32[]{:S(2)}) %collective-permute-start.9) | collective-permute-done | bytes 131104 | tf_op jit(solution)/shard_map/ppermute | solution.py:26
  79.9 1.8 %collective-permute-start.6 = (f32[256,128]{1,0:T(8,128)S(1)}, f32[256,128]{1,0:T(8,128)S(1)}, u32[]{:S(2)}, u32[]{:S(2)}) collective-permute-start(f32[256,128]{1,0:T(8,128)S(1)} %get-tuple-element.36), channel_id=1, source_target_pairs={{0,8},{4,12},{8,0},{12,4},{16,24},{20,28},{24,16},{28,20},{1,9},{5... | collective-permute-start | bytes 393224 | tf_op jit(solution)/shard_map/ppermute | solution.py:18
  86.0 2.0 %collective-permute-start.13 = (f32[256,128]{1,0:T(8,128)S(1)}, f32[256,128]{1,0:T(8,128)S(1)}, u32[]{:S(2)}, u32[]{:S(2)}) collective-permute-start(f32[256,128]{1,0:T(8,128)S(1)} %get-tuple-element.64), channel_id=1, source_target_pairs={{0,8},{4,12},{8,0},{12,4},{16,24},{20,28},{24,16},{28,20},{1,9},{5... | collective-permute-start | bytes 393224 | tf_op jit(solution)/shard_map/ppermute | solution.py:18
  88.9 3.7 %collective-permute-done.11 = f32[256,128]{1,0:T(8,128)S(1)} collective-permute-done((f32[256,128]{1,0:T(8,128)S(1)}, f32[256,128]{1,0:T(8,128)S(1)}, u32[]{:S(2)}, u32[]{:S(2)}) %collective-permute-start.11) | collective-permute-done | bytes 131104 | tf_op jit(solution)/shard_map/ppermute | solution.py:18
  94.3 2.0 %copy.95 = f32[8,128,128]{1,2,0:T(8,128)} copy(f32[8,128,128]{2,1,0:T(8,128)} %bitcast.113) | data formatting | bytes 1048576 | tf_op jit(solution)/shard_map/reshape | solution.py:198
  96.3 2.0 %fusion.28 = f32[8,128,512]{1,2,0:T(8,128)S(1)} fusion(bf16[512,8,128]{2,1,0:T(8,128)(2,1)} %bitcast.109, f32[8,128,128]{1,2,0:T(8,128)} %copy.95), kind=kOutput, calls=%fused_computation.52 | convolution fusion | flops 134348800 | bytes 3670016 | tf_op jit(solution)/shard_map/thd,hde->the/dot_general | solution.py:73
  117.9 1.9 %copy.138 = bf16[256,16,128]{2,1,0:T(8,128)(2,1)} copy(bf16[256,16,128]{2,0,1:T(8,128)(2,1)S(1)} %fusion.8) | data formatting | bytes 2097152
  (171 shorter events, 62.6 us)
Async XLA Ops:
  4.7 44.3 %collective-permute-start.20 = (f32[2048,128]{1,0:T(8,128)}, f32[2048,128]{1,0:T(8,128)}, u32[]{:S(2)}, u32[]{:S(2)}) collective-permute-start(f32[2048,128]{1,0:T(8,128)} %bitcast.18), channel_id=1, source_target_pairs={{0,4},{4,0},{8,12},{12,8},{16,20},{20,16},{24,28},{28,24},{1,5},{5... | collective-permute-start | bytes 3145736 | tf_op jit(solution)/shard_map/ppermute | solution.py:11
  13.1 30.1 %collective-permute-start.14 = (f32[256,128]{1,0:T(8,128)}, f32[256,128]{1,0:T(8,128)S(1)}, u32[]{:S(2)}, u32[]{:S(2)}) collective-permute-start(f32[256,128]{1,0:T(8,128)} %get-tuple-element.60), channel_id=1, source_target_pairs={{0,24},{4,28},{8,16},{12,20},{16,8},{20,12},{24,0},{28,4},{1,25},{... | collective-permute-start | bytes 393224 | tf_op jit(solution)/shard_map/ppermute | solution.py:18
  16.6 26.6 %collective-permute-start.15 = (f32[256,128]{1,0:T(8,128)}, f32[256,128]{1,0:T(8,128)S(1)}, u32[]{:S(2)}, u32[]{:S(2)}) collective-permute-start(f32[256,128]{1,0:T(8,128)} %get-tuple-element.59), channel_id=1, source_target_pairs={{0,16},{4,20},{8,24},{12,28},{16,0},{20,4},{24,8},{28,12},{1,17},{... | collective-permute-start | bytes 393224 | tf_op jit(solution)/shard_map/ppermute | solution.py:18
  17.1 26.1 %collective-permute-start.16 = (f32[256,128]{1,0:T(8,128)}, f32[256,128]{1,0:T(8,128)S(1)}, u32[]{:S(2)}, u32[]{:S(2)}) collective-permute-start(f32[256,128]{1,0:T(8,128)} %get-tuple-element.58), channel_id=1, source_target_pairs={{0,8},{4,12},{8,0},{12,4},{16,24},{20,28},{24,16},{28,20},{1,9},{5... | collective-permute-start | bytes 393224 | tf_op jit(solution)/shard_map/ppermute | solution.py:18
  18.7 34.6 %collective-permute-start = (f32[2048,128]{1,0:T(8,128)}, f32[2048,128]{1,0:T(8,128)}, u32[]{:S(2)}, u32[]{:S(2)}) collective-permute-start(f32[2048,128]{1,0:T(8,128)} %bitcast.1), channel_id=1, source_target_pairs={{0,4},{4,0},{8,12},{12,8},{16,20},{20,16},{24,28},{28,24},{1,5},{5... | collective-permute-start | bytes 3145736 | tf_op jit(solution)/shard_map/ppermute | solution.py:11
  44.2 11.4 %collective-permute-start.19 = (f32[256,128]{1,0:T(8,128)S(1)}, f32[256,128]{1,0:T(8,128)S(1)}, u32[]{:S(2)}, u32[]{:S(2)}) collective-permute-start(f32[256,128]{1,0:T(8,128)S(1)} %get-tuple-element.53), channel_id=1, source_target_pairs={{0,3},{1,2},{2,1},{3,0},{4,7},{5,6},{6,5},{7,4},{8,11},{9,10},{10,... | collective-permute-start | bytes 393224 | tf_op jit(solution)/shard_map/ppermute | solution.py:26
  48.3 11.7 %collective-permute-start.18 = (f32[256,128]{1,0:T(8,128)S(1)}, f32[256,128]{1,0:T(8,128)S(1)}, u32[]{:S(2)}, u32[]{:S(2)}) collective-permute-start(f32[256,128]{1,0:T(8,128)S(1)} %get-tuple-element.54), channel_id=1, source_target_pairs={{0,2},{1,3},{2,0},{3,1},{4,6},{5,7},{6,4},{7,5},{8,10},{9,11},{10,... | collective-permute-start | bytes 393224 | tf_op jit(solution)/shard_map/ppermute | solution.py:26
  48.3 13.2 %collective-permute-start.17 = (f32[256,128]{1,0:T(8,128)S(1)}, f32[256,128]{1,0:T(8,128)S(1)}, u32[]{:S(2)}, u32[]{:S(2)}) collective-permute-start(f32[256,128]{1,0:T(8,128)S(1)} %get-tuple-element.52), channel_id=1, source_target_pairs={{0,1},{1,0},{2,3},{3,2},{4,5},{5,4},{6,7},{7,6},{8,9},{9,8},{10,11... | collective-permute-start | bytes 393224 | tf_op jit(solution)/shard_map/ppermute | solution.py:26
  50.6 12.4 %collective-permute-start.24 = (f32[256,128]{1,0:T(8,128)S(1)}, f32[256,128]{1,0:T(8,128)S(1)}, u32[]{:S(2)}, u32[]{:S(2)}) collective-permute-start(f32[256,128]{1,0:T(8,128)S(1)} %get-tuple-element.46), channel_id=1, source_target_pairs={{0,24},{4,28},{8,16},{12,20},{16,8},{20,12},{24,0},{28,4},{1,25},{... | collective-permute-start | bytes 393224 | tf_op jit(solution)/shard_map/ppermute | solution.py:18
  53.3 9.8 %collective-permute-start.22 = (f32[256,128]{1,0:T(8,128)S(1)}, f32[256,128]{1,0:T(8,128)S(1)}, u32[]{:S(2)}, u32[]{:S(2)}) collective-permute-start(f32[256,128]{1,0:T(8,128)S(1)} %get-tuple-element.45), channel_id=1, source_target_pairs={{0,16},{4,20},{8,24},{12,28},{16,0},{20,4},{24,8},{28,12},{1,17},{... | collective-permute-start | bytes 393224 | tf_op jit(solution)/shard_map/ppermute | solution.py:18
  55.5 10.3 %collective-permute-start.4 = (f32[256,128]{1,0:T(8,128)S(1)}, f32[256,128]{1,0:T(8,128)S(1)}, u32[]{:S(2)}, u32[]{:S(2)}) collective-permute-start(f32[256,128]{1,0:T(8,128)S(1)} %get-tuple-element.49), channel_id=1, source_target_pairs={{0,24},{4,28},{8,16},{12,20},{16,8},{20,12},{24,0},{28,4},{1,25},{... | collective-permute-start | bytes 393224 | tf_op jit(solution)/shard_map/ppermute | solution.py:18
  64.8 7.8 %collective-permute-start.21 = (f32[256,128]{1,0:T(8,128)S(1)}, f32[256,128]{1,0:T(8,128)S(1)}, u32[]{:S(2)}, u32[]{:S(2)}) collective-permute-start(f32[256,128]{1,0:T(8,128)S(1)} %get-tuple-element.44), channel_id=1, source_target_pairs={{0,8},{4,12},{8,0},{12,4},{16,24},{20,28},{24,16},{28,20},{1,9},{5... | collective-permute-start | bytes 393224 | tf_op jit(solution)/shard_map/ppermute | solution.py:18
  66.6 8.3 %collective-permute-start.8 = (f32[256,128]{1,0:T(8,128)S(1)}, f32[256,128]{1,0:T(8,128)S(1)}, u32[]{:S(2)}, u32[]{:S(2)}) collective-permute-start(f32[256,128]{1,0:T(8,128)S(1)} %get-tuple-element.34), channel_id=1, source_target_pairs={{0,3},{1,2},{2,1},{3,0},{4,7},{5,6},{6,5},{7,4},{8,11},{9,10},{10,... | collective-permute-start | bytes 393224 | tf_op jit(solution)/shard_map/ppermute | solution.py:26
  69.5 10.4 %collective-permute-start.9 = (f32[256,128]{1,0:T(8,128)S(1)}, f32[256,128]{1,0:T(8,128)S(1)}, u32[]{:S(2)}, u32[]{:S(2)}) collective-permute-start(f32[256,128]{1,0:T(8,128)S(1)} %get-tuple-element.34), channel_id=1, source_target_pairs={{0,2},{1,3},{2,0},{3,1},{4,6},{5,7},{6,4},{7,5},{8,10},{9,11},{10,... | collective-permute-start | bytes 393224 | tf_op jit(solution)/shard_map/ppermute | solution.py:26
  69.5 12.2 %collective-permute-start.10 = (f32[256,128]{1,0:T(8,128)S(1)}, f32[256,128]{1,0:T(8,128)S(1)}, u32[]{:S(2)}, u32[]{:S(2)}) collective-permute-start(f32[256,128]{1,0:T(8,128)S(1)} %get-tuple-element.34), channel_id=1, source_target_pairs={{0,1},{1,0},{2,3},{3,2},{4,5},{5,4},{6,7},{7,6},{8,9},{9,8},{10,11... | collective-permute-start | bytes 393224 | tf_op jit(solution)/shard_map/ppermute | solution.py:26
  71.1 27.7 %collective-permute-start.26 = (f32[256,128]{1,0:T(8,128)}, f32[256,128]{1,0:T(8,128)}, u32[]{:S(2)}, u32[]{:S(2)}) collective-permute-start(f32[256,128]{1,0:T(8,128)} %get-tuple-element.26), channel_id=1, source_target_pairs={{0,8},{4,12},{8,0},{12,4},{16,24},{20,28},{24,16},{28,20},{1,9},{5... | collective-permute-start | bytes 393224 | tf_op jit(solution)/shard_map/ppermute | solution.py:18
  72.6 10.6 %collective-permute-start.3 = (f32[256,128]{1,0:T(8,128)S(1)}, f32[256,128]{1,0:T(8,128)S(1)}, u32[]{:S(2)}, u32[]{:S(2)}) collective-permute-start(f32[256,128]{1,0:T(8,128)S(1)} %get-tuple-element.35), channel_id=1, source_target_pairs={{0,24},{4,28},{8,16},{12,20},{16,8},{20,12},{24,0},{28,4},{1,25},{... | collective-permute-start | bytes 393224 | tf_op jit(solution)/shard_map/ppermute | solution.py:18
  75.0 9.8 %collective-permute-start.5 = (f32[256,128]{1,0:T(8,128)S(1)}, f32[256,128]{1,0:T(8,128)S(1)}, u32[]{:S(2)}, u32[]{:S(2)}) collective-permute-start(f32[256,128]{1,0:T(8,128)S(1)} %get-tuple-element.37), channel_id=1, source_target_pairs={{0,16},{4,20},{8,24},{12,28},{16,0},{20,4},{24,8},{28,12},{1,17},{... | collective-permute-start | bytes 393224 | tf_op jit(solution)/shard_map/ppermute | solution.py:18
  81.7 17.1 %collective-permute-start.23 = (f32[256,128]{1,0:T(8,128)}, f32[256,128]{1,0:T(8,128)}, u32[]{:S(2)}, u32[]{:S(2)}) collective-permute-start(f32[256,128]{1,0:T(8,128)} %get-tuple-element.33), channel_id=1, source_target_pairs={{0,24},{4,28},{8,16},{12,20},{16,8},{20,12},{24,0},{28,4},{1,25},{... | collective-permute-start | bytes 393224 | tf_op jit(solution)/shard_map/ppermute | solution.py:18
  83.2 9.4 %collective-permute-start.11 = (f32[256,128]{1,0:T(8,128)S(1)}, f32[256,128]{1,0:T(8,128)S(1)}, u32[]{:S(2)}, u32[]{:S(2)}) collective-permute-start(f32[256,128]{1,0:T(8,128)S(1)} %get-tuple-element.66), channel_id=1, source_target_pairs={{0,24},{4,28},{8,16},{12,20},{16,8},{20,12},{24,0},{28,4},{1,25},{... | collective-permute-start | bytes 393224 | tf_op jit(solution)/shard_map/ppermute | solution.py:18
  84.7 8.5 %collective-permute-start.12 = (f32[256,128]{1,0:T(8,128)S(1)}, f32[256,128]{1,0:T(8,128)S(1)}, u32[]{:S(2)}, u32[]{:S(2)}) collective-permute-start(f32[256,128]{1,0:T(8,128)S(1)} %get-tuple-element.65), channel_id=1, source_target_pairs={{0,16},{4,20},{8,24},{12,28},{16,0},{20,4},{24,8},{28,12},{1,17},{... | collective-permute-start | bytes 393224 | tf_op jit(solution)/shard_map/ppermute | solution.py:18
  86.0 7.4 %collective-permute-start.13 = (f32[256,128]{1,0:T(8,128)S(1)}, f32[256,128]{1,0:T(8,128)S(1)}, u32[]{:S(2)}, u32[]{:S(2)}) collective-permute-start(f32[256,128]{1,0:T(8,128)S(1)} %get-tuple-element.64), channel_id=1, source_target_pairs={{0,8},{4,12},{8,0},{12,4},{16,24},{20,28},{24,16},{28,20},{1,9},{5... | collective-permute-start | bytes 393224 | tf_op jit(solution)/shard_map/ppermute | solution.py:18
  93.3 16.4 %collective-permute-start.7 = (f32[1024,128]{1,0:T(8,128)}, f32[1024,128]{1,0:T(8,128)}, u32[]{:S(2)}, u32[]{:S(2)}) collective-permute-start(f32[1024,128]{1,0:T(8,128)} %pad_maximum_fusion), channel_id=1, source_target_pairs={{0,4},{4,0},{8,12},{12,8},{16,20},{20,16},{24,28},{28,24},{1,5},{5... | collective-permute-start | bytes 1572872 | tf_op jit(solution)/shard_map/ppermute | solution.py:11
  100.4 9.2 %collective-permute-start.27 = (f32[1024,128]{1,0:T(8,128)S(1)}, f32[1024,128]{1,0:T(8,128)S(1)}, u32[]{:S(2)}, u32[]{:S(2)}) collective-permute-start(f32[1024,128]{1,0:T(8,128)S(1)} %pad_maximum_fusion.2), channel_id=1, source_target_pairs={{0,4},{4,0},{8,12},{12,8},{16,20},{20,16},{24,28},{28,24},{1,5},{5... | collective-permute-start | bytes 1572872 | tf_op jit(solution)/shard_map/ppermute | solution.py:11
  (40 other events, 213.9 us)

commit v2 on v0

v2 whole, which is shorter than its diff:
```python
import functools

import jax
import jax.numpy as jnp
from jax import lax
from jax.experimental import pallas as pl
from jax.experimental.pallas import tpu as pltpu
from jax.sharding import PartitionSpec as P

PLANE = ("ctx", "head")
BLOCK = 256
F32 = jnp.float32
BF16 = jnp.bfloat16
ROWS_ROWS = (((0,), (0,)), ((), ()))
LAST_LAST = (((1,), (1,)), ((), ()))
LAST_ROWS = (((1,), (0,)), ((), ()))


def pair_step(block):
    count = lax.axis_size(PLANE)
    return lax.ppermute(block, PLANE, [(b, b ^ 1) for b in range(count)])


def plane_exchange(pieces):
    count = lax.axis_size(PLANE)
    moved = [pieces[0]]
    for k in range(1, len(pieces)):
        moved.append(lax.ppermute(pieces[k], PLANE, [(b, b ^ (2 * k)) for b in range(count)]))
    return moved


def resp_exchange(pieces):
    count = lax.axis_size("resp")
    moved = [pieces[0]]
    for k in range(1, len(pieces)):
        moved.append(lax.ppermute(pieces[k], "resp", [(z, z ^ k) for z in range(count)]))
    return moved


def dot(a, b, dims):
    return lax.dot_general(a, b, dims, preferred_element_type=F32)


def row_scale(first_row, row_total, head_size):
    rows = lax.broadcasted_iota(jnp.int32, (row_total, head_size), 0) + first_row
    return lax.rsqrt(float(head_size) * (rows.astype(F32) + 1.0))


def by_head(array):
    return jnp.swapaxes(array, 0, 1)


def weighted_by_head(cotangent, weight, length):
    rows = lax.broadcasted_iota(jnp.int32, cotangent.shape, 1)
    return (weight * jnp.where(rows < length, cotangent.astype(F32), 0.0)).astype(BF16)


def load(sources, buffers, arrived):
    copies = []
    for i, (source, buffer) in enumerate(zip(sources, buffers)):
        copies.append(pltpu.make_async_copy(source, buffer, arrived.at[i]))
        copies[-1].start()
    return copies


def moments_kernel(steps, place, weight, *refs):
    sources, refs = refs[:6], refs[6:]
    sent, kept, key, value, query, cotangent, r_query, r_cotangent = refs[:8]
    pieces, refs = refs[8 : 8 + steps], refs[8 + steps :]
    buffers, (r_moment, arrived) = refs[:6], refs[6:]
    copies = load(sources, buffers, arrived)
    member, pair, first_row, reply_first, length = (place[i] for i in range(5))
    heads, rows, size = query.shape
    half = heads // 2
    halves = ((sent, (1 - member) * half), (kept, member * half))
    for i, target in enumerate((key, value)):
        copies[i].wait()
        target[...] = by_head(buffers[i][...])
    for target, base in halves:

        def state(j, carry, target=target, base=base):
            h = base + j
            target[pl.ds(j * size, size), :] = dot(key[h], value[h], ROWS_ROWS)
            return carry

        lax.fori_loop(0, half, state, 0, unroll=True)
    for i, target in enumerate((query, cotangent)):
        copies[2 + i].wait()
        target[...] = by_head(buffers[2 + i][...])
    scale = row_scale(first_row, rows, size)
    for target, base in halves:

        def moment(j, carry, target=target, base=base):
            h = base + j
            scaled = (query[h].astype(F32) * scale).astype(BF16)
            target[pl.ds((half + j) * size, size), :] = dot(scaled, cotangent[h], ROWS_ROWS)
            return carry

        lax.fori_loop(0, half, moment, 0, unroll=True)
    copies[4].wait()
    r_query[...] = by_head(buffers[4][...])
    copies[5].wait()
    r_cotangent[...] = weighted_by_head(by_head(buffers[5][...]), weight[0], length)
    scale = row_scale(reply_first, r_query.shape[1], size)
    for h in range(r_query.shape[0]):
        scaled = (r_query[h].astype(F32) * scale).astype(BF16)
        r_moment[pl.ds(h * size, size), :] = dot(scaled, r_cotangent[h], ROWS_ROWS)
    piece_rows = pieces[0].shape[0]
    for k in range(steps):
        start = pl.multiple_of((pair ^ k) * piece_rows, piece_rows)
        pieces[k][...] = r_moment[pl.ds(start, piece_rows), :]


def pair_kernel(steps, place, kept, received, *pieces):
    pair = place[1]
    half_rows = kept.shape[0] // 2
    piece_rows = half_rows // steps
    for k in range(steps):
        start = pl.multiple_of((pair ^ k) * piece_rows, piece_rows)
        for part in range(2):
            source = pl.ds(part * half_rows + start, piece_rows)
            pieces[k][pl.ds(part * piece_rows, piece_rows), :] = kept[source, :] + received[source, :]


def choose_kernel(steps, place, follows, *refs):
    pieces, outs = refs[:steps], refs[steps:]
    start = place[1] ^ place[5]
    for j in range(steps):
        chosen = pieces[0][...]
        for k in range(1, steps):
            chosen = jnp.where((start ^ j) == k, pieces[k][...], chosen)
        outs[j][...] = chosen


def prefix_kernel(steps, place, follows, *refs):
    parts, moments, refs = refs[:steps], refs[steps : 2 * steps], refs[2 * steps :]
    final, returned = refs[0], refs[1:]
    pair = place[1]
    rows = final.shape[0]
    states = [part[pl.ds(0, rows), :] for part in parts]
    total = states[0]
    for k in range(1, steps):
        total = total + states[k]
    final[...] = total
    for k in range(steps):
        before = jnp.zeros_like(total)
        for m in range(steps):
            before = before + jnp.where((pair ^ m) < (pair ^ k), states[m], 0.0)
        returned[k][pl.ds(0, rows), :] = before
    reply_moment = moments[0][...]
    for k in range(1, steps):
        reply_moment = reply_moment + moments[k][...]
    later = [part[pl.ds(rows, rows), :] for part in parts]
    for k in range(steps):
        after = reply_moment
        for m in range(steps):
            after = after + jnp.where((pair ^ m) > (pair ^ k), later[m], 0.0)
        returned[k][pl.ds(rows, rows), :] = after


def halves_kernel(steps, place, follows, kept, received, *refs):
    pieces, mine, to_other = refs[:steps], refs[steps], refs[steps + 1]
    member, pair = place[0], place[1]
    half_rows = kept.shape[0] // 2
    piece_rows = half_rows // steps
    first = member == 0
    for k in range(steps):
        start = pl.multiple_of((pair ^ k) * piece_rows, piece_rows)
        for part in range(2):
            rows = pl.ds(part * half_rows + start, piece_rows)
            sums = pieces[k][pl.ds(part * piece_rows, piece_rows), :]
            add_other = first if part else jnp.logical_not(first)
            mine[rows, :] = sums + jnp.where(add_other, received[rows, :], 0.0)
            to_other[rows, :] = sums + jnp.where(add_other, 0.0, kept[rows, :])


def prompt_local_kernel(
    place,
    query,
    key,
    value,
    cotangent,
    reply_key,
    reply_value,
    follows,
    inner,
    query_part,
    key_part,
    value_part,
    r_key,
    r_value,
    mask,
    key_buffer,
    value_buffer,
    arrived,
):
    heads, rows, size = query.shape
    copies = load((reply_key, reply_value), (key_buffer, value_buffer), arrived)
    mask[...] = causal_weights(place[2], rows, size)

    def one(h, carry):
        mixing = (dot(query[h], key[h], LAST_LAST) * mask[...]).astype(BF16)
        grad_mixing = (dot(cotangent[h], value[h], LAST_LAST) * mask[...]).astype(BF16)
        inner[h] = dot(mixing, value[h], LAST_ROWS)
        query_part[h] = dot(grad_mixing, key[h], LAST_ROWS)
        key_part[h] = dot(grad_mixing, query[h], ROWS_ROWS)
        value_part[h] = dot(mixing, cotangent[h], ROWS_ROWS)
        return carry

    lax.fori_loop(0, heads, one, 0, unroll=4)
    copies[0].wait()
    r_key[...] = by_head(key_buffer[...])
    copies[1].wait()
    r_value[...] = by_head(value_buffer[...])


def causal_weights(first_row, row_total, head_size):
    rows = lax.broadcasted_iota(jnp.int32, (row_total, row_total), 0)
    columns = lax.broadcasted_iota(jnp.int32, (row_total, row_total), 1)
    scale = lax.rsqrt(float(head_size) * ((rows + first_row).astype(F32) + 1.0))
    return jnp.where(rows >= columns, scale, 0.0)


def reply_local(first_head, first_row, query, key, value, cotangent, outs, mask):
    inner, query_part, key_rows, value_rows = outs
    heads, rows, size = inner.shape
    block = mask.shape[1]
    count = rows // block
    for i in range(count):
        mask[i] = causal_weights(first_row + i * block, block, size)

    def one(own, carry):
        h = first_head + own
        key_sum, value_sum = [None] * count, [None] * count
        for i in range(count):
            mine = pl.ds(i * block, block)
            inner_sum, query_sum = None, None
            for j in range(i + 1):
                other = pl.ds(j * block, block)
                weights = mask[i] if i == j else mask[i][:, :1]
                mixing = (dot(query[h, mine], key[h, other], LAST_LAST) * weights).astype(BF16)
                grad_mixing = dot(cotangent[h, mine], value[h, other], LAST_LAST) * weights
                grad_mixing = grad_mixing.astype(BF16)
                terms = (
                    dot(mixing, value[h, other], LAST_ROWS),
                    dot(grad_mixing, key[h, other], LAST_ROWS),
                    dot(grad_mixing, query[h, mine], ROWS_ROWS),
                    dot(mixing, cotangent[h, mine], ROWS_ROWS),
                )
                inner_sum = terms[0] if j == 0 else inner_sum + terms[0]
                query_sum = terms[1] if j == 0 else query_sum + terms[1]
                key_sum[j] = terms[2] if i == j else key_sum[j] + terms[2]
                value_sum[j] = terms[3] if i == j else value_sum[j] + terms[3]
            inner[own, mine] = inner_sum
            query_part[own, mine] = query_sum
        for j in range(count):
            other = pl.ds(j * block, block)
            key_rows[own, other] = key_sum[j].astype(BF16)
            value_rows[own, other] = value_sum[j].astype(BF16)
        return carry

    lax.fori_loop(0, heads, one, 0, unroll=True)


def reply_first_kernel(place, query, key, value, cotangent, follows, *refs):
    reply_local(0, place[3], query, key, value, cotangent, refs[:4], refs[4])


def reply_second_kernel(
    place,
    query,
    key,
    value,
    cotangent,
    key_first,
    value_first,
    follows,
    inner,
    query_part,
    key_grad,
    value_grad,
    key_rows,
    value_rows,
    mask,
    staged,
    left,
):
    first_head = key_first.shape[0]
    outs = (inner, query_part, key_rows, value_rows)
    reply_local(first_head, place[3], query, key, value, cotangent, outs, mask)
    copies = []
    parts = ((key_first, key_rows, key_grad), (value_first, value_rows, value_grad))
    for i, (first, second, target) in enumerate(parts):
        staged[i] = by_head(jnp.concatenate([first[...], second[...]], 0))
        copies.append(pltpu.make_async_copy(staged.at[i], target, left.at[i]))
        copies[-1].start()
    for copy in copies:
        copy.wait()


def prompt_final_kernel(
    place,
    mine,
    other,
    inner,
    query_part,
    key_part,
    value_part,
    query,
    key,
    value,
    cotangent,
    output,
    query_grad,
    key_grad,
    value_grad,
    before,
    after,
    held,
    staged,
    left,
):
    member, first_row = place[0], place[2]
    heads, rows, size = query.shape
    half = heads // 2
    scale = row_scale(first_row, rows, size)

    def narrow(target, offset):
        for source, base in ((mine, member * half), (other, (1 - member) * half)):
            for j in range(half):
                target[base + j] = source[pl.ds((offset + j) * size, size), :].astype(BF16)

    def finish(i, target):
        staged[i] = by_head(held[...])
        copy = pltpu.make_async_copy(staged.at[i], target, left.at[i])
        copy.start()
        return copy

    narrow(before, 0)
    for h in range(heads):
        held[h] = (inner[h] + scale * dot(query[h], before[h], LAST_ROWS)).astype(BF16)
    copies = [finish(0, output)]
    for h in range(heads):
        part = scale * dot(cotangent[h], before[h], LAST_LAST)
        held[h] = (query_part[h] + part).astype(BF16)
    copies.append(finish(1, query_grad))
    narrow(after, half)
    for h in range(heads):
        held[h] = (key_part[h] + dot(value[h], after[h], LAST_LAST)).astype(BF16)
    copies.append(finish(2, key_grad))
    for h in range(heads):
        held[h] = (value_part[h] + dot(key[h], after[h], LAST_ROWS)).astype(BF16)
    copies.append(finish(3, value_grad))
    for copy in copies:
        copy.wait()


def reply_final_kernel(steps, place, follows, *refs):
    pieces, refs = refs[:steps], refs[steps:]
    inner, query_part, (query, cotangent, output, query_grad) = refs[:2], refs[2:4], refs[4:8]
    state, held, staged, left = refs[8:]
    half = inner[0].shape[0]
    pair, first_row, length = place[1], place[3], place[4]
    heads, rows, size = query.shape
    piece_rows = pieces[0].shape[0]
    for k in range(steps):
        start = pl.multiple_of((pair ^ k) * piece_rows, piece_rows)
        state[pl.ds(start, piece_rows), :] = pieces[k][...].astype(BF16)
    scale = row_scale(first_row, rows, size)
    live = lax.broadcasted_iota(jnp.int32, (rows, size), 0) < length
    copies = []

    def finish(i, target):
        staged[i] = by_head(held[...])
        copies.append(pltpu.make_async_copy(staged.at[i], target, left.at[i]))
        copies[-1].start()

    for h in range(heads):
        final = state[pl.ds(h * size, size), :]
        whole = inner[h // half][h % half] + scale * dot(query[h], final, LAST_ROWS)
        held[h] = jnp.where(live, whole, 0.0).astype(BF16)
    finish(0, output)
    for h in range(heads):
        final = state[pl.ds(h * size, size), :]
        part = scale * dot(cotangent[h], final, LAST_LAST)
        held[h] = (query_part[h // half][h % half] + part).astype(BF16)
    finish(1, query_grad)
    for copy in copies:
        copy.wait()


VMEM = pl.BlockSpec(memory_space=pltpu.VMEM)
HBM = pl.BlockSpec(memory_space=pltpu.HBM)
ANY = pl.BlockSpec(memory_space=pl.ANY)


def call(kernel, scalars, arrays, outs, scratch, flops, name):
    arrays = [
        (spec, pltpu.with_memory_space_constraint(array, pltpu.HBM) if spec is HBM else array)
        for spec, array in arrays
    ]
    return pl.pallas_call(
        kernel,
        out_shape=[out for _, out in outs],
        in_specs=[pl.BlockSpec(memory_space=pltpu.SMEM)] * len(scalars) + [s for s, _ in arrays],
        out_specs=[spec for spec, _ in outs],
        scratch_shapes=scratch,
        compiler_params=pltpu.CompilerParams(vmem_limit_bytes=24 << 20),
        cost_estimate=pl.CostEstimate(flops=1, bytes_accessed=1, transcendentals=0),
        name=name,
    )(*scalars, *[array for _, array in arrays])


def held_in(spec, arrays):
    return [(spec, array) for array in arrays]


def shards(
    prompt_query,
    prompt_key,
    prompt_value,
    prompt_cotangent,
    reply_query,
    reply_key,
    reply_value,
    reply_cotangent,
    reply_weight,
    reply_length,
):
    rows, heads, size = prompt_query.shape
    reply_query, reply_key = reply_query[0], reply_key[0]
    reply_value, reply_cotangent = reply_value[0], reply_cotangent[0]
    reply_rows, reply_heads = reply_query.shape[:2]
    block_count = lax.axis_size(PLANE)
    steps = lax.axis_size("resp")
    assert block_count == 2 * steps and steps & (steps - 1) == 0
    block_index = lax.axis_index(PLANE)
    resp_index = lax.axis_index("resp")
    pair_index, member = block_index // 2, block_index % 2
    half_rows = heads // 2 * size
    piece_rows = half_rows // steps
    laps = range(steps)
    place = jnp.stack(
        [
            member,
            pair_index,
            block_index * rows,
            block_count * rows,
            reply_length[0],
            resp_index,
        ]
    ).astype(jnp.int32)
    shape = jax.ShapeDtypeStruct
    prompt_bf16 = shape((rows, heads, size), BF16)
    reply_bf16 = shape((reply_rows, reply_heads, size), BF16)
    prompt_held = shape((heads, rows, size), BF16)
    reply_held = shape((reply_heads, reply_rows, size), BF16)
    prompt_wide = shape((heads, rows, size), F32)
    piece = shape((piece_rows, size), F32)
    two_pieces = shape((2 * piece_rows, size), F32)
    two_halves = shape((2 * half_rows, size), F32)
    state_flops = 2 * heads * rows * size * size
    reply_flops = 2 * reply_heads * reply_rows * size * size
    block = min(BLOCK, reply_rows)

    def scratch(held, count=None):
        return pltpu.VMEM(held.shape if count is None else (count, *held.shape), held.dtype)

    sent, kept, key, value, query, cotangent, r_query, r_cotangent, *moments = call(
        functools.partial(moments_kernel, steps),
        [place, reply_weight],
        held_in(
            HBM,
            [prompt_key, prompt_value, prompt_query, prompt_cotangent, reply_query, reply_cotangent],
        ),
        held_in(
            VMEM, [two_halves] * 2 + [prompt_held] * 4 + [reply_held] * 2 + [piece] * steps
        ),
        [scratch(prompt_bf16)] * 4
        + [scratch(reply_bf16)] * 2
        + [pltpu.VMEM((reply_heads * size, size), F32), pltpu.SemaphoreType.DMA((6,))],
        2 * state_flops + reply_flops,
        "moments",
    )
    received = pair_step(sent)
    moments = plane_exchange(moments)
    pieces = call(
        functools.partial(pair_kernel, steps),
        [place],
        held_in(VMEM, [kept, received]),
        held_in(VMEM, [two_pieces] * steps),
        [],
        half_rows * size * 2,
        "pair_sums",
    )
    parts = plane_exchange(pieces)
    *prompt_parts, r_key, r_value = call(
        prompt_local_kernel,
        [place],
        held_in(VMEM, [query, key, value, cotangent])
        + held_in(HBM, [reply_key, reply_value])
        + held_in(ANY, pieces[:1]),
        held_in(VMEM, [prompt_wide] * 4 + [reply_held] * 2),
        [
            pltpu.VMEM((rows, rows), F32),
            scratch(reply_bf16),
            scratch(reply_bf16),
            pltpu.SemaphoreType.DMA((2,)),
        ],
        6 * state_flops * rows // size,
        "prompt_local",
    )
    moments = call(
        functools.partial(choose_kernel, steps),
        [place],
        held_in(ANY, [r_value]) + held_in(VMEM, moments),
        held_in(VMEM, [piece] * steps),
        [],
        piece_rows * size * steps,
        "choose_moments",
    )
    half_heads = reply_heads // 2
    half_wide = shape((half_heads, reply_rows, size), F32)
    half_held = shape((half_heads, reply_rows, size), BF16)
    masks = pltpu.VMEM((reply_rows // block, block, block), F32)
    reply_arrays = held_in(VMEM, [r_query, r_key, r_value, r_cotangent])
    inner_first, part_first, key_first, value_first = call(
        reply_first_kernel,
        [place],
        reply_arrays + held_in(ANY, moments[:1]),
        held_in(VMEM, [half_wide] * 2 + [half_held] * 2),
        [masks],
        3 * reply_flops * reply_rows // size,
        "reply_first",
    )
    moments = resp_exchange(moments)
    final, *returned = call(
        functools.partial(prefix_kernel, steps),
        [place],
        held_in(ANY, [inner_first]) + held_in(VMEM, [*parts, *moments]),
        held_in(VMEM, [piece] + [two_pieces] * steps),
        [],
        piece_rows * size * steps * steps,
        "prefix_sums",
    )
    finals = resp_exchange([final] * steps)
    returned = plane_exchange(returned)
    inner_second, part_second, reply_dkey, reply_dvalue = call(
        reply_second_kernel,
        [place],
        reply_arrays + held_in(VMEM, [key_first, value_first]) + held_in(ANY, [final]),
        held_in(VMEM, [half_wide] * 2) + held_in(HBM, [reply_bf16] * 2),
        [scratch(half_held)] * 2
        + [masks, scratch(reply_bf16, 2), pltpu.SemaphoreType.DMA((2,))],
        3 * reply_flops * reply_rows // size,
        "reply_second",
    )
    finals = call(
        functools.partial(choose_kernel, steps),
        [place],
        held_in(ANY, [inner_second]) + held_in(VMEM, finals),
        held_in(VMEM, [piece] * steps),
        [],
        piece_rows * size * steps,
        "choose_states",
    )
    chosen = finals[:1]
    finals = plane_exchange(finals)
    mine, to_other = call(
        functools.partial(halves_kernel, steps),
        [place],
        held_in(ANY, chosen) + held_in(VMEM, [kept, received, *returned]),
        held_in(VMEM, [two_halves] * 2),
        [],
        half_rows * size * 4,
        "halves",
    )
    other = pair_step(to_other)
    prompt_output, prompt_dquery, prompt_dkey, prompt_dvalue = call(
        prompt_final_kernel,
        [place],
        held_in(VMEM, [mine, other, *prompt_parts, query, key, value, cotangent]),
        held_in(HBM, [prompt_bf16] * 4),
        [pltpu.VMEM((heads, size, size), BF16)] * 2
        + [scratch(prompt_held), scratch(prompt_bf16, 4), pltpu.SemaphoreType.DMA((4,))],
        4 * state_flops,
        "prompt_final",
    )
    reply_output, reply_dquery = call(
        functools.partial(reply_final_kernel, steps),
        [place],
        held_in(ANY, [prompt_output])
        + held_in(VMEM, [*finals, inner_first, inner_second, part_first, part_second])
        + held_in(VMEM, [r_query, r_cotangent]),
        held_in(HBM, [reply_bf16] * 2),
        [
            pltpu.VMEM((reply_heads * size, size), BF16),
            scratch(reply_held),
            scratch(reply_bf16, 2),
            pltpu.SemaphoreType.DMA((2,)),
        ],
        2 * reply_flops,
        "reply_final",
    )
    return (
        prompt_output,
        reply_output[None],
        prompt_dquery,
        prompt_dkey,
        prompt_dvalue,
        reply_dquery[None],
        reply_dkey[None],
        reply_dvalue[None],
    )


def solution(mesh):
    prompt = P(PLANE, "resp", None)
    reply = P("resp", None, PLANE, None)
    return jax.shard_map(
        shards,
        mesh=mesh,
        in_specs=(prompt,) * 4 + (reply,) * 4 + (P("resp"),) * 2,
        out_specs=(prompt, reply, prompt, prompt, prompt, reply, reply, reply),
        check_vma=False,
    )
```

time: 272 us -> 74.5 us (0.27)
  waiting for transfers between devices: 171 us -> 4.43 us
  matrix products: 38.9 us -> 0 us
  Pallas kernels: 0 us -> 37.1 us
  starting transfers between devices: 0.17 us -> 29.1 us
  other arithmetic: 21.5 us -> 0 us
  local copies, waits for them, and re-layouts: 21.8 us -> 1.31 us
  between operations: 17.6 us -> 2.3 us
    psum x3 -> x0, waiting for transfers between devices: 106 us -> none  [the longest x1 54.5 us: shards(): prompt_total = lax.psum(prompt_local, ('ctx', 'head'))]
    all_gather x2 -> x0, waiting for transfers between devices: 65.1 us -> none  [prefix(): gathered = lax.all_gather(part, axis)]
    dot_general x29 -> x0, matrix products: 38.9 us -> none  [the longest x6 5.77 us: narrow_first(): jnp.einsum(form, narrow, lower, preferred_element_type=jnp.float32)]
    pallas_call x0 -> x11, Pallas kernels: none -> 37.1 us  [call(): pl.pallas_call(kernel, out_shape=[out for _, out in outs], in_specs=[pl.B...]
    ppermute x0 -> x20, starting transfers between devices: none -> 29.1 us  [the longest x12 14.6 us: plane_exchange(): lax.ppermute(pieces[k], PLANE, [(b, b ^ 2 * k) for b in range(count)])]
    unnamed x66 -> x2, local copies, waits for them, and re-layouts: 21.7 us -> 1.23 us
    add x7 -> x0, other arithmetic: 10.5 us -> none  [add_states(): return earlier + later]
    convert_element_type x4 -> x0, other arithmetic: 7.77 us -> none  [split_wide(): lower = (wide - upper.astype(jnp.float32)).astype(jnp.bfloat16)]
  transfers between devices with their start and end apart: 5 -> 20, of which waited for: 5 -> 2; matrix products, arithmetic and copies ran while one was open for 20% -> 0% of each run, Pallas kernels for 0% -> 34%
where the time goes in v2:
time: 74.5 us; the launch traced here: 74.3 us
  Pallas kernels  37.1 us (50%)
  starting transfers between devices  29.1 us (39%)
  waiting for transfers between devices  4.43 us (6%)
  between operations  2.3 us (3%)
  local copies, waits for them, and re-layouts  1.31 us (2%)
    pallas_call x11, Pallas kernels, call(): pl.pallas_call(kernel, out_shape=[out for _, out in outs], in_specs=[pl.B...  37.1 us
    ppermute x12, starting transfers between devices, plane_exchange(): lax.ppermute(pieces[k], PLANE, [(b, b ^ 2 * k) for b in range(count)])  14.6 us
    ppermute x6, starting transfers between devices, resp_exchange(): lax.ppermute(pieces[k], 'resp', [(z, z ^ k) for z in range(count)])  13.9 us
    ppermute x6, waiting for transfers between devices, resp_exchange(): lax.ppermute(pieces[k], 'resp', [(z, z ^ k) for z in range(count)])  2.8 us
    ppermute x12, waiting for transfers between devices, plane_exchange(): lax.ppermute(pieces[k], PLANE, [(b, b ^ 2 * k) for b in range(count)])  1.62 us
  transfers between devices with their start and end apart: 20, of which 2 were waited for; matrix products, arithmetic and copies ran while one was open for 0% of the time, Pallas kernels for 34%

profile of v2, /device:TPU:0, one launch (start us, length us, event | category | flops | bytes accessed | tf_op | source)
XLA Modules:
  0.0 74.3 jit_solution(14582951323670249150)
XLA Ops:
  2.0 6.2 %moments.1 = (f32[2048,128]{1,0:T(8,128)S(1)}, f32[2048,128]{1,0:T(8,128)S(1)}, bf16[16,256,128]{2,1,0:T(8,128)(2,1)S(1)}, bf16[16,256,128]{2,1,0:T(8,128)(2,1)S...) custom-call(s32[6]{0:T(128)S(1)} %stack.19.place, ...), custom_call_target="tpu_custom_call" | custom-call | flops 1 | bytes 1 | tf_op jit(solution)/shard_map/moments/pallas_call | solution.py:402
  8.7 2.6 %collective-permute-start.1 = (f32[256,128]{1,0:T(8,128)S(1)}, f32[256,128]{1,0:T(8,128)S(1)}, u32[]{:S(2)}, u32[]{:S(2)}) collective-permute-start(f32[256,128]{1,0:T(8,128)S(1)} %get-tuple-element.71), channel_id=1, source_target_pairs={{0,8},{4,12},{8,0},{12,4},{16,24},{20,28},{24,16},{28,20},{1,9},{5... | collective-permute-start | bytes 393224 | tf_op jit(solution)/shard_map/ppermute | solution.py:28
  11.3 1.5 %collective-permute-start.2 = (f32[256,128]{1,0:T(8,128)S(1)}, f32[256,128]{1,0:T(8,128)S(1)}, u32[]{:S(2)}, u32[]{:S(2)}) collective-permute-start(f32[256,128]{1,0:T(8,128)S(1)} %get-tuple-element.72), channel_id=1, source_target_pairs={{0,16},{4,20},{8,24},{12,28},{16,0},{20,4},{24,8},{28,12},{1,17},{... | collective-permute-start | bytes 393224 | tf_op jit(solution)/shard_map/ppermute | solution.py:28
  13.5 7.9 %prompt_local.1 = (f32[16,256,128]{2,1,0:T(8,128)S(1)}, f32[16,256,128]{2,1,0:T(8,128)S(1)}, f32[16,256,128]{2,1,0:T(8,128)S(1)}, f32[16,256,128]{2,1,0:T(8,128)...) custom-call(s32[6]{0:T(128)S(1)} %stack.19.place, ...), custom_call_target="tpu_custom_call" | custom-call | flops 1 | bytes 1 | tf_op jit(solution)/shard_map/prompt_local/pallas_call | solution.py:402
  22.1 2.1 %collective-permute-start.7 = (f32[256,128]{1,0:T(8,128)S(1)}, f32[256,128]{1,0:T(8,128)S(1)}, u32[]{:S(2)}, u32[]{:S(2)}) collective-permute-start(f32[256,128]{1,0:T(8,128)S(1)} %get-tuple-element.81), channel_id=1, source_target_pairs={{0,1},{1,0},{2,3},{3,2},{4,5},{5,4},{6,7},{7,6},{8,9},{9,8},{10,11... | collective-permute-start | bytes 393224 | tf_op jit(solution)/shard_map/ppermute | solution.py:36
  24.2 1.5 %collective-permute-start.4 = (f32[512,128]{1,0:T(8,128)S(1)}, f32[512,128]{1,0:T(8,128)S(1)}, u32[]{:S(2)}, u32[]{:S(2)}) collective-permute-start(f32[512,128]{1,0:T(8,128)S(1)} %get-tuple-element.78), channel_id=1, source_target_pairs={{0,8},{4,12},{8,0},{12,4},{16,24},{20,28},{24,16},{28,20},{1,9},{5... | collective-permute-start | bytes 786440 | tf_op jit(solution)/shard_map/ppermute | solution.py:28
  25.7 1.5 %collective-permute-start.5 = (f32[512,128]{1,0:T(8,128)S(1)}, f32[512,128]{1,0:T(8,128)S(1)}, u32[]{:S(2)}, u32[]{:S(2)}) collective-permute-start(f32[512,128]{1,0:T(8,128)S(1)} %get-tuple-element.79), channel_id=1, source_target_pairs={{0,16},{4,20},{8,24},{12,28},{16,0},{20,4},{24,8},{28,12},{1,17},{... | collective-permute-start | bytes 786440 | tf_op jit(solution)/shard_map/ppermute | solution.py:28
  27.7 2.6 %collective-permute-start.8 = (f32[256,128]{1,0:T(8,128)S(1)}, f32[256,128]{1,0:T(8,128)S(1)}, u32[]{:S(2)}, u32[]{:S(2)}) collective-permute-start(f32[256,128]{1,0:T(8,128)S(1)} %get-tuple-element.82), channel_id=1, source_target_pairs={{0,2},{1,3},{2,0},{3,1},{4,6},{5,7},{6,4},{7,5},{8,10},{9,11},{10,... | collective-permute-start | bytes 393224 | tf_op jit(solution)/shard_map/ppermute | solution.py:36
  30.3 1.0 %collective-permute-start.9 = (f32[256,128]{1,0:T(8,128)S(1)}, f32[256,128]{1,0:T(8,128)S(1)}, u32[]{:S(2)}, u32[]{:S(2)}) collective-permute-start(f32[256,128]{1,0:T(8,128)S(1)} %get-tuple-element.83), channel_id=1, source_target_pairs={{0,3},{1,2},{2,1},{3,0},{4,7},{5,6},{6,5},{7,4},{8,11},{9,10},{10,... | collective-permute-start | bytes 393224 | tf_op jit(solution)/shard_map/ppermute | solution.py:36
  31.3 4.9 %reply_first.1 = (f32[4,512,128]{2,1,0:T(8,128)S(1)}, f32[4,512,128]{2,1,0:T(8,128)S(1)}, bf16[4,512,128]{2,1,0:T(8,128)(2,1)S(1)}, bf16[4,512,128]{2,1,0:T(8,128)(2,1)S(1)}) custom-call(s32[6]{0:T(128)S(1)} %stack.19.place, bf16[8,512,128]{2,1,0:T(8,128)(2,1)S(1)} %get-tuple-element.59.query.refs_8_, bf16[8,512,128]{2,1,0:T(8,128)(2,1)S(1)} %get-tuple-element.67.key, ...), custom_call_target="tpu_custom_call" | custom-call | flops 1 | bytes 1 | tf_op jit(solution)/shard_map/reply_first/pallas_call | solution.py:402
  36.1 2.8 %collective-permute-done.8.refs_6_ = f32[256,128]{1,0:T(8,128)S(1)} collective-permute-done((f32[256,128]{1,0:T(8,128)S(1)}, f32[256,128]{1,0:T(8,128)S(1)}, u32[]{:S(2)}, u32[]{:S(2)}) %collective-permute-start.8) | collective-permute-done | bytes 131104 | tf_op jit(solution)/shard_map/ppermute | solution.py:36
  39.8 2.9 %collective-permute-start.12 = (f32[256,128]{1,0:T(8,128)S(1)}, f32[256,128]{1,0:T(8,128)S(1)}, u32[]{:S(2)}, u32[]{:S(2)}) collective-permute-start(f32[256,128]{1,0:T(8,128)S(1)} %get-tuple-element.84.follows.refs_0_), channel_id=1, source_target_pairs={{0,3},{1,2},{2,1},{3,0},{4,7},{5,6},{6,5},{7,4},{8,11},{9,10},{10,... | collective-permute-start | bytes 393224 | tf_op jit(solution)/shard_map/ppermute | solution.py:36
  42.7 1.5 %collective-permute-start.13 = (f32[512,128]{1,0:T(8,128)S(1)}, f32[512,128]{1,0:T(8,128)S(1)}, u32[]{:S(2)}, u32[]{:S(2)}) collective-permute-start(f32[512,128]{1,0:T(8,128)S(1)} %get-tuple-element.88), channel_id=1, source_target_pairs={{0,8},{4,12},{8,0},{12,4},{16,24},{20,28},{24,16},{28,20},{1,9},{5... | collective-permute-start | bytes 786440 | tf_op jit(solution)/shard_map/ppermute | solution.py:28
  44.2 1.5 %collective-permute-start.14 = (f32[512,128]{1,0:T(8,128)S(1)}, f32[512,128]{1,0:T(8,128)S(1)}, u32[]{:S(2)}, u32[]{:S(2)}) collective-permute-start(f32[512,128]{1,0:T(8,128)S(1)} %get-tuple-element.89), channel_id=1, source_target_pairs={{0,16},{4,20},{8,24},{12,28},{16,0},{20,4},{24,8},{28,12},{1,17},{... | collective-permute-start | bytes 786440 | tf_op jit(solution)/shard_map/ppermute | solution.py:28
  46.2 1.1 %collective-permute-start.11 = (f32[256,128]{1,0:T(8,128)S(1)}, f32[256,128]{1,0:T(8,128)S(1)}, u32[]{:S(2)}, u32[]{:S(2)}) collective-permute-start(f32[256,128]{1,0:T(8,128)S(1)} %get-tuple-element.84.follows.refs_0_), channel_id=1, source_target_pairs={{0,2},{1,3},{2,0},{3,1},{4,6},{5,7},{6,4},{7,5},{8,10},{9,11},{10,... | collective-permute-start | bytes 393224 | tf_op jit(solution)/shard_map/ppermute | solution.py:36
  47.3 4.2 %collective-permute-start.10 = (f32[256,128]{1,0:T(8,128)S(1)}, f32[256,128]{1,0:T(8,128)S(1)}, u32[]{:S(2)}, u32[]{:S(2)}) collective-permute-start(f32[256,128]{1,0:T(8,128)S(1)} %get-tuple-element.84.follows.refs_0_), channel_id=1, source_target_pairs={{0,1},{1,0},{2,3},{3,2},{4,5},{5,4},{6,7},{7,6},{8,9},{9,8},{10,11... | collective-permute-start | bytes 393224 | tf_op jit(solution)/shard_map/ppermute | solution.py:36
  51.5 6.6 %reply_second.1 = (f32[4,512,128]{2,1,0:T(8,128)S(1)}, f32[4,512,128]{2,1,0:T(8,128)S(1)}, bf16[512,8,128]{2,1,0:T(8,128)(2,1)}, bf16[512,8,128]{2,1,0:T(8,128)(2,1)}) custom-call(s32[6]{0:T(128)S(1)} %stack.19.place, bf16[8,512,128]{2,1,0:T(8,128)(2,1)S(1)} %get-tuple-element.59.query.refs_8_, bf16[8,512,128]{2,1,0:T(8,128)(2,1)S(1)} %get-tuple-element.67.key, ...), custom_call_target="tpu_custom_call" | custom-call | flops 1 | bytes 1 | tf_op jit(solution)/shard_map/reply_second/pallas_call | solution.py:402
  58.8 0.8 %halves.1 = (f32[2048,128]{1,0:T(8,128)S(1)}, f32[2048,128]{1,0:T(8,128)S(1)}) custom-call(s32[6]{0:T(128)S(1)} %stack.19.place, f32[256,128]{1,0:T(8,128)S(1)} %get-tuple-element.86.follows.refs_0_, f32[2048,128]{1,0:T(8,128)S(1)} %get-tuple-element.64.kept, f32[2048,128]{1,0:T(8,128)S(1)} %collective-permute-done.received, ...), custom_call_target="tpu_custom_call" | custom-call | flops 1 | bytes 1 | tf_op jit(solution)/shard_map/halves/pallas_call | solution.py:402
  59.7 1.7 %collective-permute-start.17 = (f32[256,128]{1,0:T(8,128)S(1)}, f32[256,128]{1,0:T(8,128)S(1)}, u32[]{:S(2)}, u32[]{:S(2)}) collective-permute-start(f32[256,128]{1,0:T(8,128)S(1)} %get-tuple-element.98), channel_id=1, source_target_pairs={{0,8},{4,12},{8,0},{12,4},{16,24},{20,28},{24,16},{28,20},{1,9},{5... | collective-permute-start | bytes 393224 | tf_op jit(solution)/shard_map/ppermute | solution.py:28
  61.4 1.5 %collective-permute-start.18 = (f32[256,128]{1,0:T(8,128)S(1)}, f32[256,128]{1,0:T(8,128)S(1)}, u32[]{:S(2)}, u32[]{:S(2)}) collective-permute-start(f32[256,128]{1,0:T(8,128)S(1)} %get-tuple-element.99), channel_id=1, source_target_pairs={{0,16},{4,20},{8,24},{12,28},{16,0},{20,4},{24,8},{28,12},{1,17},{... | collective-permute-start | bytes 393224 | tf_op jit(solution)/shard_map/ppermute | solution.py:28
  63.3 4.9 %prompt_final.1 = (bf16[256,16,128]{2,1,0:T(8,128)(2,1)}, bf16[256,16,128]{2,1,0:T(8,128)(2,1)}, bf16[256,16,128]{2,1,0:T(8,128)(2,1)}, bf16[256,16,128]{2,1,0:T(8,128)(2,1)}) custom-call(s32[6]{0:T(128)S(1)} %stack.19.place, f32[2048,128]{1,0:T(8,128)S(1)} %get-tuple-element.91.mine, f32[2048,128]{1,0:T(8,128)S(1)} %collective-permute-done.16.other, ...), custom_call_target="tpu_custom_call" | custom-call | flops 1 | bytes 1 | tf_op jit(solution)/shard_map/prompt_final/pallas_call | solution.py:402
  68.2 1.6 %collective-permute-done.18.refs_2_ = f32[256,128]{1,0:T(8,128)S(1)} collective-permute-done((f32[256,128]{1,0:T(8,128)S(1)}, f32[256,128]{1,0:T(8,128)S(1)}, u32[]{:S(2)}, u32[]{:S(2)}) %collective-permute-start.18) | collective-permute-done | bytes 131104 | tf_op jit(solution)/shard_map/ppermute | solution.py:28
  69.8 1.2 %copy-done = bf16[256,16,128]{2,1,0:T(8,128)(2,1)S(1)} copy-done((bf16[256,16,128]{2,1,0:T(8,128)(2,1)S(1)}, bf16[256,16,128]{2,1,0:T(8,128)(2,1)}, u32[]{:S(2)}) %copy-start) | copy-done | bytes 1048600
  71.0 3.1 %reply_final.1 = (bf16[512,8,128]{2,1,0:T(8,128)(2,1)}, bf16[512,8,128]{2,1,0:T(8,128)(2,1)}) custom-call(s32[6]{0:T(128)S(1)} %stack.19.place, bf16[256,16,128]{2,1,0:T(8,128)(2,1)S(1)} %copy-done, f32[256,128]{1,0:T(8,128)S(1)} %get-tuple-element.86.follows.refs_0_, f32[256,128]{1,0:T(8,128)S(1)} %collective-permute-done.17.refs_1_, ...), custom_call_target="tpu_custom_call" | custom-call | flops 1 | bytes 1 | tf_op jit(solution)/shard_map/reply_final/pallas_call | solution.py:402
  (30 shorter events, 4.8 us)
Async XLA Ops:
  8.2 4.6 %collective-permute-start = (f32[2048,128]{1,0:T(8,128)S(1)}, f32[2048,128]{1,0:T(8,128)S(1)}, u32[]{:S(2)}, u32[]{:S(2)}) collective-permute-start(f32[2048,128]{1,0:T(8,128)S(1)} %get-tuple-element.65), channel_id=1, source_target_pairs={{0,4},{4,0},{8,12},{12,8},{16,20},{20,16},{24,28},{28,24},{1,5},{5... | collective-permute-start | bytes 3145736 | tf_op jit(solution)/shard_map/ppermute | solution.py:21
  8.7 12.7 %collective-permute-start.1 = (f32[256,128]{1,0:T(8,128)S(1)}, f32[256,128]{1,0:T(8,128)S(1)}, u32[]{:S(2)}, u32[]{:S(2)}) collective-permute-start(f32[256,128]{1,0:T(8,128)S(1)} %get-tuple-element.71), channel_id=1, source_target_pairs={{0,8},{4,12},{8,0},{12,4},{16,24},{20,28},{24,16},{28,20},{1,9},{5... | collective-permute-start | bytes 393224 | tf_op jit(solution)/shard_map/ppermute | solution.py:28
  11.3 10.2 %collective-permute-start.2 = (f32[256,128]{1,0:T(8,128)S(1)}, f32[256,128]{1,0:T(8,128)S(1)}, u32[]{:S(2)}, u32[]{:S(2)}) collective-permute-start(f32[256,128]{1,0:T(8,128)S(1)} %get-tuple-element.72), channel_id=1, source_target_pairs={{0,16},{4,20},{8,24},{12,28},{16,0},{20,4},{24,8},{28,12},{1,17},{... | collective-permute-start | bytes 393224 | tf_op jit(solution)/shard_map/ppermute | solution.py:28
  12.8 8.6 %collective-permute-start.3 = (f32[256,128]{1,0:T(8,128)S(1)}, f32[256,128]{1,0:T(8,128)S(1)}, u32[]{:S(2)}, u32[]{:S(2)}) collective-permute-start(f32[256,128]{1,0:T(8,128)S(1)} %get-tuple-element.73), channel_id=1, source_target_pairs={{0,24},{4,28},{8,16},{12,20},{16,8},{20,12},{24,0},{28,4},{1,25},{... | collective-permute-start | bytes 393224 | tf_op jit(solution)/shard_map/ppermute | solution.py:28
  22.1 8.2 %collective-permute-start.7 = (f32[256,128]{1,0:T(8,128)S(1)}, f32[256,128]{1,0:T(8,128)S(1)}, u32[]{:S(2)}, u32[]{:S(2)}) collective-permute-start(f32[256,128]{1,0:T(8,128)S(1)} %get-tuple-element.81), channel_id=1, source_target_pairs={{0,1},{1,0},{2,3},{3,2},{4,5},{5,4},{6,7},{7,6},{8,9},{9,8},{10,11... | collective-permute-start | bytes 393224 | tf_op jit(solution)/shard_map/ppermute | solution.py:36
  24.2 14.7 %collective-permute-start.4 = (f32[512,128]{1,0:T(8,128)S(1)}, f32[512,128]{1,0:T(8,128)S(1)}, u32[]{:S(2)}, u32[]{:S(2)}) collective-permute-start(f32[512,128]{1,0:T(8,128)S(1)} %get-tuple-element.78), channel_id=1, source_target_pairs={{0,8},{4,12},{8,0},{12,4},{16,24},{20,28},{24,16},{28,20},{1,9},{5... | collective-permute-start | bytes 786440 | tf_op jit(solution)/shard_map/ppermute | solution.py:28
  25.7 13.2 %collective-permute-start.5 = (f32[512,128]{1,0:T(8,128)S(1)}, f32[512,128]{1,0:T(8,128)S(1)}, u32[]{:S(2)}, u32[]{:S(2)}) collective-permute-start(f32[512,128]{1,0:T(8,128)S(1)} %get-tuple-element.79), channel_id=1, source_target_pairs={{0,16},{4,20},{8,24},{12,28},{16,0},{20,4},{24,8},{28,12},{1,17},{... | collective-permute-start | bytes 786440 | tf_op jit(solution)/shard_map/ppermute | solution.py:28
  27.2 11.7 %collective-permute-start.6 = (f32[512,128]{1,0:T(8,128)S(1)}, f32[512,128]{1,0:T(8,128)S(1)}, u32[]{:S(2)}, u32[]{:S(2)}) collective-permute-start(f32[512,128]{1,0:T(8,128)S(1)} %get-tuple-element.80), channel_id=1, source_target_pairs={{0,24},{4,28},{8,16},{12,20},{16,8},{20,12},{24,0},{28,4},{1,25},{... | collective-permute-start | bytes 786440 | tf_op jit(solution)/shard_map/ppermute | solution.py:28
  27.7 11.2 %collective-permute-start.8 = (f32[256,128]{1,0:T(8,128)S(1)}, f32[256,128]{1,0:T(8,128)S(1)}, u32[]{:S(2)}, u32[]{:S(2)}) collective-permute-start(f32[256,128]{1,0:T(8,128)S(1)} %get-tuple-element.82), channel_id=1, source_target_pairs={{0,2},{1,3},{2,0},{3,1},{4,6},{5,7},{6,4},{7,5},{8,10},{9,11},{10,... | collective-permute-start | bytes 393224 | tf_op jit(solution)/shard_map/ppermute | solution.py:36
  30.3 8.6 %collective-permute-start.9 = (f32[256,128]{1,0:T(8,128)S(1)}, f32[256,128]{1,0:T(8,128)S(1)}, u32[]{:S(2)}, u32[]{:S(2)}) collective-permute-start(f32[256,128]{1,0:T(8,128)S(1)} %get-tuple-element.83), channel_id=1, source_target_pairs={{0,3},{1,2},{2,1},{3,0},{4,7},{5,6},{6,5},{7,4},{8,11},{9,10},{10,... | collective-permute-start | bytes 393224 | tf_op jit(solution)/shard_map/ppermute | solution.py:36
  39.8 7.5 %collective-permute-start.12 = (f32[256,128]{1,0:T(8,128)S(1)}, f32[256,128]{1,0:T(8,128)S(1)}, u32[]{:S(2)}, u32[]{:S(2)}) collective-permute-start(f32[256,128]{1,0:T(8,128)S(1)} %get-tuple-element.84.follows.refs_0_), channel_id=1, source_target_pairs={{0,3},{1,2},{2,1},{3,0},{4,7},{5,6},{6,5},{7,4},{8,11},{9,10},{10,... | collective-permute-start | bytes 393224 | tf_op jit(solution)/shard_map/ppermute | solution.py:36
  42.7 16.1 %collective-permute-start.13 = (f32[512,128]{1,0:T(8,128)S(1)}, f32[512,128]{1,0:T(8,128)S(1)}, u32[]{:S(2)}, u32[]{:S(2)}) collective-permute-start(f32[512,128]{1,0:T(8,128)S(1)} %get-tuple-element.88), channel_id=1, source_target_pairs={{0,8},{4,12},{8,0},{12,4},{16,24},{20,28},{24,16},{28,20},{1,9},{5... | collective-permute-start | bytes 786440 | tf_op jit(solution)/shard_map/ppermute | solution.py:28
  44.2 14.6 %collective-permute-start.14 = (f32[512,128]{1,0:T(8,128)S(1)}, f32[512,128]{1,0:T(8,128)S(1)}, u32[]{:S(2)}, u32[]{:S(2)}) collective-permute-start(f32[512,128]{1,0:T(8,128)S(1)} %get-tuple-element.89), channel_id=1, source_target_pairs={{0,16},{4,20},{8,24},{12,28},{16,0},{20,4},{24,8},{28,12},{1,17},{... | collective-permute-start | bytes 786440 | tf_op jit(solution)/shard_map/ppermute | solution.py:28
  45.7 13.1 %collective-permute-start.15 = (f32[512,128]{1,0:T(8,128)S(1)}, f32[512,128]{1,0:T(8,128)S(1)}, u32[]{:S(2)}, u32[]{:S(2)}) collective-permute-start(f32[512,128]{1,0:T(8,128)S(1)} %get-tuple-element.90), channel_id=1, source_target_pairs={{0,24},{4,28},{8,16},{12,20},{16,8},{20,12},{24,0},{28,4},{1,25},{... | collective-permute-start | bytes 786440 | tf_op jit(solution)/shard_map/ppermute | solution.py:28
  46.2 11.9 %collective-permute-start.11 = (f32[256,128]{1,0:T(8,128)S(1)}, f32[256,128]{1,0:T(8,128)S(1)}, u32[]{:S(2)}, u32[]{:S(2)}) collective-permute-start(f32[256,128]{1,0:T(8,128)S(1)} %get-tuple-element.84.follows.refs_0_), channel_id=1, source_target_pairs={{0,2},{1,3},{2,0},{3,1},{4,6},{5,7},{6,4},{7,5},{8,10},{9,11},{10,... | collective-permute-start | bytes 393224 | tf_op jit(solution)/shard_map/ppermute | solution.py:36
  47.3 10.8 %collective-permute-start.10 = (f32[256,128]{1,0:T(8,128)S(1)}, f32[256,128]{1,0:T(8,128)S(1)}, u32[]{:S(2)}, u32[]{:S(2)}) collective-permute-start(f32[256,128]{1,0:T(8,128)S(1)} %get-tuple-element.84.follows.refs_0_), channel_id=1, source_target_pairs={{0,1},{1,0},{2,3},{3,2},{4,5},{5,4},{6,7},{7,6},{8,9},{9,8},{10,11... | collective-permute-start | bytes 393224 | tf_op jit(solution)/shard_map/ppermute | solution.py:36
  59.6 3.6 %collective-permute-start.16 = (f32[2048,128]{1,0:T(8,128)S(1)}, f32[2048,128]{1,0:T(8,128)S(1)}, u32[]{:S(2)}, u32[]{:S(2)}) collective-permute-start(f32[2048,128]{1,0:T(8,128)S(1)} %get-tuple-element.92), channel_id=1, source_target_pairs={{0,4},{4,0},{8,12},{12,8},{16,20},{20,16},{24,28},{28,24},{1,5},{5... | collective-permute-start | bytes 3145736 | tf_op jit(solution)/shard_map/ppermute | solution.py:21
  59.7 8.4 %collective-permute-start.17 = (f32[256,128]{1,0:T(8,128)S(1)}, f32[256,128]{1,0:T(8,128)S(1)}, u32[]{:S(2)}, u32[]{:S(2)}) collective-permute-start(f32[256,128]{1,0:T(8,128)S(1)} %get-tuple-element.98), channel_id=1, source_target_pairs={{0,8},{4,12},{8,0},{12,4},{16,24},{20,28},{24,16},{28,20},{1,9},{5... | collective-permute-start | bytes 393224 | tf_op jit(solution)/shard_map/ppermute | solution.py:28
  61.4 8.4 %collective-permute-start.18 = (f32[256,128]{1,0:T(8,128)S(1)}, f32[256,128]{1,0:T(8,128)S(1)}, u32[]{:S(2)}, u32[]{:S(2)}) collective-permute-start(f32[256,128]{1,0:T(8,128)S(1)} %get-tuple-element.99), channel_id=1, source_target_pairs={{0,16},{4,20},{8,24},{12,28},{16,0},{20,4},{24,8},{28,12},{1,17},{... | collective-permute-start | bytes 393224 | tf_op jit(solution)/shard_map/ppermute | solution.py:28
  62.9 6.9 %collective-permute-start.19 = (f32[256,128]{1,0:T(8,128)S(1)}, f32[256,128]{1,0:T(8,128)S(1)}, u32[]{:S(2)}, u32[]{:S(2)}) collective-permute-start(f32[256,128]{1,0:T(8,128)S(1)} %get-tuple-element.100), channel_id=1, source_target_pairs={{0,24},{4,28},{8,16},{12,20},{16,8},{20,12},{24,0},{28,4},{1,25},{... | collective-permute-start | bytes 393224 | tf_op jit(solution)/shard_map/ppermute | solution.py:28
  69.8 1.2 %copy-start = (bf16[256,16,128]{2,1,0:T(8,128)(2,1)S(1)}, bf16[256,16,128]{2,1,0:T(8,128)(2,1)}, u32[]{:S(2)}) copy-start(bf16[256,16,128]{2,1,0:T(8,128)(2,1)} %get-tuple-element.51.follows) | copy-start | bytes 3145732

commit v3 on v2

v3 whole, which is shorter than its diff:
```python
import functools

import jax
import jax.numpy as jnp
from jax import lax
from jax.experimental import pallas as pl
from jax.experimental.pallas import tpu as pltpu
from jax.sharding import PartitionSpec as P

PLANE = ("ctx", "head")
BLOCK = 256
CHUNK = 64
F32 = jnp.float32
BF16 = jnp.bfloat16
ROWS_ROWS = (((0,), (0,)), ((), ()))
LAST_LAST = (((1,), (1,)), ((), ()))
LAST_ROWS = (((1,), (0,)), ((), ()))


def pair_step(block):
    count = lax.axis_size(PLANE)
    return lax.ppermute(block, PLANE, [(b, b ^ 1) for b in range(count)])


def plane_exchange(pieces):
    count = lax.axis_size(PLANE)
    moved = [pieces[0]]
    for k in range(1, len(pieces)):
        moved.append(lax.ppermute(pieces[k], PLANE, [(b, b ^ (2 * k)) for b in range(count)]))
    return moved


def resp_masks(count):
    return [3 if mask == 2 else mask for mask in (1 << i for i in range(count.bit_length() - 1))]


def resp_step(array, mask):
    count = lax.axis_size("resp")
    return lax.ppermute(array, "resp", [(z, z ^ mask) for z in range(count)])


def resp_gather(piece):
    held = {0: piece}
    for mask in resp_masks(lax.axis_size("resp")):
        held.update({j ^ mask: resp_step(array, mask) for j, array in list(held.items())})
    return [held[j] for j in range(len(held))]


def halving_order(count):
    order = [0]
    for mask in reversed(resp_masks(count)):
        order = order + [j ^ mask for j in order]
    return order


def dot(a, b, dims):
    return lax.dot_general(a, b, dims, preferred_element_type=F32)


def row_scale(first_row, row_total, head_size):
    rows = lax.broadcasted_iota(jnp.int32, (row_total, head_size), 0) + first_row
    return lax.rsqrt(float(head_size) * (rows.astype(F32) + 1.0))


def to_heads(target, source, factor=None):
    rows = source.shape[0]
    chunk = CHUNK if rows % CHUNK == 0 else rows

    def one(i, carry):
        span = pl.ds(pl.multiple_of(i * chunk, chunk), chunk)
        part = jnp.swapaxes(source[span], 0, 1)
        if factor is not None:
            part = (part.astype(F32) * factor[span][None]).astype(BF16)
        target[:, span, :] = part
        return carry

    lax.fori_loop(0, rows // chunk, one, 0)


def by_head(array):
    return jnp.swapaxes(array, 0, 1)


def load(sources, buffers, arrived):
    copies = []
    for i, (source, buffer) in enumerate(zip(sources, buffers)):
        copies.append(pltpu.make_async_copy(source, buffer, arrived.at[i]))
        copies[-1].start()
    return copies


def moments_kernel(steps, place, weight, *refs):
    sources, refs = refs[:6], refs[6:]
    sent, kept, key, value, query, cotangent, r_query, r_cotangent = refs[:8]
    pieces, refs = refs[8 : 8 + steps], refs[8 + steps :]
    buffers, (scaled, r_scaled, r_moment, factor, arrived) = refs[:6], refs[6:]
    copies = load(sources, buffers, arrived)
    member, first_row, reply_first, length = (place[i] for i in (0, 2, 3, 4))
    heads, rows, size = query.shape
    half = heads // 2
    halves = ((sent, (1 - member) * half), (kept, member * half))
    for i, target in enumerate((key, value)):
        copies[i].wait()
        to_heads(target, buffers[i])
    for target, base in halves:

        def state(j, carry, target=target, base=base):
            h = base + j
            target[pl.ds(j * size, size), :] = dot(key[h], value[h], ROWS_ROWS)
            return carry

        lax.fori_loop(0, half, state, 0, unroll=True)
    for i, target in enumerate((query, cotangent)):
        copies[2 + i].wait()
        to_heads(target, buffers[2 + i])
    scale = row_scale(first_row, rows, size)
    for h in range(heads):
        scaled[h] = (query[h].astype(F32) * scale).astype(BF16)
    for target, base in halves:

        def moment(j, carry, target=target, base=base):
            h = base + j
            target[pl.ds((half + j) * size, size), :] = dot(scaled[h], cotangent[h], ROWS_ROWS)
            return carry

        lax.fori_loop(0, half, moment, 0, unroll=True)
    copies[4].wait()
    to_heads(r_query, buffers[4])
    copies[5].wait()
    live = lax.broadcasted_iota(jnp.int32, factor.shape, 0) < length
    factor[...] = jnp.where(live, weight[0], 0.0)
    to_heads(r_cotangent, buffers[5], factor)
    scale = row_scale(reply_first, r_query.shape[1], size)
    for h in range(r_query.shape[0]):
        r_scaled[h] = (r_query[h].astype(F32) * scale).astype(BF16)
    for h in range(r_query.shape[0]):
        r_moment[pl.ds(h * size, size), :] = dot(r_scaled[h], r_cotangent[h], ROWS_ROWS)
    piece_rows = pieces[0].shape[0]
    for k in range(steps):
        start = pl.multiple_of((place[1] ^ k) * piece_rows, piece_rows)
        pieces[k][...] = r_moment[pl.ds(start, piece_rows), :]


def pair_kernel(steps, place, kept, received, *pieces):
    pair = place[1]
    half_rows = kept.shape[0] // 2
    piece_rows = half_rows // steps
    for k in range(steps):
        start = pl.multiple_of((pair ^ k) * piece_rows, piece_rows)
        for part in range(2):
            source = pl.ds(part * half_rows + start, piece_rows)
            pieces[k][pl.ds(part * piece_rows, piece_rows), :] = kept[source, :] + received[source, :]


def choose(place, pieces, targets):
    start = place[1] ^ place[5]
    for j, (target, rows) in targets.items():
        chosen = pieces[0][...]
        for k in range(1, len(pieces)):
            chosen = jnp.where((start ^ j) == k, pieces[k][...], chosen)
        target[rows, :] = chosen


def choose_kernel(steps, place, follows, *refs):
    pieces, (stays, leaves, token) = refs[:steps], refs[steps:]
    token[...] = jnp.zeros_like(token)
    rows = pieces[0].shape[0]
    order, half = halving_order(steps), steps // 2
    targets = {
        j: (leaves if i >= half else stays, pl.ds(i % half * rows, rows)) for i, j in enumerate(order)
    }
    choose(place, pieces, targets)


def halve_kernel(follows, mine, other, stays, leaves):
    rows = stays.shape[0]
    stays[...] = mine[pl.ds(0, rows), :] + other[pl.ds(0, rows), :]
    leaves[...] = mine[pl.ds(rows, rows), :] + other[pl.ds(rows, rows), :]


def prefix_kernel(steps, place, follows, *refs):
    parts, moments, refs = refs[:steps], refs[steps : steps + 2], refs[steps + 2 :]
    final, returned = refs[0], refs[1:]
    pair = place[1]
    rows = final.shape[0]
    states = [part[pl.ds(0, rows), :] for part in parts]
    total = states[0]
    for k in range(1, steps):
        total = total + states[k]
    final[...] = total
    for k in range(steps):
        before = jnp.zeros_like(total)
        for m in range(steps):
            before = before + jnp.where((pair ^ m) < (pair ^ k), states[m], 0.0)
        returned[k][pl.ds(0, rows), :] = before
    reply_moment = moments[0][...] + moments[1][...]
    later = [part[pl.ds(rows, rows), :] for part in parts]
    for k in range(steps):
        after = reply_moment
        for m in range(steps):
            after = after + jnp.where((pair ^ m) > (pair ^ k), later[m], 0.0)
        returned[k][pl.ds(rows, rows), :] = after


def halves_kernel(steps, place, follows, kept, received, *refs):
    pieces, finals, refs = refs[:steps], refs[steps : 2 * steps], refs[2 * steps :]
    mine, to_other = refs[:2]
    rows = finals[0].shape[0]
    choose(place, finals, {j: (ref, pl.ds(0, rows)) for j, ref in enumerate(refs[2:])})
    member, pair = place[0], place[1]
    half_rows = kept.shape[0] // 2
    piece_rows = half_rows // steps
    first = member == 0
    for k in range(steps):
        start = pl.multiple_of((pair ^ k) * piece_rows, piece_rows)
        for part in range(2):
            rows = pl.ds(part * half_rows + start, piece_rows)
            sums = pieces[k][pl.ds(part * piece_rows, piece_rows), :]
            add_other = first if part else jnp.logical_not(first)
            mine[rows, :] = sums + jnp.where(add_other, received[rows, :], 0.0)
            to_other[rows, :] = sums + jnp.where(add_other, 0.0, kept[rows, :])


def local_terms(first_head, first_row, query, key, value, cotangent, outs, work):
    inner, query_part, key_part, value_part = outs
    weights, mixing, grad_mixing = work
    heads, rows, size = inner.shape
    block = weights.shape[1]
    count = rows // block
    spans = [pl.ds(i * block, block) for i in range(count)]
    for i in range(count):
        weights[i], weights[count + i] = causal_weights(first_row + i * block, block, size)

    def mix(own):
        h, slot = first_head + own, own % 2
        for i in range(count):
            for j in range(i + 1):
                factor = weights[i if i == j else count + i]
                scores = dot(query[h, spans[i]], key[h, spans[j]], LAST_LAST)
                mixing[slot, spans[i], spans[j]] = (scores * factor).astype(BF16)
                scores = dot(cotangent[h, spans[i]], value[h, spans[j]], LAST_LAST)
                grad_mixing[slot, spans[i], spans[j]] = (scores * factor).astype(BF16)

    mix(0)
    for own in range(heads):
        if own + 1 < heads:
            mix(own + 1)
        h, slot = first_head + own, own % 2
        for i in range(count):
            seen = pl.ds(0, (i + 1) * block)
            inner[own, spans[i]] = dot(mixing[slot, spans[i], seen], value[h, seen], LAST_ROWS)
            query_part[own, spans[i]] = dot(
                grad_mixing[slot, spans[i], seen], key[h, seen], LAST_ROWS
            )
            later = pl.ds(i * block, rows - i * block)
            part = dot(grad_mixing[slot, later, spans[i]], query[h, later], ROWS_ROWS)
            key_part[own, spans[i]] = part.astype(key_part.dtype)
            part = dot(mixing[slot, later, spans[i]], cotangent[h, later], ROWS_ROWS)
            value_part[own, spans[i]] = part.astype(value_part.dtype)


def prompt_local_kernel(place, query, key, value, cotangent, reply_key, reply_value, *refs):
    outs, (r_key, r_value, token), work = refs[1:5], refs[5:8], refs[8:11]
    key_buffer, value_buffer, arrived = refs[11:]
    copies = load((reply_key, reply_value), (key_buffer, value_buffer), arrived)
    local_terms(0, place[2], query, key, value, cotangent, outs, work)
    copies[0].wait()
    r_key[...] = by_head(key_buffer[...])
    copies[1].wait()
    r_value[...] = by_head(value_buffer[...])
    token[...] = jnp.zeros_like(token)


def reply_local_kernel(first_head, place, query, key, value, cotangent, follows, *refs):
    outs, token, work = refs[:4], refs[4], refs[5:]
    local_terms(first_head, place[3], query, key, value, cotangent, outs, work)
    token[...] = jnp.zeros_like(token)


def reply_grads_kernel(follows, key_first, value_first, key_second, value_second, *refs):
    grads, token, staged, left = refs[:2], refs[2], refs[3], refs[4]
    token[...] = jnp.zeros_like(token)
    copies = []
    for i, parts in enumerate(((key_first, key_second), (value_first, value_second))):
        staged[i] = by_head(jnp.concatenate([part[...] for part in parts], 0))
        copies.append(pltpu.make_async_copy(staged.at[i], grads[i], left.at[i]))
        copies[-1].start()
    for copy in copies:
        copy.wait()


def causal_weights(first_row, row_total, head_size):
    rows = lax.broadcasted_iota(jnp.int32, (row_total, row_total), 0)
    columns = lax.broadcasted_iota(jnp.int32, (row_total, row_total), 1)
    scale = lax.rsqrt(float(head_size) * ((rows + first_row).astype(F32) + 1.0))
    return jnp.where(rows >= columns, scale, 0.0), scale


def prompt_final_kernel(place, mine, other, *refs):
    parts, (query, key, value, cotangent), grads = refs[:4], refs[4:8], refs[8:12]
    token, before, after, held, staged, left = refs[12:]
    token[...] = jnp.zeros_like(token)
    member, first_row = place[0], place[2]
    heads, rows, size = query.shape
    half = heads // 2
    scale = row_scale(first_row, rows, size)
    copies = []

    def leave(source, target):
        copies.append(pltpu.make_async_copy(source, target, left.at[len(copies)]))
        copies[-1].start()

    for target, offset in ((before, 0), (after, half)):
        for source, base in ((mine, member * half), (other, (1 - member) * half)):
            for j in range(half):
                target[base + j] = source[pl.ds((offset + j) * size, size), :].astype(BF16)
    for i, (array, state, dims) in enumerate(
        (
            (query, before, LAST_ROWS),
            (cotangent, before, LAST_LAST),
            (value, after, LAST_LAST),
            (key, after, LAST_ROWS),
        )
    ):
        for h in range(heads):
            part = dot(array[h], state[h], dims)
            part = scale * part if i < 2 else part
            held[i, h] = (parts[i][h] + part).astype(BF16)
        staged[i] = by_head(held[i])
        leave(staged.at[i], grads[i])
    for copy in copies:
        copy.wait()


def reply_final_kernel(steps, place, follows, *refs):
    pieces, refs = refs[:steps], refs[steps:]
    inner, query_part, (query, cotangent, output, query_grad) = refs[:2], refs[2:4], refs[4:8]
    state, held, staged, left = refs[8:]
    half = inner[0].shape[0]
    pair, first_row, length = place[1], place[3], place[4]
    heads, rows, size = query.shape
    piece_rows = pieces[0].shape[0]
    for k in range(steps):
        start = pl.multiple_of((pair ^ k) * piece_rows, piece_rows)
        state[pl.ds(start, piece_rows), :] = pieces[k][...].astype(BF16)
    scale = row_scale(first_row, rows, size)
    live = lax.broadcasted_iota(jnp.int32, (rows, size), 0) < length
    copies = []

    def finish(i, target):
        staged[i] = by_head(held[i])
        copies.append(pltpu.make_async_copy(staged.at[i], target, left.at[i]))
        copies[-1].start()

    for h in range(heads):
        final = state[pl.ds(h * size, size), :]
        whole = inner[h // half][h % half] + scale * dot(query[h], final, LAST_ROWS)
        held[0, h] = jnp.where(live, whole, 0.0).astype(BF16)
    finish(0, output)
    for h in range(heads):
        final = state[pl.ds(h * size, size), :]
        part = scale * dot(cotangent[h], final, LAST_LAST)
        held[1, h] = (query_part[h // half][h % half] + part).astype(BF16)
    finish(1, query_grad)
    for copy in copies:
        copy.wait()


VMEM = pl.BlockSpec(memory_space=pltpu.VMEM)
HBM = pl.BlockSpec(memory_space=pltpu.HBM)
ANY = pl.BlockSpec(memory_space=pl.ANY)


def call(kernel, scalars, arrays, outs, scratch, name):
    arrays = [
        (spec, pltpu.with_memory_space_constraint(array, pltpu.HBM) if spec is HBM else array)
        for spec, array in arrays
    ]
    return pl.pallas_call(
        kernel,
        out_shape=[out for _, out in outs],
        in_specs=[pl.BlockSpec(memory_space=pltpu.SMEM)] * len(scalars) + [s for s, _ in arrays],
        out_specs=[spec for spec, _ in outs],
        scratch_shapes=scratch,
        compiler_params=pltpu.CompilerParams(vmem_limit_bytes=24 << 20),
        cost_estimate=pl.CostEstimate(flops=1, bytes_accessed=1, transcendentals=0),
        name=name,
    )(*scalars, *[array for _, array in arrays])


def held_in(spec, arrays):
    return [(spec, array) for array in arrays]


def shards(
    prompt_query,
    prompt_key,
    prompt_value,
    prompt_cotangent,
    reply_query,
    reply_key,
    reply_value,
    reply_cotangent,
    reply_weight,
    reply_length,
):
    rows, heads, size = prompt_query.shape
    reply_query, reply_key = reply_query[0], reply_key[0]
    reply_value, reply_cotangent = reply_value[0], reply_cotangent[0]
    reply_rows, reply_heads = reply_query.shape[:2]
    block_count = lax.axis_size(PLANE)
    steps = lax.axis_size("resp")
    assert block_count == 2 * steps and steps & (steps - 1) == 0
    block_index = lax.axis_index(PLANE)
    resp_index = lax.axis_index("resp")
    pair_index, member = block_index // 2, block_index % 2
    half_rows = heads // 2 * size
    piece_rows = half_rows // steps
    place = jnp.stack(
        [
            member,
            pair_index,
            block_index * rows,
            block_count * rows,
            reply_length[0],
            resp_index,
        ]
    ).astype(jnp.int32)
    shape = jax.ShapeDtypeStruct
    prompt_bf16 = shape((rows, heads, size), BF16)
    reply_bf16 = shape((reply_rows, reply_heads, size), BF16)
    prompt_held = shape((heads, rows, size), BF16)
    reply_held = shape((reply_heads, reply_rows, size), BF16)
    piece = shape((piece_rows, size), F32)
    two_pieces = shape((2 * piece_rows, size), F32)
    two_halves = shape((2 * half_rows, size), F32)

    def scratch(held, count=None):
        return pltpu.VMEM(held.shape if count is None else (count, *held.shape), held.dtype)

    sent, kept, key, value, query, cotangent, r_query, r_cotangent, *moments = call(
        functools.partial(moments_kernel, steps),
        [place, reply_weight],
        held_in(
            HBM,
            [prompt_key, prompt_value, prompt_query, prompt_cotangent, reply_query, reply_cotangent],
        ),
        held_in(
            VMEM, [two_halves] * 2 + [prompt_held] * 4 + [reply_held] * 2 + [piece] * steps
        ),
        [scratch(prompt_bf16)] * 4
        + [scratch(reply_bf16)] * 2
        + [scratch(prompt_held), scratch(reply_held)]
        + [pltpu.VMEM((reply_heads * size, size), F32), pltpu.VMEM((reply_rows, size), F32)]
        + [pltpu.SemaphoreType.DMA((6,))],
        "moments",
    )
    received = pair_step(sent)
    moments = plane_exchange(moments)
    pieces = call(
        functools.partial(pair_kernel, steps),
        [place],
        held_in(VMEM, [kept, received]),
        held_in(VMEM, [two_pieces] * steps),
        [],
        "pair_sums",
    )
    parts = plane_exchange(pieces)
    half_heads = reply_heads // 2
    half_reply = shape((half_heads, reply_rows, size), F32)
    half_held = shape((half_heads, reply_rows, size), BF16)
    prompt_wide = shape((heads, rows, size), F32)
    token = shape((8, 128), F32)

    def work(total):
        block = min(BLOCK, total)
        mixing = pltpu.VMEM((2, total, total), BF16)
        return [pltpu.VMEM((2 * (total // block), block, block), F32), mixing, mixing]

    prompt_arrays = held_in(VMEM, [query, key, value, cotangent])
    *prompt_parts, r_key, r_value, done = call(
        prompt_local_kernel,
        [place],
        prompt_arrays + held_in(HBM, [reply_key, reply_value]) + held_in(ANY, pieces[:1]),
        held_in(VMEM, [prompt_wide] * 4 + [reply_held] * 2 + [token]),
        work(rows) + [scratch(reply_bf16)] * 2 + [pltpu.SemaphoreType.DMA((2,))],
        "prompt_local",
    )
    stays, leaves, done = call(
        functools.partial(choose_kernel, steps),
        [place],
        held_in(ANY, [done]) + held_in(VMEM, moments),
        held_in(VMEM, [shape((steps // 2 * piece_rows, size), F32)] * 2 + [token]),
        [],
        "choose_moments",
    )
    reply_arrays = held_in(VMEM, [r_query, r_key, r_value, r_cotangent])
    reply_terms = held_in(VMEM, [half_reply] * 2 + [half_held] * 2 + [token])
    inner_first, part_first, key_first, value_first, done = call(
        functools.partial(reply_local_kernel, 0),
        [place],
        reply_arrays + held_in(ANY, [done]),
        reply_terms,
        work(reply_rows),
        "reply_local_first",
    )
    masks = resp_masks(steps)
    for mask in masks[:-1]:
        rows_left = stays.shape[0] // 2
        stays, leaves = call(
            halve_kernel,
            [],
            held_in(ANY, [done]) + held_in(VMEM, [stays, resp_step(leaves, mask)]),
            held_in(VMEM, [shape((rows_left, size), F32)] * 2),
            [],
            "reply_moments",
        )
    inner_second, part_second, key_second, value_second, done = call(
        functools.partial(reply_local_kernel, half_heads),
        [place],
        reply_arrays + held_in(ANY, [leaves]),
        reply_terms,
        work(reply_rows),
        "reply_local_second",
    )
    final, *returned = call(
        functools.partial(prefix_kernel, steps),
        [place],
        held_in(ANY, [done]) + held_in(VMEM, [*parts, stays, resp_step(leaves, masks[-1])]),
        held_in(VMEM, [piece] + [two_pieces] * steps),
        [],
        "prefix_sums",
    )
    finals = resp_gather(final)
    returned = plane_exchange(returned)
    reply_dkey, reply_dvalue, done = call(
        reply_grads_kernel,
        [],
        held_in(ANY, [final])
        + held_in(VMEM, [key_first, value_first, key_second, value_second]),
        held_in(HBM, [reply_bf16] * 2) + held_in(VMEM, [token]),
        [scratch(reply_bf16, 2), pltpu.SemaphoreType.DMA((2,))],
        "reply_grads",
    )
    mine, to_other, *finals = call(
        functools.partial(halves_kernel, steps),
        [place],
        held_in(ANY, [done]) + held_in(VMEM, [kept, received, *returned, *finals]),
        held_in(VMEM, [two_halves] * 2 + [piece] * steps),
        [],
        "halves",
    )
    finals = plane_exchange(finals)
    other = pair_step(to_other)
    *prompt_results, done = call(
        prompt_final_kernel,
        [place],
        held_in(VMEM, [mine, other, *prompt_parts]) + prompt_arrays,
        held_in(HBM, [prompt_bf16] * 4) + held_in(VMEM, [token]),
        [pltpu.VMEM((heads, size, size), BF16)] * 2
        + [scratch(prompt_held, 4), scratch(prompt_bf16, 4)]
        + [pltpu.SemaphoreType.DMA((4,))],
        "prompt_final",
    )
    prompt_output, prompt_dquery, prompt_dkey, prompt_dvalue = prompt_results
    reply_output, reply_dquery = call(
        functools.partial(reply_final_kernel, steps),
        [place],
        held_in(ANY, [done])
        + held_in(VMEM, [*finals, inner_first, inner_second, part_first, part_second])
        + held_in(VMEM, [r_query, r_cotangent]),
        held_in(HBM, [reply_bf16] * 2),
        [
            pltpu.VMEM((reply_heads * size, size), BF16),
            scratch(reply_held, 2),
            scratch(reply_bf16, 2),
            pltpu.SemaphoreType.DMA((2,)),
        ],
        "reply_final",
    )
    return (
        prompt_output,
        reply_output[None],
        prompt_dquery,
        prompt_dkey,
        prompt_dvalue,
        reply_dquery[None],
        reply_dkey[None],
        reply_dvalue[None],
    )


def solution(mesh):
    prompt = P(PLANE, "resp", None)
    reply = P("resp", None, PLANE, None)
    return jax.shard_map(
        shards,
        mesh=mesh,
        in_specs=(prompt,) * 4 + (reply,) * 4 + (P("resp"),) * 2,
        out_specs=(prompt, reply, prompt, prompt, prompt, reply, reply, reply),
        check_vma=False,
    )
```

time: 74.5 us -> 65.2 us (0.88)
  Pallas kernels: 37.1 us -> 30.3 us
  starting transfers between devices: 29.1 us -> 24.1 us
  waiting for transfers between devices: 4.43 us -> 8.26 us
  local copies, waits for them, and re-layouts: 1.31 us -> 0.08 us
    pallas_call x11 -> x12, Pallas kernels: 37.1 us -> 30.3 us  [call(): pl.pallas_call(kernel, out_shape=[out for _, out in outs], in_specs=[pl.B...]
    ppermute x6 -> x5, starting transfers between devices: 13.9 us -> 8.9 us  [resp_step(): return lax.ppermute(array, 'resp', [(z, z ^ mask) for z in range(count)])]
    ppermute x6 -> x5, waiting for transfers between devices: 2.8 us -> 4.8 us  [resp_step(): return lax.ppermute(array, 'resp', [(z, z ^ mask) for z in range(count)])]
    ppermute x12, waiting for transfers between devices: 1.62 us -> 3.45 us  [plane_exchange(): lax.ppermute(pieces[k], PLANE, [(b, b ^ 2 * k) for b in range(count)])]
    unnamed x2 -> x0, local copies, waits for them, and re-layouts: 1.23 us -> none
  transfers between devices with their start and end apart: 20 -> 19, of which waited for: 2 -> 6; matrix products, arithmetic and copies ran while one was open for 0% -> 0% of each run, Pallas kernels for 34% -> 29%
where the time goes in v3:
time: 65.2 us; the launch traced here: 65 us
  Pallas kernels  30.3 us (46%)
  starting transfers between devices  24.1 us (37%)
  waiting for transfers between devices  8.26 us (13%)
  between operations  2.23 us (3%)
    pallas_call x12, Pallas kernels, call(): pl.pallas_call(kernel, out_shape=[out for _, out in outs], in_specs=[pl.B...  30.3 us
    ppermute x12, starting transfers between devices, plane_exchange(): lax.ppermute(pieces[k], PLANE, [(b, b ^ 2 * k) for b in range(count)])  14.6 us
    ppermute x5, starting transfers between devices, resp_step(): return lax.ppermute(array, 'resp', [(z, z ^ mask) for z in range(count)])  8.9 us
    ppermute x5, waiting for transfers between devices, resp_step(): return lax.ppermute(array, 'resp', [(z, z ^ mask) for z in range(count)])  4.8 us
    ppermute x12, waiting for transfers between devices, plane_exchange(): lax.ppermute(pieces[k], PLANE, [(b, b ^ 2 * k) for b in range(count)])  3.45 us
  transfers between devices with their start and end apart: 19, of which 6 were waited for; matrix products, arithmetic and copies ran while one was open for 0% of the time, Pallas kernels for 29%

profile of v3, /device:TPU:0, one launch (start us, length us, event | category | flops | bytes accessed | tf_op | source)
XLA Modules:
  0.0 65.0 jit_solution(13657418329308155037)
XLA Ops:
  2.0 5.8 %moments.1 = (f32[2048,128]{1,0:T(8,128)S(1)}, f32[2048,128]{1,0:T(8,128)S(1)}, bf16[16,256,128]{2,1,0:T(8,128)(2,1)S(1)}, bf16[16,256,128]{2,1,0:T(8,128)(2,1)S...) custom-call(s32[6]{0:T(128)S(1)} %stack.19.place, ...), custom_call_target="tpu_custom_call" | custom-call | flops 1 | bytes 1 | tf_op jit(solution)/shard_map/moments/pallas_call | solution.py:379
  8.4 2.6 %collective-permute-start.1 = (f32[256,128]{1,0:T(8,128)S(1)}, f32[256,128]{1,0:T(8,128)S(1)}, u32[]{:S(2)}, u32[]{:S(2)}) collective-permute-start(f32[256,128]{1,0:T(8,128)S(1)} %get-tuple-element.80), channel_id=1, source_target_pairs={{0,8},{4,12},{8,0},{12,4},{16,24},{20,28},{24,16},{28,20},{1,9},{5... | collective-permute-start | bytes 393224 | tf_op jit(solution)/shard_map/ppermute | solution.py:29
  10.9 1.5 %collective-permute-start.2 = (f32[256,128]{1,0:T(8,128)S(1)}, f32[256,128]{1,0:T(8,128)S(1)}, u32[]{:S(2)}, u32[]{:S(2)}) collective-permute-start(f32[256,128]{1,0:T(8,128)S(1)} %get-tuple-element.81), channel_id=1, source_target_pairs={{0,16},{4,20},{8,24},{12,28},{16,0},{20,4},{24,8},{28,12},{1,17},{... | collective-permute-start | bytes 393224 | tf_op jit(solution)/shard_map/ppermute | solution.py:29
  13.1 5.4 %prompt_local.1 = (f32[16,256,128]{2,1,0:T(8,128)S(1)}, f32[16,256,128]{2,1,0:T(8,128)S(1)}, f32[16,256,128]{2,1,0:T(8,128)S(1)}, f32[16,256,128]{2,1,0:T(8,128)...) custom-call(s32[6]{0:T(128)S(1)} %stack.19.place, ...), custom_call_target="tpu_custom_call" | custom-call | flops 1 | bytes 1 | tf_op jit(solution)/shard_map/prompt_local/pallas_call | solution.py:379
  20.0 1.6 %collective-permute-start.4 = (f32[512,128]{1,0:T(8,128)S(1)}, f32[512,128]{1,0:T(8,128)S(1)}, u32[]{:S(2)}, u32[]{:S(2)}) collective-permute-start(f32[512,128]{1,0:T(8,128)S(1)} %get-tuple-element.86), channel_id=1, source_target_pairs={{0,1},{1,0},{2,3},{3,2},{4,5},{5,4},{6,7},{7,6},{8,9},{9,8},{10,11... | collective-permute-start | bytes 786440 | tf_op jit(solution)/shard_map/ppermute | solution.py:39
  21.6 1.2 %collective-permute-start.5 = (f32[512,128]{1,0:T(8,128)S(1)}, f32[512,128]{1,0:T(8,128)S(1)}, u32[]{:S(2)}, u32[]{:S(2)}) collective-permute-start(f32[512,128]{1,0:T(8,128)S(1)} %get-tuple-element.89), channel_id=1, source_target_pairs={{0,8},{4,12},{8,0},{12,4},{16,24},{20,28},{24,16},{28,20},{1,9},{5... | collective-permute-start | bytes 786440 | tf_op jit(solution)/shard_map/ppermute | solution.py:29
  22.8 1.5 %collective-permute-start.6 = (f32[512,128]{1,0:T(8,128)S(1)}, f32[512,128]{1,0:T(8,128)S(1)}, u32[]{:S(2)}, u32[]{:S(2)}) collective-permute-start(f32[512,128]{1,0:T(8,128)S(1)} %get-tuple-element.90), channel_id=1, source_target_pairs={{0,16},{4,20},{8,24},{12,28},{16,0},{20,4},{24,8},{28,12},{1,17},{... | collective-permute-start | bytes 786440 | tf_op jit(solution)/shard_map/ppermute | solution.py:29
  25.1 3.2 %reply_local_first.1 = (f32[4,512,128]{2,1,0:T(8,128)S(1)}, f32[4,512,128]{2,1,0:T(8,128)S(1)}, bf16[4,512,128]{2,1,0:T(8,128)(2,1)S(1)}, bf16[4,512,128]{2,1,0:T(8,128)(2,1)S(1)}, f32[8,128]{1,0:T(8,128)S(1)}) custom-call(s32[6]{0:T(128)S(1)} %stack.19.place, bf16[8,512,128]{2,1,0:T(8,128)(2,1)S(1)} %get-tuple-element.67.query.refs_8_, ...), custom_call_target="tpu_custom_call" | custom-call | flops 1 | bytes 1 | tf_op jit(solution)/shard_map/reply_local_first/pallas_call | solution.py:379
  28.4 2.9 %collective-permute-start.8 = (f32[256,128]{1,0:T(8,128)S(1)}, f32[256,128]{1,0:T(8,128)S(1)}, u32[]{:S(2)}, u32[]{:S(2)}) collective-permute-start(f32[256,128]{1,0:T(8,128)S(1)} %get-tuple-element.87.follows), channel_id=1, source_target_pairs={{0,3},{1,2},{2,1},{3,0},{4,7},{5,6},{6,5},{7,4},{8,11},{9,10},{10,... | collective-permute-start | bytes 393224 | tf_op jit(solution)/shard_map/ppermute | solution.py:39
  31.3 3.2 %reply_local_second.1 = (f32[4,512,128]{2,1,0:T(8,128)S(1)}, f32[4,512,128]{2,1,0:T(8,128)S(1)}, bf16[4,512,128]{2,1,0:T(8,128)(2,1)S(1)}, bf16[4,512,128]{2,1,0:T(8,128)(2,1)S(1)}, f32[8,128]{1,0:T(8,128)S(1)}) custom-call(s32[6]{0:T(128)S(1)} %stack.19.place, bf16[8,512,128]{2,1,0:T(8,128)(2,1)S(1)} %get-tuple-element.67.query.refs_8_, ...), custom_call_target="tpu_custom_call" | custom-call | flops 1 | bytes 1 | tf_op jit(solution)/shard_map/reply_local_second/pallas_call | solution.py:379
  34.5 1.3 %collective-permute-done.6.refs_2_ = f32[512,128]{1,0:T(8,128)S(1)} collective-permute-done((f32[512,128]{1,0:T(8,128)S(1)}, f32[512,128]{1,0:T(8,128)S(1)}, u32[]{:S(2)}, u32[]{:S(2)}) %collective-permute-start.6) | collective-permute-done | bytes 262176 | tf_op jit(solution)/shard_map/ppermute | solution.py:29
  37.1 1.6 %collective-permute-start.9 = (f32[512,128]{1,0:T(8,128)S(1)}, f32[512,128]{1,0:T(8,128)S(1)}, u32[]{:S(2)}, u32[]{:S(2)}) collective-permute-start(f32[512,128]{1,0:T(8,128)S(1)} %get-tuple-element.100), channel_id=1, source_target_pairs={{0,8},{4,12},{8,0},{12,4},{16,24},{20,28},{24,16},{28,20},{1,9},{5... | collective-permute-start | bytes 786440 | tf_op jit(solution)/shard_map/ppermute | solution.py:29
  38.7 1.4 %collective-permute-start.10 = (f32[512,128]{1,0:T(8,128)S(1)}, f32[512,128]{1,0:T(8,128)S(1)}, u32[]{:S(2)}, u32[]{:S(2)}) collective-permute-start(f32[512,128]{1,0:T(8,128)S(1)} %get-tuple-element.101), channel_id=1, source_target_pairs={{0,16},{4,20},{8,24},{12,28},{16,0},{20,4},{24,8},{28,12},{1,17},{... | collective-permute-start | bytes 786440 | tf_op jit(solution)/shard_map/ppermute | solution.py:29
  40.6 3.6 %collective-permute-start.14 = (f32[256,128]{1,0:T(8,128)S(1)}, f32[256,128]{1,0:T(8,128)S(1)}, u32[]{:S(2)}, u32[]{:S(2)}) collective-permute-start(f32[256,128]{1,0:T(8,128)S(1)} %get-tuple-element.93.follows.refs_4_), channel_id=1, source_target_pairs={{0,3},{1,2},{2,1},{3,0},{4,7},{5,6},{6,5},{7,4},{8,11},{9,10},{10,... | collective-permute-start | bytes 393224 | tf_op jit(solution)/shard_map/ppermute | solution.py:39
  44.4 1.8 %reply_grads.1 = (bf16[512,8,128]{2,1,0:T(8,128)(2,1)}, bf16[512,8,128]{2,1,0:T(8,128)(2,1)}, f32[8,128]{1,0:T(8,128)S(1)}) custom-call(f32[256,128]{1,0:T(8,128)S(1)} %get-tuple-element.93.follows.refs_4_, bf16[4,512,128]{2,1,0:T(8,128)(2,1)S(1)} %get-tuple-element.94.key_first, bf16[4,512,128]{2,1,0:T(8,128)(2,1)S(1)} %get-tuple-element.95.value_first, ...), custom_call_target="tpu_custom_call" | custom-call | flops 1 | bytes 1 | tf_op jit(solution)/shard_map/reply_grads/pallas_call | solution.py:379
  46.3 1.7 %collective-permute-done.14.refs_7_ = f32[256,128]{1,0:T(8,128)S(1)} collective-permute-done((f32[256,128]{1,0:T(8,128)S(1)}, f32[256,128]{1,0:T(8,128)S(1)}, u32[]{:S(2)}, u32[]{:S(2)}) %collective-permute-start.14) | collective-permute-done | bytes 131104 | tf_op jit(solution)/shard_map/ppermute | solution.py:39
  47.9 3.1 %collective-permute-done.13.refs_6_ = f32[256,128]{1,0:T(8,128)S(1)} collective-permute-done((f32[256,128]{1,0:T(8,128)S(1)}, f32[256,128]{1,0:T(8,128)S(1)}, u32[]{:S(2)}, u32[]{:S(2)}) %collective-permute-start.13) | collective-permute-done | bytes 131104 | tf_op jit(solution)/shard_map/ppermute | solution.py:39
  51.1 0.9 %halves.1 = (f32[2048,128]{1,0:T(8,128)S(1)}, f32[2048,128]{1,0:T(8,128)S(1)}, f32[256,128]{1,0:T(8,128)S(1)}, f32[256,128]{1,0:T(8,128)S(1)}, f32[256,128]{1,0:T(8,128)S(1)}, /*index=5*/f32[256,128]{1,0:T(8,128)S(1)}) custom-call(s32[6]{0:T(128)S(1)} %stack.19.place, f32[8,128]{1,0:T(8,128)S(1)} %get-tuple-element.98.follows, ...), custom_call_target="tpu_custom_call" | custom-call | flops 1 | bytes 1 | tf_op jit(solution)/shard_map/halves/pallas_call | solution.py:379
  52.1 1.2 %collective-permute-start.16 = (f32[256,128]{1,0:T(8,128)S(1)}, f32[256,128]{1,0:T(8,128)S(1)}, u32[]{:S(2)}, u32[]{:S(2)}) collective-permute-start(f32[256,128]{1,0:T(8,128)S(1)} %get-tuple-element.112), channel_id=1, source_target_pairs={{0,8},{4,12},{8,0},{12,4},{16,24},{20,28},{24,16},{28,20},{1,9},{5... | collective-permute-start | bytes 393224 | tf_op jit(solution)/shard_map/ppermute | solution.py:29
  53.3 1.2 %collective-permute-start.17 = (f32[256,128]{1,0:T(8,128)S(1)}, f32[256,128]{1,0:T(8,128)S(1)}, u32[]{:S(2)}, u32[]{:S(2)}) collective-permute-start(f32[256,128]{1,0:T(8,128)S(1)} %get-tuple-element.113), channel_id=1, source_target_pairs={{0,16},{4,20},{8,24},{12,28},{16,0},{20,4},{24,8},{28,12},{1,17},{... | collective-permute-start | bytes 393224 | tf_op jit(solution)/shard_map/ppermute | solution.py:29
  54.5 1.2 %collective-permute-start.18 = (f32[256,128]{1,0:T(8,128)S(1)}, f32[256,128]{1,0:T(8,128)S(1)}, u32[]{:S(2)}, u32[]{:S(2)}) collective-permute-start(f32[256,128]{1,0:T(8,128)S(1)} %get-tuple-element.114), channel_id=1, source_target_pairs={{0,24},{4,28},{8,16},{12,20},{16,8},{20,12},{24,0},{28,4},{1,25},{... | collective-permute-start | bytes 393224 | tf_op jit(solution)/shard_map/ppermute | solution.py:29
  55.6 4.6 %prompt_final.1 = (bf16[256,16,128]{2,1,0:T(8,128)(2,1)}, bf16[256,16,128]{2,1,0:T(8,128)(2,1)}, bf16[256,16,128]{2,1,0:T(8,128)(2,1)}, bf16[256,16,128]{2,1,0:T(8,128)(2,1)}, f32[8,128]{1,0:T(8,128)S(1)}) custom-call(s32[6]{0:T(128)S(1)} %stack.19.place, f32[2048,128]{1,0:T(8,128)S(1)} %get-tuple-element.103.mine, ...), custom_call_target="tpu_custom_call" | custom-call | flops 1 | bytes 1 | tf_op jit(solution)/shard_map/prompt_final/pallas_call | solution.py:379
  60.4 1.3 %collective-permute-done.18.refs_3_ = f32[256,128]{1,0:T(8,128)S(1)} collective-permute-done((f32[256,128]{1,0:T(8,128)S(1)}, f32[256,128]{1,0:T(8,128)S(1)}, u32[]{:S(2)}, u32[]{:S(2)}) %collective-permute-start.18) | collective-permute-done | bytes 131104 | tf_op jit(solution)/shard_map/ppermute | solution.py:29
  61.7 3.2 %reply_final.1 = (bf16[512,8,128]{2,1,0:T(8,128)(2,1)}, bf16[512,8,128]{2,1,0:T(8,128)(2,1)}) custom-call(s32[6]{0:T(128)S(1)} %stack.19.place, f32[8,128]{1,0:T(8,128)S(1)} %get-tuple-element.110.follows, f32[256,128]{1,0:T(8,128)S(1)} %get-tuple-element.111.refs_0_, f32[256,128]{1,0:T(8,128)S(1)} %collective-permute-done.16.refs_1_, ...), custom_call_target="tpu_custom_call" | custom-call | flops 1 | bytes 1 | tf_op jit(solution)/shard_map/reply_final/pallas_call | solution.py:379
  (27 shorter events, 5.8 us)
Async XLA Ops:
  7.8 4.6 %collective-permute-start = (f32[2048,128]{1,0:T(8,128)S(1)}, f32[2048,128]{1,0:T(8,128)S(1)}, u32[]{:S(2)}, u32[]{:S(2)}) collective-permute-start(f32[2048,128]{1,0:T(8,128)S(1)} %get-tuple-element.73), channel_id=1, source_target_pairs={{0,4},{4,0},{8,12},{12,8},{16,20},{20,16},{24,28},{28,24},{1,5},{5... | collective-permute-start | bytes 3145736 | tf_op jit(solution)/shard_map/ppermute | solution.py:22
  8.4 10.1 %collective-permute-start.1 = (f32[256,128]{1,0:T(8,128)S(1)}, f32[256,128]{1,0:T(8,128)S(1)}, u32[]{:S(2)}, u32[]{:S(2)}) collective-permute-start(f32[256,128]{1,0:T(8,128)S(1)} %get-tuple-element.80), channel_id=1, source_target_pairs={{0,8},{4,12},{8,0},{12,4},{16,24},{20,28},{24,16},{28,20},{1,9},{5... | collective-permute-start | bytes 393224 | tf_op jit(solution)/shard_map/ppermute | solution.py:29
  10.9 8.4 %collective-permute-start.2 = (f32[256,128]{1,0:T(8,128)S(1)}, f32[256,128]{1,0:T(8,128)S(1)}, u32[]{:S(2)}, u32[]{:S(2)}) collective-permute-start(f32[256,128]{1,0:T(8,128)S(1)} %get-tuple-element.81), channel_id=1, source_target_pairs={{0,16},{4,20},{8,24},{12,28},{16,0},{20,4},{24,8},{28,12},{1,17},{... | collective-permute-start | bytes 393224 | tf_op jit(solution)/shard_map/ppermute | solution.py:29
  12.4 6.8 %collective-permute-start.3 = (f32[256,128]{1,0:T(8,128)S(1)}, f32[256,128]{1,0:T(8,128)S(1)}, u32[]{:S(2)}, u32[]{:S(2)}) collective-permute-start(f32[256,128]{1,0:T(8,128)S(1)} %get-tuple-element.82), channel_id=1, source_target_pairs={{0,24},{4,28},{8,16},{12,20},{16,8},{20,12},{24,0},{28,4},{1,25},{... | collective-permute-start | bytes 393224 | tf_op jit(solution)/shard_map/ppermute | solution.py:29
  20.0 8.4 %collective-permute-start.4 = (f32[512,128]{1,0:T(8,128)S(1)}, f32[512,128]{1,0:T(8,128)S(1)}, u32[]{:S(2)}, u32[]{:S(2)}) collective-permute-start(f32[512,128]{1,0:T(8,128)S(1)} %get-tuple-element.86), channel_id=1, source_target_pairs={{0,1},{1,0},{2,3},{3,2},{4,5},{5,4},{6,7},{7,6},{8,9},{9,8},{10,11... | collective-permute-start | bytes 786440 | tf_op jit(solution)/shard_map/ppermute | solution.py:39
  21.6 12.9 %collective-permute-start.5 = (f32[512,128]{1,0:T(8,128)S(1)}, f32[512,128]{1,0:T(8,128)S(1)}, u32[]{:S(2)}, u32[]{:S(2)}) collective-permute-start(f32[512,128]{1,0:T(8,128)S(1)} %get-tuple-element.89), channel_id=1, source_target_pairs={{0,8},{4,12},{8,0},{12,4},{16,24},{20,28},{24,16},{28,20},{1,9},{5... | collective-permute-start | bytes 786440 | tf_op jit(solution)/shard_map/ppermute | solution.py:29
  22.8 12.9 %collective-permute-start.6 = (f32[512,128]{1,0:T(8,128)S(1)}, f32[512,128]{1,0:T(8,128)S(1)}, u32[]{:S(2)}, u32[]{:S(2)}) collective-permute-start(f32[512,128]{1,0:T(8,128)S(1)} %get-tuple-element.90), channel_id=1, source_target_pairs={{0,16},{4,20},{8,24},{12,28},{16,0},{20,4},{24,8},{28,12},{1,17},{... | collective-permute-start | bytes 786440 | tf_op jit(solution)/shard_map/ppermute | solution.py:29
  24.3 11.5 %collective-permute-start.7 = (f32[512,128]{1,0:T(8,128)S(1)}, f32[512,128]{1,0:T(8,128)S(1)}, u32[]{:S(2)}, u32[]{:S(2)}) collective-permute-start(f32[512,128]{1,0:T(8,128)S(1)} %get-tuple-element.91), channel_id=1, source_target_pairs={{0,24},{4,28},{8,16},{12,20},{16,8},{20,12},{24,0},{28,4},{1,25},{... | collective-permute-start | bytes 786440 | tf_op jit(solution)/shard_map/ppermute | solution.py:29
  28.4 7.4 %collective-permute-start.8 = (f32[256,128]{1,0:T(8,128)S(1)}, f32[256,128]{1,0:T(8,128)S(1)}, u32[]{:S(2)}, u32[]{:S(2)}) collective-permute-start(f32[256,128]{1,0:T(8,128)S(1)} %get-tuple-element.87.follows), channel_id=1, source_target_pairs={{0,3},{1,2},{2,1},{3,0},{4,7},{5,6},{6,5},{7,4},{8,11},{9,10},{10,... | collective-permute-start | bytes 393224 | tf_op jit(solution)/shard_map/ppermute | solution.py:39
  36.6 7.6 %collective-permute-start.12 = (f32[256,128]{1,0:T(8,128)S(1)}, f32[256,128]{1,0:T(8,128)S(1)}, u32[]{:S(2)}, u32[]{:S(2)}) collective-permute-start(f32[256,128]{1,0:T(8,128)S(1)} %get-tuple-element.93.follows.refs_4_), channel_id=1, source_target_pairs={{0,1},{1,0},{2,3},{3,2},{4,5},{5,4},{6,7},{7,6},{8,9},{9,8},{10,11... | collective-permute-start | bytes 393224 | tf_op jit(solution)/shard_map/ppermute | solution.py:39
  37.1 14.0 %collective-permute-start.9 = (f32[512,128]{1,0:T(8,128)S(1)}, f32[512,128]{1,0:T(8,128)S(1)}, u32[]{:S(2)}, u32[]{:S(2)}) collective-permute-start(f32[512,128]{1,0:T(8,128)S(1)} %get-tuple-element.100), channel_id=1, source_target_pairs={{0,8},{4,12},{8,0},{12,4},{16,24},{20,28},{24,16},{28,20},{1,9},{5... | collective-permute-start | bytes 786440 | tf_op jit(solution)/shard_map/ppermute | solution.py:29
  38.7 12.4 %collective-permute-start.10 = (f32[512,128]{1,0:T(8,128)S(1)}, f32[512,128]{1,0:T(8,128)S(1)}, u32[]{:S(2)}, u32[]{:S(2)}) collective-permute-start(f32[512,128]{1,0:T(8,128)S(1)} %get-tuple-element.101), channel_id=1, source_target_pairs={{0,16},{4,20},{8,24},{12,28},{16,0},{20,4},{24,8},{28,12},{1,17},{... | collective-permute-start | bytes 786440 | tf_op jit(solution)/shard_map/ppermute | solution.py:29
  40.1 11.0 %collective-permute-start.11 = (f32[512,128]{1,0:T(8,128)S(1)}, f32[512,128]{1,0:T(8,128)S(1)}, u32[]{:S(2)}, u32[]{:S(2)}) collective-permute-start(f32[512,128]{1,0:T(8,128)S(1)} %get-tuple-element.102), channel_id=1, source_target_pairs={{0,24},{4,28},{8,16},{12,20},{16,8},{20,12},{24,0},{28,4},{1,25},{... | collective-permute-start | bytes 786440 | tf_op jit(solution)/shard_map/ppermute | solution.py:29
  40.6 7.3 %collective-permute-start.14 = (f32[256,128]{1,0:T(8,128)S(1)}, f32[256,128]{1,0:T(8,128)S(1)}, u32[]{:S(2)}, u32[]{:S(2)}) collective-permute-start(f32[256,128]{1,0:T(8,128)S(1)} %get-tuple-element.93.follows.refs_4_), channel_id=1, source_target_pairs={{0,3},{1,2},{2,1},{3,0},{4,7},{5,6},{6,5},{7,4},{8,11},{9,10},{10,... | collective-permute-start | bytes 393224 | tf_op jit(solution)/shard_map/ppermute | solution.py:39
  44.2 6.9 %collective-permute-start.13 = (f32[256,128]{1,0:T(8,128)S(1)}, f32[256,128]{1,0:T(8,128)S(1)}, u32[]{:S(2)}, u32[]{:S(2)}) collective-permute-start(f32[256,128]{1,0:T(8,128)S(1)} %collective-permute-done.12.refs_5_), channel_id=1, source_target_pairs={{0,3},{1,2},{2,1},{3,0},{4,7},{5,6},{6,5},{7,4},{8,11},{9,10},{10,... | collective-permute-start | bytes 393224 | tf_op jit(solution)/shard_map/ppermute | solution.py:39
  52.0 3.6 %collective-permute-start.15 = (f32[2048,128]{1,0:T(8,128)S(1)}, f32[2048,128]{1,0:T(8,128)S(1)}, u32[]{:S(2)}, u32[]{:S(2)}) collective-permute-start(f32[2048,128]{1,0:T(8,128)S(1)} %get-tuple-element.104), channel_id=1, source_target_pairs={{0,4},{4,0},{8,12},{12,8},{16,20},{20,16},{24,28},{28,24},{1,5},{5... | collective-permute-start | bytes 3145736 | tf_op jit(solution)/shard_map/ppermute | solution.py:22
  52.1 8.2 %collective-permute-start.16 = (f32[256,128]{1,0:T(8,128)S(1)}, f32[256,128]{1,0:T(8,128)S(1)}, u32[]{:S(2)}, u32[]{:S(2)}) collective-permute-start(f32[256,128]{1,0:T(8,128)S(1)} %get-tuple-element.112), channel_id=1, source_target_pairs={{0,8},{4,12},{8,0},{12,4},{16,24},{20,28},{24,16},{28,20},{1,9},{5... | collective-permute-start | bytes 393224 | tf_op jit(solution)/shard_map/ppermute | solution.py:29
  53.3 7.1 %collective-permute-start.17 = (f32[256,128]{1,0:T(8,128)S(1)}, f32[256,128]{1,0:T(8,128)S(1)}, u32[]{:S(2)}, u32[]{:S(2)}) collective-permute-start(f32[256,128]{1,0:T(8,128)S(1)} %get-tuple-element.113), channel_id=1, source_target_pairs={{0,16},{4,20},{8,24},{12,28},{16,0},{20,4},{24,8},{28,12},{1,17},{... | collective-permute-start | bytes 393224 | tf_op jit(solution)/shard_map/ppermute | solution.py:29
  54.5 7.2 %collective-permute-start.18 = (f32[256,128]{1,0:T(8,128)S(1)}, f32[256,128]{1,0:T(8,128)S(1)}, u32[]{:S(2)}, u32[]{:S(2)}) collective-permute-start(f32[256,128]{1,0:T(8,128)S(1)} %get-tuple-element.114), channel_id=1, source_target_pairs={{0,24},{4,28},{8,16},{12,20},{16,8},{20,12},{24,0},{28,4},{1,25},{... | collective-permute-start | bytes 393224 | tf_op jit(solution)/shard_map/ppermute | solution.py:29

commit v4 on v3

--- a/solution.py
+++ b/solution.py
@@ -62,15 +62,20 @@
     return lax.rsqrt(float(head_size) * (rows.astype(F32) + 1.0))
 
 
-def to_heads(target, source, factor=None):
+def to_heads(target, source, factor=None, scaled=None):
     rows = source.shape[0]
     chunk = CHUNK if rows % CHUNK == 0 else rows
 
     def one(i, carry):
-        span = pl.ds(pl.multiple_of(i * chunk, chunk), chunk)
+        start = pl.multiple_of(i * chunk, chunk)
+        span = pl.ds(start, chunk)
         part = jnp.swapaxes(source[span], 0, 1)
         if factor is not None:
-            part = (part.astype(F32) * factor[span][None]).astype(BF16)
+            product = (part.astype(F32) * factor(start, chunk)[None]).astype(BF16)
+            if scaled is None:
+                part = product
+            else:
+                scaled[:, span, :] = product
         target[:, span, :] = part
         return carry
 
@@ -93,7 +98,7 @@
     sources, refs = refs[:6], refs[6:]
     sent, kept, key, value, query, cotangent, r_query, r_cotangent = refs[:8]
     pieces, refs = refs[8 : 8 + steps], refs[8 + steps :]
-    buffers, (scaled, r_scaled, r_moment, factor, arrived) = refs[:6], refs[6:]
+    buffers, (scaled, r_scaled, r_moment, arrived) = refs[:6], refs[6:]
     copies = load(sources, buffers, arrived)
     member, first_row, reply_first, length = (place[i] for i in (0, 2, 3, 4))
     heads, rows, size = query.shape
@@ -110,12 +115,12 @@
             return carry
 
         lax.fori_loop(0, half, state, 0, unroll=True)
-    for i, target in enumerate((query, cotangent)):
-        copies[2 + i].wait()
-        to_heads(target, buffers[2 + i])
-    scale = row_scale(first_row, rows, size)
-    for h in range(heads):
-        scaled[h] = (query[h].astype(F32) * scale).astype(BF16)
+    copies[2].wait()
+    to_heads(
+        query, buffers[2], lambda start, total: row_scale(first_row + start, total, size), scaled
+    )
+    copies[3].wait()
+    to_heads(cotangent, buffers[3])
     for target, base in halves:
 
         def moment(j, carry, target=target, base=base):
@@ -124,15 +129,19 @@
             return carry
 
         lax.fori_loop(0, half, moment, 0, unroll=True)
+    def live_weight(start, total):
+        rows_at = lax.broadcasted_iota(jnp.int32, (total, size), 0) + start
+        return jnp.where(rows_at < length, weight[0], 0.0)
+
     copies[4].wait()
-    to_heads(r_query, buffers[4])
+    to_heads(
+        r_query,
+        buffers[4],
+        lambda start, total: row_scale(reply_first + start, total, size),
+        r_scaled,
+    )
     copies[5].wait()
-    live = lax.broadcasted_iota(jnp.int32, factor.shape, 0) < length
-    factor[...] = jnp.where(live, weight[0], 0.0)
-    to_heads(r_cotangent, buffers[5], factor)
-    scale = row_scale(reply_first, r_query.shape[1], size)
-    for h in range(r_query.shape[0]):
-        r_scaled[h] = (r_query[h].astype(F32) * scale).astype(BF16)
+    to_heads(r_cotangent, buffers[5], live_weight)
     for h in range(r_query.shape[0]):
         r_moment[pl.ds(h * size, size), :] = dot(r_scaled[h], r_cotangent[h], ROWS_ROWS)
     piece_rows = pieces[0].shape[0]
@@ -348,9 +357,14 @@
     copies = []
 
     def finish(i, target):
-        staged[i] = by_head(held[i])
-        copies.append(pltpu.make_async_copy(staged.at[i], target, left.at[i]))
-        copies[-1].start()
+        part = rows // 4
+        for start in range(0, rows, part):
+            span = pl.ds(start, part)
+            staged[i, span] = by_head(held[i, :, span])
+            copies.append(
+                pltpu.make_async_copy(staged.at[i, span], target.at[span], left.at[len(copies)])
+            )
+            copies[-1].start()
 
     for h in range(heads):
         final = state[pl.ds(h * size, size), :]
@@ -451,7 +465,7 @@
         [scratch(prompt_bf16)] * 4
         + [scratch(reply_bf16)] * 2
         + [scratch(prompt_held), scratch(reply_held)]
-        + [pltpu.VMEM((reply_heads * size, size), F32), pltpu.VMEM((reply_rows, size), F32)]
+        + [pltpu.VMEM((reply_heads * size, size), F32)]
         + [pltpu.SemaphoreType.DMA((6,))],
         "moments",
     )
@@ -574,7 +588,7 @@
             pltpu.VMEM((reply_heads * size, size), BF16),
             scratch(reply_held, 2),
             scratch(reply_bf16, 2),
-            pltpu.SemaphoreType.DMA((2,)),
+            pltpu.SemaphoreType.DMA((8,)),
         ],
         "reply_final",
     )

time: 65.2 us -> 65 us (level)
  no operation moved by 1% of the time
where the time goes in v4:
time: 65 us; the launch traced here: 64.8 us
  Pallas kernels  30.1 us (46%)
  starting transfers between devices  24.1 us (37%)
  waiting for transfers between devices  8.28 us (13%)
  between operations  2.23 us (3%)
    pallas_call x12, Pallas kernels, call(): pl.pallas_call(kernel, out_shape=[out for _, out in outs], in_specs=[pl.B...  30.1 us
    ppermute x12, starting transfers between devices, plane_exchange(): lax.ppermute(pieces[k], PLANE, [(b, b ^ 2 * k) for b in range(count)])  14.6 us
    ppermute x5, starting transfers between devices, resp_step(): return lax.ppermute(array, 'resp', [(z, z ^ mask) for z in range(count)])  8.88 us
    ppermute x5, waiting for transfers between devices, resp_step(): return lax.ppermute(array, 'resp', [(z, z ^ mask) for z in range(count)])  4.81 us
    ppermute x12, waiting for transfers between devices, plane_exchange(): lax.ppermute(pieces[k], PLANE, [(b, b ^ 2 * k) for b in range(count)])  3.47 us
  transfers between devices with their start and end apart: 19, of which 6 were waited for; matrix products, arithmetic and copies ran while one was open for 0% of the time, Pallas kernels for 29%

profile of v4, /device:TPU:0, one launch (start us, length us, event | category | flops | bytes accessed | tf_op | source)
XLA Modules:
  0.0 64.8 jit_solution(14399858807138929335)
XLA Ops:
  2.0 5.9 %moments.1 = (f32[2048,128]{1,0:T(8,128)S(1)}, f32[2048,128]{1,0:T(8,128)S(1)}, bf16[16,256,128]{2,1,0:T(8,128)(2,1)S(1)}, bf16[16,256,128]{2,1,0:T(8,128)(2,1)S...) custom-call(s32[6]{0:T(128)S(1)} %stack.19.place, ...), custom_call_target="tpu_custom_call" | custom-call | flops 1 | bytes 1 | tf_op jit(solution)/shard_map/moments/pallas_call | solution.py:393
  8.4 2.6 %collective-permute-start.1 = (f32[256,128]{1,0:T(8,128)S(1)}, f32[256,128]{1,0:T(8,128)S(1)}, u32[]{:S(2)}, u32[]{:S(2)}) collective-permute-start(f32[256,128]{1,0:T(8,128)S(1)} %get-tuple-element.80), channel_id=1, source_target_pairs={{0,8},{4,12},{8,0},{12,4},{16,24},{20,28},{24,16},{28,20},{1,9},{5... | collective-permute-start | bytes 393224 | tf_op jit(solution)/shard_map/ppermute | solution.py:29
  11.0 1.5 %collective-permute-start.2 = (f32[256,128]{1,0:T(8,128)S(1)}, f32[256,128]{1,0:T(8,128)S(1)}, u32[]{:S(2)}, u32[]{:S(2)}) collective-permute-start(f32[256,128]{1,0:T(8,128)S(1)} %get-tuple-element.81), channel_id=1, source_target_pairs={{0,16},{4,20},{8,24},{12,28},{16,0},{20,4},{24,8},{28,12},{1,17},{... | collective-permute-start | bytes 393224 | tf_op jit(solution)/shard_map/ppermute | solution.py:29
  13.2 5.4 %prompt_local.1 = (f32[16,256,128]{2,1,0:T(8,128)S(1)}, f32[16,256,128]{2,1,0:T(8,128)S(1)}, f32[16,256,128]{2,1,0:T(8,128)S(1)}, f32[16,256,128]{2,1,0:T(8,128)...) custom-call(s32[6]{0:T(128)S(1)} %stack.19.place, ...), custom_call_target="tpu_custom_call" | custom-call | flops 1 | bytes 1 | tf_op jit(solution)/shard_map/prompt_local/pallas_call | solution.py:393
  20.0 1.6 %collective-permute-start.4 = (f32[512,128]{1,0:T(8,128)S(1)}, f32[512,128]{1,0:T(8,128)S(1)}, u32[]{:S(2)}, u32[]{:S(2)}) collective-permute-start(f32[512,128]{1,0:T(8,128)S(1)} %get-tuple-element.86), channel_id=1, source_target_pairs={{0,1},{1,0},{2,3},{3,2},{4,5},{5,4},{6,7},{7,6},{8,9},{9,8},{10,11... | collective-permute-start | bytes 786440 | tf_op jit(solution)/shard_map/ppermute | solution.py:39
  21.7 1.2 %collective-permute-start.5 = (f32[512,128]{1,0:T(8,128)S(1)}, f32[512,128]{1,0:T(8,128)S(1)}, u32[]{:S(2)}, u32[]{:S(2)}) collective-permute-start(f32[512,128]{1,0:T(8,128)S(1)} %get-tuple-element.89), channel_id=1, source_target_pairs={{0,8},{4,12},{8,0},{12,4},{16,24},{20,28},{24,16},{28,20},{1,9},{5... | collective-permute-start | bytes 786440 | tf_op jit(solution)/shard_map/ppermute | solution.py:29
  22.9 1.5 %collective-permute-start.6 = (f32[512,128]{1,0:T(8,128)S(1)}, f32[512,128]{1,0:T(8,128)S(1)}, u32[]{:S(2)}, u32[]{:S(2)}) collective-permute-start(f32[512,128]{1,0:T(8,128)S(1)} %get-tuple-element.90), channel_id=1, source_target_pairs={{0,16},{4,20},{8,24},{12,28},{16,0},{20,4},{24,8},{28,12},{1,17},{... | collective-permute-start | bytes 786440 | tf_op jit(solution)/shard_map/ppermute | solution.py:29
  25.1 3.2 %reply_local_first.1 = (f32[4,512,128]{2,1,0:T(8,128)S(1)}, f32[4,512,128]{2,1,0:T(8,128)S(1)}, bf16[4,512,128]{2,1,0:T(8,128)(2,1)S(1)}, bf16[4,512,128]{2,1,0:T(8,128)(2,1)S(1)}, f32[8,128]{1,0:T(8,128)S(1)}) custom-call(s32[6]{0:T(128)S(1)} %stack.19.place, bf16[8,512,128]{2,1,0:T(8,128)(2,1)S(1)} %get-tuple-element.67.query.refs_8_, ...), custom_call_target="tpu_custom_call" | custom-call | flops 1 | bytes 1 | tf_op jit(solution)/shard_map/reply_local_first/pallas_call | solution.py:393
  28.4 2.9 %collective-permute-start.8 = (f32[256,128]{1,0:T(8,128)S(1)}, f32[256,128]{1,0:T(8,128)S(1)}, u32[]{:S(2)}, u32[]{:S(2)}) collective-permute-start(f32[256,128]{1,0:T(8,128)S(1)} %get-tuple-element.87.follows), channel_id=1, source_target_pairs={{0,3},{1,2},{2,1},{3,0},{4,7},{5,6},{6,5},{7,4},{8,11},{9,10},{10,... | collective-permute-start | bytes 393224 | tf_op jit(solution)/shard_map/ppermute | solution.py:39
  31.3 3.2 %reply_local_second.1 = (f32[4,512,128]{2,1,0:T(8,128)S(1)}, f32[4,512,128]{2,1,0:T(8,128)S(1)}, bf16[4,512,128]{2,1,0:T(8,128)(2,1)S(1)}, bf16[4,512,128]{2,1,0:T(8,128)(2,1)S(1)}, f32[8,128]{1,0:T(8,128)S(1)}) custom-call(s32[6]{0:T(128)S(1)} %stack.19.place, bf16[8,512,128]{2,1,0:T(8,128)(2,1)S(1)} %get-tuple-element.67.query.refs_8_, ...), custom_call_target="tpu_custom_call" | custom-call | flops 1 | bytes 1 | tf_op jit(solution)/shard_map/reply_local_second/pallas_call | solution.py:393
  34.5 1.3 %collective-permute-done.6.refs_2_ = f32[512,128]{1,0:T(8,128)S(1)} collective-permute-done((f32[512,128]{1,0:T(8,128)S(1)}, f32[512,128]{1,0:T(8,128)S(1)}, u32[]{:S(2)}, u32[]{:S(2)}) %collective-permute-start.6) | collective-permute-done | bytes 262176 | tf_op jit(solution)/shard_map/ppermute | solution.py:29
  37.2 1.6 %collective-permute-start.9 = (f32[512,128]{1,0:T(8,128)S(1)}, f32[512,128]{1,0:T(8,128)S(1)}, u32[]{:S(2)}, u32[]{:S(2)}) collective-permute-start(f32[512,128]{1,0:T(8,128)S(1)} %get-tuple-element.100), channel_id=1, source_target_pairs={{0,8},{4,12},{8,0},{12,4},{16,24},{20,28},{24,16},{28,20},{1,9},{5... | collective-permute-start | bytes 786440 | tf_op jit(solution)/shard_map/ppermute | solution.py:29
  38.7 1.4 %collective-permute-start.10 = (f32[512,128]{1,0:T(8,128)S(1)}, f32[512,128]{1,0:T(8,128)S(1)}, u32[]{:S(2)}, u32[]{:S(2)}) collective-permute-start(f32[512,128]{1,0:T(8,128)S(1)} %get-tuple-element.101), channel_id=1, source_target_pairs={{0,16},{4,20},{8,24},{12,28},{16,0},{20,4},{24,8},{28,12},{1,17},{... | collective-permute-start | bytes 786440 | tf_op jit(solution)/shard_map/ppermute | solution.py:29
  40.6 3.6 %collective-permute-start.14 = (f32[256,128]{1,0:T(8,128)S(1)}, f32[256,128]{1,0:T(8,128)S(1)}, u32[]{:S(2)}, u32[]{:S(2)}) collective-permute-start(f32[256,128]{1,0:T(8,128)S(1)} %get-tuple-element.93.follows.refs_4_), channel_id=1, source_target_pairs={{0,3},{1,2},{2,1},{3,0},{4,7},{5,6},{6,5},{7,4},{8,11},{9,10},{10,... | collective-permute-start | bytes 393224 | tf_op jit(solution)/shard_map/ppermute | solution.py:39
  44.5 1.8 %reply_grads.1 = (bf16[512,8,128]{2,1,0:T(8,128)(2,1)}, bf16[512,8,128]{2,1,0:T(8,128)(2,1)}, f32[8,128]{1,0:T(8,128)S(1)}) custom-call(f32[256,128]{1,0:T(8,128)S(1)} %get-tuple-element.93.follows.refs_4_, bf16[4,512,128]{2,1,0:T(8,128)(2,1)S(1)} %get-tuple-element.94.key_first, bf16[4,512,128]{2,1,0:T(8,128)(2,1)S(1)} %get-tuple-element.95.value_first, ...), custom_call_target="tpu_custom_call" | custom-call | flops 1 | bytes 1 | tf_op jit(solution)/shard_map/reply_grads/pallas_call | solution.py:393
  46.3 1.7 %collective-permute-done.14.refs_7_ = f32[256,128]{1,0:T(8,128)S(1)} collective-permute-done((f32[256,128]{1,0:T(8,128)S(1)}, f32[256,128]{1,0:T(8,128)S(1)}, u32[]{:S(2)}, u32[]{:S(2)}) %collective-permute-start.14) | collective-permute-done | bytes 131104 | tf_op jit(solution)/shard_map/ppermute | solution.py:39
  48.0 3.1 %collective-permute-done.13.refs_6_ = f32[256,128]{1,0:T(8,128)S(1)} collective-permute-done((f32[256,128]{1,0:T(8,128)S(1)}, f32[256,128]{1,0:T(8,128)S(1)}, u32[]{:S(2)}, u32[]{:S(2)}) %collective-permute-start.13) | collective-permute-done | bytes 131104 | tf_op jit(solution)/shard_map/ppermute | solution.py:39
  51.1 0.9 %halves.1 = (f32[2048,128]{1,0:T(8,128)S(1)}, f32[2048,128]{1,0:T(8,128)S(1)}, f32[256,128]{1,0:T(8,128)S(1)}, f32[256,128]{1,0:T(8,128)S(1)}, f32[256,128]{1,0:T(8,128)S(1)}, /*index=5*/f32[256,128]{1,0:T(8,128)S(1)}) custom-call(s32[6]{0:T(128)S(1)} %stack.19.place, f32[8,128]{1,0:T(8,128)S(1)} %get-tuple-element.98.follows, ...), custom_call_target="tpu_custom_call" | custom-call | flops 1 | bytes 1 | tf_op jit(solution)/shard_map/halves/pallas_call | solution.py:393
  52.1 1.2 %collective-permute-start.16 = (f32[256,128]{1,0:T(8,128)S(1)}, f32[256,128]{1,0:T(8,128)S(1)}, u32[]{:S(2)}, u32[]{:S(2)}) collective-permute-start(f32[256,128]{1,0:T(8,128)S(1)} %get-tuple-element.112), channel_id=1, source_target_pairs={{0,8},{4,12},{8,0},{12,4},{16,24},{20,28},{24,16},{28,20},{1,9},{5... | collective-permute-start | bytes 393224 | tf_op jit(solution)/shard_map/ppermute | solution.py:29
  53.3 1.2 %collective-permute-start.17 = (f32[256,128]{1,0:T(8,128)S(1)}, f32[256,128]{1,0:T(8,128)S(1)}, u32[]{:S(2)}, u32[]{:S(2)}) collective-permute-start(f32[256,128]{1,0:T(8,128)S(1)} %get-tuple-element.113), channel_id=1, source_target_pairs={{0,16},{4,20},{8,24},{12,28},{16,0},{20,4},{24,8},{28,12},{1,17},{... | collective-permute-start | bytes 393224 | tf_op jit(solution)/shard_map/ppermute | solution.py:29
  54.5 1.2 %collective-permute-start.18 = (f32[256,128]{1,0:T(8,128)S(1)}, f32[256,128]{1,0:T(8,128)S(1)}, u32[]{:S(2)}, u32[]{:S(2)}) collective-permute-start(f32[256,128]{1,0:T(8,128)S(1)} %get-tuple-element.114), channel_id=1, source_target_pairs={{0,24},{4,28},{8,16},{12,20},{16,8},{20,12},{24,0},{28,4},{1,25},{... | collective-permute-start | bytes 393224 | tf_op jit(solution)/shard_map/ppermute | solution.py:29
  55.7 4.6 %prompt_final.1 = (bf16[256,16,128]{2,1,0:T(8,128)(2,1)}, bf16[256,16,128]{2,1,0:T(8,128)(2,1)}, bf16[256,16,128]{2,1,0:T(8,128)(2,1)}, bf16[256,16,128]{2,1,0:T(8,128)(2,1)}, f32[8,128]{1,0:T(8,128)S(1)}) custom-call(s32[6]{0:T(128)S(1)} %stack.19.place, f32[2048,128]{1,0:T(8,128)S(1)} %get-tuple-element.103.mine, ...), custom_call_target="tpu_custom_call" | custom-call | flops 1 | bytes 1 | tf_op jit(solution)/shard_map/prompt_final/pallas_call | solution.py:393
  60.4 1.3 %collective-permute-done.18.refs_3_ = f32[256,128]{1,0:T(8,128)S(1)} collective-permute-done((f32[256,128]{1,0:T(8,128)S(1)}, f32[256,128]{1,0:T(8,128)S(1)}, u32[]{:S(2)}, u32[]{:S(2)}) %collective-permute-start.18) | collective-permute-done | bytes 131104 | tf_op jit(solution)/shard_map/ppermute | solution.py:29
  61.7 2.9 %reply_final.1 = (bf16[512,8,128]{2,1,0:T(8,128)(2,1)}, bf16[512,8,128]{2,1,0:T(8,128)(2,1)}) custom-call(s32[6]{0:T(128)S(1)} %stack.19.place, f32[8,128]{1,0:T(8,128)S(1)} %get-tuple-element.110.follows, f32[256,128]{1,0:T(8,128)S(1)} %get-tuple-element.111.refs_0_, f32[256,128]{1,0:T(8,128)S(1)} %collective-permute-done.16.refs_1_, ...), custom_call_target="tpu_custom_call" | custom-call | flops 1 | bytes 1 | tf_op jit(solution)/shard_map/reply_final/pallas_call | solution.py:393
  (27 shorter events, 5.8 us)
Async XLA Ops:
  7.9 4.6 %collective-permute-start = (f32[2048,128]{1,0:T(8,128)S(1)}, f32[2048,128]{1,0:T(8,128)S(1)}, u32[]{:S(2)}, u32[]{:S(2)}) collective-permute-start(f32[2048,128]{1,0:T(8,128)S(1)} %get-tuple-element.73), channel_id=1, source_target_pairs={{0,4},{4,0},{8,12},{12,8},{16,20},{20,16},{24,28},{28,24},{1,5},{5... | collective-permute-start | bytes 3145736 | tf_op jit(solution)/shard_map/ppermute | solution.py:22
  8.4 10.2 %collective-permute-start.1 = (f32[256,128]{1,0:T(8,128)S(1)}, f32[256,128]{1,0:T(8,128)S(1)}, u32[]{:S(2)}, u32[]{:S(2)}) collective-permute-start(f32[256,128]{1,0:T(8,128)S(1)} %get-tuple-element.80), channel_id=1, source_target_pairs={{0,8},{4,12},{8,0},{12,4},{16,24},{20,28},{24,16},{28,20},{1,9},{5... | collective-permute-start | bytes 393224 | tf_op jit(solution)/shard_map/ppermute | solution.py:29
  11.0 8.4 %collective-permute-start.2 = (f32[256,128]{1,0:T(8,128)S(1)}, f32[256,128]{1,0:T(8,128)S(1)}, u32[]{:S(2)}, u32[]{:S(2)}) collective-permute-start(f32[256,128]{1,0:T(8,128)S(1)} %get-tuple-element.81), channel_id=1, source_target_pairs={{0,16},{4,20},{8,24},{12,28},{16,0},{20,4},{24,8},{28,12},{1,17},{... | collective-permute-start | bytes 393224 | tf_op jit(solution)/shard_map/ppermute | solution.py:29
  12.5 6.9 %collective-permute-start.3 = (f32[256,128]{1,0:T(8,128)S(1)}, f32[256,128]{1,0:T(8,128)S(1)}, u32[]{:S(2)}, u32[]{:S(2)}) collective-permute-start(f32[256,128]{1,0:T(8,128)S(1)} %get-tuple-element.82), channel_id=1, source_target_pairs={{0,24},{4,28},{8,16},{12,20},{16,8},{20,12},{24,0},{28,4},{1,25},{... | collective-permute-start | bytes 393224 | tf_op jit(solution)/shard_map/ppermute | solution.py:29
  20.0 8.4 %collective-permute-start.4 = (f32[512,128]{1,0:T(8,128)S(1)}, f32[512,128]{1,0:T(8,128)S(1)}, u32[]{:S(2)}, u32[]{:S(2)}) collective-permute-start(f32[512,128]{1,0:T(8,128)S(1)} %get-tuple-element.86), channel_id=1, source_target_pairs={{0,1},{1,0},{2,3},{3,2},{4,5},{5,4},{6,7},{7,6},{8,9},{9,8},{10,11... | collective-permute-start | bytes 786440 | tf_op jit(solution)/shard_map/ppermute | solution.py:39
  21.7 12.9 %collective-permute-start.5 = (f32[512,128]{1,0:T(8,128)S(1)}, f32[512,128]{1,0:T(8,128)S(1)}, u32[]{:S(2)}, u32[]{:S(2)}) collective-permute-start(f32[512,128]{1,0:T(8,128)S(1)} %get-tuple-element.89), channel_id=1, source_target_pairs={{0,8},{4,12},{8,0},{12,4},{16,24},{20,28},{24,16},{28,20},{1,9},{5... | collective-permute-start | bytes 786440 | tf_op jit(solution)/shard_map/ppermute | solution.py:29
  22.9 12.9 %collective-permute-start.6 = (f32[512,128]{1,0:T(8,128)S(1)}, f32[512,128]{1,0:T(8,128)S(1)}, u32[]{:S(2)}, u32[]{:S(2)}) collective-permute-start(f32[512,128]{1,0:T(8,128)S(1)} %get-tuple-element.90), channel_id=1, source_target_pairs={{0,16},{4,20},{8,24},{12,28},{16,0},{20,4},{24,8},{28,12},{1,17},{... | collective-permute-start | bytes 786440 | tf_op jit(solution)/shard_map/ppermute | solution.py:29
  24.4 11.5 %collective-permute-start.7 = (f32[512,128]{1,0:T(8,128)S(1)}, f32[512,128]{1,0:T(8,128)S(1)}, u32[]{:S(2)}, u32[]{:S(2)}) collective-permute-start(f32[512,128]{1,0:T(8,128)S(1)} %get-tuple-element.91), channel_id=1, source_target_pairs={{0,24},{4,28},{8,16},{12,20},{16,8},{20,12},{24,0},{28,4},{1,25},{... | collective-permute-start | bytes 786440 | tf_op jit(solution)/shard_map/ppermute | solution.py:29
  28.4 7.4 %collective-permute-start.8 = (f32[256,128]{1,0:T(8,128)S(1)}, f32[256,128]{1,0:T(8,128)S(1)}, u32[]{:S(2)}, u32[]{:S(2)}) collective-permute-start(f32[256,128]{1,0:T(8,128)S(1)} %get-tuple-element.87.follows), channel_id=1, source_target_pairs={{0,3},{1,2},{2,1},{3,0},{4,7},{5,6},{6,5},{7,4},{8,11},{9,10},{10,... | collective-permute-start | bytes 393224 | tf_op jit(solution)/shard_map/ppermute | solution.py:39
  36.6 7.6 %collective-permute-start.12 = (f32[256,128]{1,0:T(8,128)S(1)}, f32[256,128]{1,0:T(8,128)S(1)}, u32[]{:S(2)}, u32[]{:S(2)}) collective-permute-start(f32[256,128]{1,0:T(8,128)S(1)} %get-tuple-element.93.follows.refs_4_), channel_id=1, source_target_pairs={{0,1},{1,0},{2,3},{3,2},{4,5},{5,4},{6,7},{7,6},{8,9},{9,8},{10,11... | collective-permute-start | bytes 393224 | tf_op jit(solution)/shard_map/ppermute | solution.py:39
  37.2 14.0 %collective-permute-start.9 = (f32[512,128]{1,0:T(8,128)S(1)}, f32[512,128]{1,0:T(8,128)S(1)}, u32[]{:S(2)}, u32[]{:S(2)}) collective-permute-start(f32[512,128]{1,0:T(8,128)S(1)} %get-tuple-element.100), channel_id=1, source_target_pairs={{0,8},{4,12},{8,0},{12,4},{16,24},{20,28},{24,16},{28,20},{1,9},{5... | collective-permute-start | bytes 786440 | tf_op jit(solution)/shard_map/ppermute | solution.py:29
  38.7 12.4 %collective-permute-start.10 = (f32[512,128]{1,0:T(8,128)S(1)}, f32[512,128]{1,0:T(8,128)S(1)}, u32[]{:S(2)}, u32[]{:S(2)}) collective-permute-start(f32[512,128]{1,0:T(8,128)S(1)} %get-tuple-element.101), channel_id=1, source_target_pairs={{0,16},{4,20},{8,24},{12,28},{16,0},{20,4},{24,8},{28,12},{1,17},{... | collective-permute-start | bytes 786440 | tf_op jit(solution)/shard_map/ppermute | solution.py:29
  40.2 10.9 %collective-permute-start.11 = (f32[512,128]{1,0:T(8,128)S(1)}, f32[512,128]{1,0:T(8,128)S(1)}, u32[]{:S(2)}, u32[]{:S(2)}) collective-permute-start(f32[512,128]{1,0:T(8,128)S(1)} %get-tuple-element.102), channel_id=1, source_target_pairs={{0,24},{4,28},{8,16},{12,20},{16,8},{20,12},{24,0},{28,4},{1,25},{... | collective-permute-start | bytes 786440 | tf_op jit(solution)/shard_map/ppermute | solution.py:29
  40.6 7.4 %collective-permute-start.14 = (f32[256,128]{1,0:T(8,128)S(1)}, f32[256,128]{1,0:T(8,128)S(1)}, u32[]{:S(2)}, u32[]{:S(2)}) collective-permute-start(f32[256,128]{1,0:T(8,128)S(1)} %get-tuple-element.93.follows.refs_4_), channel_id=1, source_target_pairs={{0,3},{1,2},{2,1},{3,0},{4,7},{5,6},{6,5},{7,4},{8,11},{9,10},{10,... | collective-permute-start | bytes 393224 | tf_op jit(solution)/shard_map/ppermute | solution.py:39
  44.2 6.9 %collective-permute-start.13 = (f32[256,128]{1,0:T(8,128)S(1)}, f32[256,128]{1,0:T(8,128)S(1)}, u32[]{:S(2)}, u32[]{:S(2)}) collective-permute-start(f32[256,128]{1,0:T(8,128)S(1)} %collective-permute-done.12.refs_5_), channel_id=1, source_target_pairs={{0,3},{1,2},{2,1},{3,0},{4,7},{5,6},{6,5},{7,4},{8,11},{9,10},{10,... | collective-permute-start | bytes 393224 | tf_op jit(solution)/shard_map/ppermute | solution.py:39
  52.1 3.6 %collective-permute-start.15 = (f32[2048,128]{1,0:T(8,128)S(1)}, f32[2048,128]{1,0:T(8,128)S(1)}, u32[]{:S(2)}, u32[]{:S(2)}) collective-permute-start(f32[2048,128]{1,0:T(8,128)S(1)} %get-tuple-element.104), channel_id=1, source_target_pairs={{0,4},{4,0},{8,12},{12,8},{16,20},{20,16},{24,28},{28,24},{1,5},{5... | collective-permute-start | bytes 3145736 | tf_op jit(solution)/shard_map/ppermute | solution.py:22
  52.1 8.2 %collective-permute-start.16 = (f32[256,128]{1,0:T(8,128)S(1)}, f32[256,128]{1,0:T(8,128)S(1)}, u32[]{:S(2)}, u32[]{:S(2)}) collective-permute-start(f32[256,128]{1,0:T(8,128)S(1)} %get-tuple-element.112), channel_id=1, source_target_pairs={{0,8},{4,12},{8,0},{12,4},{16,24},{20,28},{24,16},{28,20},{1,9},{5... | collective-permute-start | bytes 393224 | tf_op jit(solution)/shard_map/ppermute | solution.py:29
  53.3 7.1 %collective-permute-start.17 = (f32[256,128]{1,0:T(8,128)S(1)}, f32[256,128]{1,0:T(8,128)S(1)}, u32[]{:S(2)}, u32[]{:S(2)}) collective-permute-start(f32[256,128]{1,0:T(8,128)S(1)} %get-tuple-element.113), channel_id=1, source_target_pairs={{0,16},{4,20},{8,24},{12,28},{16,0},{20,4},{24,8},{28,12},{1,17},{... | collective-permute-start | bytes 393224 | tf_op jit(solution)/shard_map/ppermute | solution.py:29
  54.5 7.2 %collective-permute-start.18 = (f32[256,128]{1,0:T(8,128)S(1)}, f32[256,128]{1,0:T(8,128)S(1)}, u32[]{:S(2)}, u32[]{:S(2)}) collective-permute-start(f32[256,128]{1,0:T(8,128)S(1)} %get-tuple-element.114), channel_id=1, source_target_pairs={{0,24},{4,28},{8,16},{12,20},{16,8},{20,12},{24,0},{28,4},{1,25},{... | collective-permute-start | bytes 393224 | tf_op jit(solution)/shard_map/ppermute | solution.py:29

commit v5 on v4

--- a/solution.py
+++ b/solution.py
@@ -342,7 +342,7 @@
 
 
 def reply_final_kernel(steps, place, follows, *refs):
-    pieces, refs = refs[:steps], refs[steps:]
+    pieces, refs = refs[steps - 1 :: -1], refs[steps:]
     inner, query_part, (query, cotangent, output, query_grad) = refs[:2], refs[2:4], refs[4:8]
     state, held, staged, left = refs[8:]
     half = inner[0].shape[0]
@@ -581,7 +581,7 @@
         functools.partial(reply_final_kernel, steps),
         [place],
         held_in(ANY, [done])
-        + held_in(VMEM, [*finals, inner_first, inner_second, part_first, part_second])
+        + held_in(VMEM, [*finals[::-1], inner_first, inner_second, part_first, part_second])
         + held_in(VMEM, [r_query, r_cotangent]),
         held_in(HBM, [reply_bf16] * 2),
         [

time: 65 us -> 65 us (level)
  transfers between devices with their start and end apart: 19 -> 19, of which waited for: 6 -> 5; matrix products, arithmetic and copies ran while one was open for 0% -> 0% of each run, Pallas kernels for 29% -> 29%
where the time goes in v5:
time: 65 us; the launch traced here: 64.9 us
  Pallas kernels  30.1 us (46%)
  starting transfers between devices  24.1 us (37%)
  waiting for transfers between devices  8.33 us (13%)
  between operations  2.23 us (3%)
    pallas_call x12, Pallas kernels, call(): pl.pallas_call(kernel, out_shape=[out for _, out in outs], in_specs=[pl.B...  30.1 us
    ppermute x12, starting transfers between devices, plane_exchange(): lax.ppermute(pieces[k], PLANE, [(b, b ^ 2 * k) for b in range(count)])  14.6 us
    ppermute x5, starting transfers between devices, resp_step(): return lax.ppermute(array, 'resp', [(z, z ^ mask) for z in range(count)])  8.88 us
    ppermute x5, waiting for transfers between devices, resp_step(): return lax.ppermute(array, 'resp', [(z, z ^ mask) for z in range(count)])  4.81 us
    ppermute x12, waiting for transfers between devices, plane_exchange(): lax.ppermute(pieces[k], PLANE, [(b, b ^ 2 * k) for b in range(count)])  3.52 us
  transfers between devices with their start and end apart: 19, of which 5 were waited for; matrix products, arithmetic and copies ran while one was open for 0% of the time, Pallas kernels for 29%

profile of v5, /device:TPU:0, one launch (start us, length us, event | category | flops | bytes accessed | tf_op | source)
XLA Modules:
  0.0 64.9 jit_solution(8382247478028402638)
XLA Ops:
  2.0 5.9 %moments.1 = (f32[2048,128]{1,0:T(8,128)S(1)}, f32[2048,128]{1,0:T(8,128)S(1)}, bf16[16,256,128]{2,1,0:T(8,128)(2,1)S(1)}, bf16[16,256,128]{2,1,0:T(8,128)(2,1)S...) custom-call(s32[6]{0:T(128)S(1)} %stack.19.place, ...), custom_call_target="tpu_custom_call" | custom-call | flops 1 | bytes 1 | tf_op jit(solution)/shard_map/moments/pallas_call | solution.py:393
  8.4 2.6 %collective-permute-start.1 = (f32[256,128]{1,0:T(8,128)S(1)}, f32[256,128]{1,0:T(8,128)S(1)}, u32[]{:S(2)}, u32[]{:S(2)}) collective-permute-start(f32[256,128]{1,0:T(8,128)S(1)} %get-tuple-element.80), channel_id=1, source_target_pairs={{0,8},{4,12},{8,0},{12,4},{16,24},{20,28},{24,16},{28,20},{1,9},{5... | collective-permute-start | bytes 393224 | tf_op jit(solution)/shard_map/ppermute | solution.py:29
  11.0 1.5 %collective-permute-start.2 = (f32[256,128]{1,0:T(8,128)S(1)}, f32[256,128]{1,0:T(8,128)S(1)}, u32[]{:S(2)}, u32[]{:S(2)}) collective-permute-start(f32[256,128]{1,0:T(8,128)S(1)} %get-tuple-element.81), channel_id=1, source_target_pairs={{0,16},{4,20},{8,24},{12,28},{16,0},{20,4},{24,8},{28,12},{1,17},{... | collective-permute-start | bytes 393224 | tf_op jit(solution)/shard_map/ppermute | solution.py:29
  13.2 5.4 %prompt_local.1 = (f32[16,256,128]{2,1,0:T(8,128)S(1)}, f32[16,256,128]{2,1,0:T(8,128)S(1)}, f32[16,256,128]{2,1,0:T(8,128)S(1)}, f32[16,256,128]{2,1,0:T(8,128)...) custom-call(s32[6]{0:T(128)S(1)} %stack.19.place, ...), custom_call_target="tpu_custom_call" | custom-call | flops 1 | bytes 1 | tf_op jit(solution)/shard_map/prompt_local/pallas_call | solution.py:393
  20.0 1.6 %collective-permute-start.4 = (f32[512,128]{1,0:T(8,128)S(1)}, f32[512,128]{1,0:T(8,128)S(1)}, u32[]{:S(2)}, u32[]{:S(2)}) collective-permute-start(f32[512,128]{1,0:T(8,128)S(1)} %get-tuple-element.86), channel_id=1, source_target_pairs={{0,1},{1,0},{2,3},{3,2},{4,5},{5,4},{6,7},{7,6},{8,9},{9,8},{10,11... | collective-permute-start | bytes 786440 | tf_op jit(solution)/shard_map/ppermute | solution.py:39
  21.7 1.2 %collective-permute-start.5 = (f32[512,128]{1,0:T(8,128)S(1)}, f32[512,128]{1,0:T(8,128)S(1)}, u32[]{:S(2)}, u32[]{:S(2)}) collective-permute-start(f32[512,128]{1,0:T(8,128)S(1)} %get-tuple-element.89), channel_id=1, source_target_pairs={{0,8},{4,12},{8,0},{12,4},{16,24},{20,28},{24,16},{28,20},{1,9},{5... | collective-permute-start | bytes 786440 | tf_op jit(solution)/shard_map/ppermute | solution.py:29
  22.9 1.5 %collective-permute-start.6 = (f32[512,128]{1,0:T(8,128)S(1)}, f32[512,128]{1,0:T(8,128)S(1)}, u32[]{:S(2)}, u32[]{:S(2)}) collective-permute-start(f32[512,128]{1,0:T(8,128)S(1)} %get-tuple-element.90), channel_id=1, source_target_pairs={{0,16},{4,20},{8,24},{12,28},{16,0},{20,4},{24,8},{28,12},{1,17},{... | collective-permute-start | bytes 786440 | tf_op jit(solution)/shard_map/ppermute | solution.py:29
  25.1 3.2 %reply_local_first.1 = (f32[4,512,128]{2,1,0:T(8,128)S(1)}, f32[4,512,128]{2,1,0:T(8,128)S(1)}, bf16[4,512,128]{2,1,0:T(8,128)(2,1)S(1)}, bf16[4,512,128]{2,1,0:T(8,128)(2,1)S(1)}, f32[8,128]{1,0:T(8,128)S(1)}) custom-call(s32[6]{0:T(128)S(1)} %stack.19.place, bf16[8,512,128]{2,1,0:T(8,128)(2,1)S(1)} %get-tuple-element.67.query.refs_8_, ...), custom_call_target="tpu_custom_call" | custom-call | flops 1 | bytes 1 | tf_op jit(solution)/shard_map/reply_local_first/pallas_call | solution.py:393
  28.4 2.9 %collective-permute-start.8 = (f32[256,128]{1,0:T(8,128)S(1)}, f32[256,128]{1,0:T(8,128)S(1)}, u32[]{:S(2)}, u32[]{:S(2)}) collective-permute-start(f32[256,128]{1,0:T(8,128)S(1)} %get-tuple-element.87.follows), channel_id=1, source_target_pairs={{0,3},{1,2},{2,1},{3,0},{4,7},{5,6},{6,5},{7,4},{8,11},{9,10},{10,... | collective-permute-start | bytes 393224 | tf_op jit(solution)/shard_map/ppermute | solution.py:39
  31.3 3.2 %reply_local_second.1 = (f32[4,512,128]{2,1,0:T(8,128)S(1)}, f32[4,512,128]{2,1,0:T(8,128)S(1)}, bf16[4,512,128]{2,1,0:T(8,128)(2,1)S(1)}, bf16[4,512,128]{2,1,0:T(8,128)(2,1)S(1)}, f32[8,128]{1,0:T(8,128)S(1)}) custom-call(s32[6]{0:T(128)S(1)} %stack.19.place, bf16[8,512,128]{2,1,0:T(8,128)(2,1)S(1)} %get-tuple-element.67.query.refs_8_, ...), custom_call_target="tpu_custom_call" | custom-call | flops 1 | bytes 1 | tf_op jit(solution)/shard_map/reply_local_second/pallas_call | solution.py:393
  34.5 1.3 %collective-permute-done.6.refs_2_ = f32[512,128]{1,0:T(8,128)S(1)} collective-permute-done((f32[512,128]{1,0:T(8,128)S(1)}, f32[512,128]{1,0:T(8,128)S(1)}, u32[]{:S(2)}, u32[]{:S(2)}) %collective-permute-start.6) | collective-permute-done | bytes 262176 | tf_op jit(solution)/shard_map/ppermute | solution.py:29
  37.2 1.6 %collective-permute-start.9 = (f32[512,128]{1,0:T(8,128)S(1)}, f32[512,128]{1,0:T(8,128)S(1)}, u32[]{:S(2)}, u32[]{:S(2)}) collective-permute-start(f32[512,128]{1,0:T(8,128)S(1)} %get-tuple-element.100), channel_id=1, source_target_pairs={{0,8},{4,12},{8,0},{12,4},{16,24},{20,28},{24,16},{28,20},{1,9},{5... | collective-permute-start | bytes 786440 | tf_op jit(solution)/shard_map/ppermute | solution.py:29
  38.7 1.4 %collective-permute-start.10 = (f32[512,128]{1,0:T(8,128)S(1)}, f32[512,128]{1,0:T(8,128)S(1)}, u32[]{:S(2)}, u32[]{:S(2)}) collective-permute-start(f32[512,128]{1,0:T(8,128)S(1)} %get-tuple-element.101), channel_id=1, source_target_pairs={{0,16},{4,20},{8,24},{12,28},{16,0},{20,4},{24,8},{28,12},{1,17},{... | collective-permute-start | bytes 786440 | tf_op jit(solution)/shard_map/ppermute | solution.py:29
  40.6 3.6 %collective-permute-start.14 = (f32[256,128]{1,0:T(8,128)S(1)}, f32[256,128]{1,0:T(8,128)S(1)}, u32[]{:S(2)}, u32[]{:S(2)}) collective-permute-start(f32[256,128]{1,0:T(8,128)S(1)} %get-tuple-element.93.follows.refs_4_), channel_id=1, source_target_pairs={{0,3},{1,2},{2,1},{3,0},{4,7},{5,6},{6,5},{7,4},{8,11},{9,10},{10,... | collective-permute-start | bytes 393224 | tf_op jit(solution)/shard_map/ppermute | solution.py:39
  44.5 1.8 %reply_grads.1 = (bf16[512,8,128]{2,1,0:T(8,128)(2,1)}, bf16[512,8,128]{2,1,0:T(8,128)(2,1)}, f32[8,128]{1,0:T(8,128)S(1)}) custom-call(f32[256,128]{1,0:T(8,128)S(1)} %get-tuple-element.93.follows.refs_4_, bf16[4,512,128]{2,1,0:T(8,128)(2,1)S(1)} %get-tuple-element.94.key_first, bf16[4,512,128]{2,1,0:T(8,128)(2,1)S(1)} %get-tuple-element.95.value_first, ...), custom_call_target="tpu_custom_call" | custom-call | flops 1 | bytes 1 | tf_op jit(solution)/shard_map/reply_grads/pallas_call | solution.py:393
  46.3 1.7 %collective-permute-done.14.refs_7_ = f32[256,128]{1,0:T(8,128)S(1)} collective-permute-done((f32[256,128]{1,0:T(8,128)S(1)}, f32[256,128]{1,0:T(8,128)S(1)}, u32[]{:S(2)}, u32[]{:S(2)}) %collective-permute-start.14) | collective-permute-done | bytes 131104 | tf_op jit(solution)/shard_map/ppermute | solution.py:39
  48.0 3.1 %collective-permute-done.13.refs_6_ = f32[256,128]{1,0:T(8,128)S(1)} collective-permute-done((f32[256,128]{1,0:T(8,128)S(1)}, f32[256,128]{1,0:T(8,128)S(1)}, u32[]{:S(2)}, u32[]{:S(2)}) %collective-permute-start.13) | collective-permute-done | bytes 131104 | tf_op jit(solution)/shard_map/ppermute | solution.py:39
  51.1 0.9 %halves.1 = (f32[2048,128]{1,0:T(8,128)S(1)}, f32[2048,128]{1,0:T(8,128)S(1)}, f32[256,128]{1,0:T(8,128)S(1)}, f32[256,128]{1,0:T(8,128)S(1)}, f32[256,128]{1,0:T(8,128)S(1)}, /*index=5*/f32[256,128]{1,0:T(8,128)S(1)}) custom-call(s32[6]{0:T(128)S(1)} %stack.19.place, f32[8,128]{1,0:T(8,128)S(1)} %get-tuple-element.98.follows, ...), custom_call_target="tpu_custom_call" | custom-call | flops 1 | bytes 1 | tf_op jit(solution)/shard_map/halves/pallas_call | solution.py:393
  52.1 1.8 %collective-permute-start.16 = (f32[256,128]{1,0:T(8,128)S(1)}, f32[256,128]{1,0:T(8,128)S(1)}, u32[]{:S(2)}, u32[]{:S(2)}) collective-permute-start(f32[256,128]{1,0:T(8,128)S(1)} %get-tuple-element.111), channel_id=1, source_target_pairs={{0,24},{4,28},{8,16},{12,20},{16,8},{20,12},{24,0},{28,4},{1,25},{... | collective-permute-start | bytes 393224 | tf_op jit(solution)/shard_map/ppermute | solution.py:29
  53.9 0.9 %collective-permute-start.17 = (f32[256,128]{1,0:T(8,128)S(1)}, f32[256,128]{1,0:T(8,128)S(1)}, u32[]{:S(2)}, u32[]{:S(2)}) collective-permute-start(f32[256,128]{1,0:T(8,128)S(1)} %get-tuple-element.112), channel_id=1, source_target_pairs={{0,16},{4,20},{8,24},{12,28},{16,0},{20,4},{24,8},{28,12},{1,17},{... | collective-permute-start | bytes 393224 | tf_op jit(solution)/shard_map/ppermute | solution.py:29
  54.8 0.9 %collective-permute-start.18 = (f32[256,128]{1,0:T(8,128)S(1)}, f32[256,128]{1,0:T(8,128)S(1)}, u32[]{:S(2)}, u32[]{:S(2)}) collective-permute-start(f32[256,128]{1,0:T(8,128)S(1)} %get-tuple-element.113), channel_id=1, source_target_pairs={{0,8},{4,12},{8,0},{12,4},{16,24},{20,28},{24,16},{28,20},{1,9},{5... | collective-permute-start | bytes 393224 | tf_op jit(solution)/shard_map/ppermute | solution.py:29
  55.7 4.6 %prompt_final.1 = (bf16[256,16,128]{2,1,0:T(8,128)(2,1)}, bf16[256,16,128]{2,1,0:T(8,128)(2,1)}, bf16[256,16,128]{2,1,0:T(8,128)(2,1)}, bf16[256,16,128]{2,1,0:T(8,128)(2,1)}, f32[8,128]{1,0:T(8,128)S(1)}) custom-call(s32[6]{0:T(128)S(1)} %stack.19.place, f32[2048,128]{1,0:T(8,128)S(1)} %get-tuple-element.103.mine, ...), custom_call_target="tpu_custom_call" | custom-call | flops 1 | bytes 1 | tf_op jit(solution)/shard_map/prompt_final/pallas_call | solution.py:393
  60.3 1.4 %collective-permute-done.17.refs_1_ = f32[256,128]{1,0:T(8,128)S(1)} collective-permute-done((f32[256,128]{1,0:T(8,128)S(1)}, f32[256,128]{1,0:T(8,128)S(1)}, u32[]{:S(2)}, u32[]{:S(2)}) %collective-permute-start.17) | collective-permute-done | bytes 131104 | tf_op jit(solution)/shard_map/ppermute | solution.py:29
  61.8 2.9 %reply_final.1 = (bf16[512,8,128]{2,1,0:T(8,128)(2,1)}, bf16[512,8,128]{2,1,0:T(8,128)(2,1)}) custom-call(s32[6]{0:T(128)S(1)} %stack.19.place, f32[8,128]{1,0:T(8,128)S(1)} %get-tuple-element.110.follows, f32[256,128]{1,0:T(8,128)S(1)} %collective-permute-done.16.refs_0_, f32[256,128]{1,0:T(8,128)S(1)} %collective-permute-done.17.refs_1_, ...), custom_call_target="tpu_custom_call" | custom-call | flops 1 | bytes 1 | tf_op jit(solution)/shard_map/reply_final/pallas_call | solution.py:393
  (27 shorter events, 5.7 us)
Async XLA Ops:
  7.9 4.6 %collective-permute-start = (f32[2048,128]{1,0:T(8,128)S(1)}, f32[2048,128]{1,0:T(8,128)S(1)}, u32[]{:S(2)}, u32[]{:S(2)}) collective-permute-start(f32[2048,128]{1,0:T(8,128)S(1)} %get-tuple-element.73), channel_id=1, source_target_pairs={{0,4},{4,0},{8,12},{12,8},{16,20},{20,16},{24,28},{28,24},{1,5},{5... | collective-permute-start | bytes 3145736 | tf_op jit(solution)/shard_map/ppermute | solution.py:22
  8.4 10.2 %collective-permute-start.1 = (f32[256,128]{1,0:T(8,128)S(1)}, f32[256,128]{1,0:T(8,128)S(1)}, u32[]{:S(2)}, u32[]{:S(2)}) collective-permute-start(f32[256,128]{1,0:T(8,128)S(1)} %get-tuple-element.80), channel_id=1, source_target_pairs={{0,8},{4,12},{8,0},{12,4},{16,24},{20,28},{24,16},{28,20},{1,9},{5... | collective-permute-start | bytes 393224 | tf_op jit(solution)/shard_map/ppermute | solution.py:29
  11.0 8.4 %collective-permute-start.2 = (f32[256,128]{1,0:T(8,128)S(1)}, f32[256,128]{1,0:T(8,128)S(1)}, u32[]{:S(2)}, u32[]{:S(2)}) collective-permute-start(f32[256,128]{1,0:T(8,128)S(1)} %get-tuple-element.81), channel_id=1, source_target_pairs={{0,16},{4,20},{8,24},{12,28},{16,0},{20,4},{24,8},{28,12},{1,17},{... | collective-permute-start | bytes 393224 | tf_op jit(solution)/shard_map/ppermute | solution.py:29
  12.5 6.9 %collective-permute-start.3 = (f32[256,128]{1,0:T(8,128)S(1)}, f32[256,128]{1,0:T(8,128)S(1)}, u32[]{:S(2)}, u32[]{:S(2)}) collective-permute-start(f32[256,128]{1,0:T(8,128)S(1)} %get-tuple-element.82), channel_id=1, source_target_pairs={{0,24},{4,28},{8,16},{12,20},{16,8},{20,12},{24,0},{28,4},{1,25},{... | collective-permute-start | bytes 393224 | tf_op jit(solution)/shard_map/ppermute | solution.py:29
  20.0 8.4 %collective-permute-start.4 = (f32[512,128]{1,0:T(8,128)S(1)}, f32[512,128]{1,0:T(8,128)S(1)}, u32[]{:S(2)}, u32[]{:S(2)}) collective-permute-start(f32[512,128]{1,0:T(8,128)S(1)} %get-tuple-element.86), channel_id=1, source_target_pairs={{0,1},{1,0},{2,3},{3,2},{4,5},{5,4},{6,7},{7,6},{8,9},{9,8},{10,11... | collective-permute-start | bytes 786440 | tf_op jit(solution)/shard_map/ppermute | solution.py:39
  21.7 12.9 %collective-permute-start.5 = (f32[512,128]{1,0:T(8,128)S(1)}, f32[512,128]{1,0:T(8,128)S(1)}, u32[]{:S(2)}, u32[]{:S(2)}) collective-permute-start(f32[512,128]{1,0:T(8,128)S(1)} %get-tuple-element.89), channel_id=1, source_target_pairs={{0,8},{4,12},{8,0},{12,4},{16,24},{20,28},{24,16},{28,20},{1,9},{5... | collective-permute-start | bytes 786440 | tf_op jit(solution)/shard_map/ppermute | solution.py:29
  22.9 12.9 %collective-permute-start.6 = (f32[512,128]{1,0:T(8,128)S(1)}, f32[512,128]{1,0:T(8,128)S(1)}, u32[]{:S(2)}, u32[]{:S(2)}) collective-permute-start(f32[512,128]{1,0:T(8,128)S(1)} %get-tuple-element.90), channel_id=1, source_target_pairs={{0,16},{4,20},{8,24},{12,28},{16,0},{20,4},{24,8},{28,12},{1,17},{... | collective-permute-start | bytes 786440 | tf_op jit(solution)/shard_map/ppermute | solution.py:29
  24.4 11.5 %collective-permute-start.7 = (f32[512,128]{1,0:T(8,128)S(1)}, f32[512,128]{1,0:T(8,128)S(1)}, u32[]{:S(2)}, u32[]{:S(2)}) collective-permute-start(f32[512,128]{1,0:T(8,128)S(1)} %get-tuple-element.91), channel_id=1, source_target_pairs={{0,24},{4,28},{8,16},{12,20},{16,8},{20,12},{24,0},{28,4},{1,25},{... | collective-permute-start | bytes 786440 | tf_op jit(solution)/shard_map/ppermute | solution.py:29
  28.4 7.4 %collective-permute-start.8 = (f32[256,128]{1,0:T(8,128)S(1)}, f32[256,128]{1,0:T(8,128)S(1)}, u32[]{:S(2)}, u32[]{:S(2)}) collective-permute-start(f32[256,128]{1,0:T(8,128)S(1)} %get-tuple-element.87.follows), channel_id=1, source_target_pairs={{0,3},{1,2},{2,1},{3,0},{4,7},{5,6},{6,5},{7,4},{8,11},{9,10},{10,... | collective-permute-start | bytes 393224 | tf_op jit(solution)/shard_map/ppermute | solution.py:39
  36.6 7.6 %collective-permute-start.12 = (f32[256,128]{1,0:T(8,128)S(1)}, f32[256,128]{1,0:T(8,128)S(1)}, u32[]{:S(2)}, u32[]{:S(2)}) collective-permute-start(f32[256,128]{1,0:T(8,128)S(1)} %get-tuple-element.93.follows.refs_4_), channel_id=1, source_target_pairs={{0,1},{1,0},{2,3},{3,2},{4,5},{5,4},{6,7},{7,6},{8,9},{9,8},{10,11... | collective-permute-start | bytes 393224 | tf_op jit(solution)/shard_map/ppermute | solution.py:39
  37.2 14.0 %collective-permute-start.9 = (f32[512,128]{1,0:T(8,128)S(1)}, f32[512,128]{1,0:T(8,128)S(1)}, u32[]{:S(2)}, u32[]{:S(2)}) collective-permute-start(f32[512,128]{1,0:T(8,128)S(1)} %get-tuple-element.100), channel_id=1, source_target_pairs={{0,8},{4,12},{8,0},{12,4},{16,24},{20,28},{24,16},{28,20},{1,9},{5... | collective-permute-start | bytes 786440 | tf_op jit(solution)/shard_map/ppermute | solution.py:29
  38.7 12.4 %collective-permute-start.10 = (f32[512,128]{1,0:T(8,128)S(1)}, f32[512,128]{1,0:T(8,128)S(1)}, u32[]{:S(2)}, u32[]{:S(2)}) collective-permute-start(f32[512,128]{1,0:T(8,128)S(1)} %get-tuple-element.101), channel_id=1, source_target_pairs={{0,16},{4,20},{8,24},{12,28},{16,0},{20,4},{24,8},{28,12},{1,17},{... | collective-permute-start | bytes 786440 | tf_op jit(solution)/shard_map/ppermute | solution.py:29
  40.2 10.9 %collective-permute-start.11 = (f32[512,128]{1,0:T(8,128)S(1)}, f32[512,128]{1,0:T(8,128)S(1)}, u32[]{:S(2)}, u32[]{:S(2)}) collective-permute-start(f32[512,128]{1,0:T(8,128)S(1)} %get-tuple-element.102), channel_id=1, source_target_pairs={{0,24},{4,28},{8,16},{12,20},{16,8},{20,12},{24,0},{28,4},{1,25},{... | collective-permute-start | bytes 786440 | tf_op jit(solution)/shard_map/ppermute | solution.py:29
  40.6 7.4 %collective-permute-start.14 = (f32[256,128]{1,0:T(8,128)S(1)}, f32[256,128]{1,0:T(8,128)S(1)}, u32[]{:S(2)}, u32[]{:S(2)}) collective-permute-start(f32[256,128]{1,0:T(8,128)S(1)} %get-tuple-element.93.follows.refs_4_), channel_id=1, source_target_pairs={{0,3},{1,2},{2,1},{3,0},{4,7},{5,6},{6,5},{7,4},{8,11},{9,10},{10,... | collective-permute-start | bytes 393224 | tf_op jit(solution)/shard_map/ppermute | solution.py:39
  44.2 6.9 %collective-permute-start.13 = (f32[256,128]{1,0:T(8,128)S(1)}, f32[256,128]{1,0:T(8,128)S(1)}, u32[]{:S(2)}, u32[]{:S(2)}) collective-permute-start(f32[256,128]{1,0:T(8,128)S(1)} %collective-permute-done.12.refs_5_), channel_id=1, source_target_pairs={{0,3},{1,2},{2,1},{3,0},{4,7},{5,6},{6,5},{7,4},{8,11},{9,10},{10,... | collective-permute-start | bytes 393224 | tf_op jit(solution)/shard_map/ppermute | solution.py:39
  52.1 3.6 %collective-permute-start.15 = (f32[2048,128]{1,0:T(8,128)S(1)}, f32[2048,128]{1,0:T(8,128)S(1)}, u32[]{:S(2)}, u32[]{:S(2)}) collective-permute-start(f32[2048,128]{1,0:T(8,128)S(1)} %get-tuple-element.104), channel_id=1, source_target_pairs={{0,4},{4,0},{8,12},{12,8},{16,20},{20,16},{24,28},{28,24},{1,5},{5... | collective-permute-start | bytes 3145736 | tf_op jit(solution)/shard_map/ppermute | solution.py:22
  52.1 8.2 %collective-permute-start.16 = (f32[256,128]{1,0:T(8,128)S(1)}, f32[256,128]{1,0:T(8,128)S(1)}, u32[]{:S(2)}, u32[]{:S(2)}) collective-permute-start(f32[256,128]{1,0:T(8,128)S(1)} %get-tuple-element.111), channel_id=1, source_target_pairs={{0,24},{4,28},{8,16},{12,20},{16,8},{20,12},{24,0},{28,4},{1,25},{... | collective-permute-start | bytes 393224 | tf_op jit(solution)/shard_map/ppermute | solution.py:29
  53.9 7.8 %collective-permute-start.17 = (f32[256,128]{1,0:T(8,128)S(1)}, f32[256,128]{1,0:T(8,128)S(1)}, u32[]{:S(2)}, u32[]{:S(2)}) collective-permute-start(f32[256,128]{1,0:T(8,128)S(1)} %get-tuple-element.112), channel_id=1, source_target_pairs={{0,16},{4,20},{8,24},{12,28},{16,0},{20,4},{24,8},{28,12},{1,17},{... | collective-permute-start | bytes 393224 | tf_op jit(solution)/shard_map/ppermute | solution.py:29
  54.8 7.0 %collective-permute-start.18 = (f32[256,128]{1,0:T(8,128)S(1)}, f32[256,128]{1,0:T(8,128)S(1)}, u32[]{:S(2)}, u32[]{:S(2)}) collective-permute-start(f32[256,128]{1,0:T(8,128)S(1)} %get-tuple-element.113), channel_id=1, source_target_pairs={{0,8},{4,12},{8,0},{12,4},{16,24},{20,28},{24,16},{28,20},{1,9},{5... | collective-permute-start | bytes 393224 | tf_op jit(solution)/shard_map/ppermute | solution.py:29
